TPU v7x, 32 devices: a whole 2x2x4 slice. The times are simulated.
32 devices in a mesh: rep: 8 (over y, x, core), shard: 4 (over z).
Axes of the slice: x: 2, y: 2, z: 4, core: 2. Of those that a mesh axis runs over, the one named last changes fastest.
Arguments:
- tokens: bfloat16 [8192, 2048], P(('rep', 'shard')), may hold values from -6 to 6
- cotangent: bfloat16 [8192, 2048], P(('rep', 'shard')), may hold values from -6 to 6
- segments: int32 [32, 256], P(('rep', 'shard')), may hold values from 0 to 3, never falling along the last dimension, each value on 1 to 128 neighbouring positions
- padding: int32 [32, 256], P(('rep', 'shard')), may hold values from 0 to 1, as said below
- routes: int32 [8192, 8], P(('rep', 'shard')), may hold values from 0 to 15, all different within a row; in each aligned block of 256 rows (0 to 255, 256 to 511, ...) at most 160 rows name the same one
- route_weights: float32 [8192, 8], P(('rep', 'shard')), may hold values from 0.05 to 0.3
- adapter_set: int32 [32], P(('rep', 'shard')), may hold values from 0 to 1
- norm_one: float32 [2048], replicated, may hold values from 0.1 to 1.9
- norm_two: float32 [2048], replicated, may hold values from 0.1 to 1.9
- query_weight: bfloat16 [2048, 2048], P(None, 'shard'), may hold values from -0.125 to 0.125
- key_weight: bfloat16 [2048, 2048], P(None, 'shard'), may hold values from -0.125 to 0.125
- value_weight: bfloat16 [2048, 2048], P(None, 'shard'), may hold values from -0.125 to 0.125
- output_weight: bfloat16 [2048, 2048], P(None, 'shard'), may hold values from -0.5 to 0.5
- query_down: bfloat16 [2048, 2, 16], P('shard'), may hold values from -0.125 to 0.125
- key_down: bfloat16 [2048, 2, 16], P('shard'), may hold values from -0.125 to 0.125
- value_down: bfloat16 [2048, 2, 16], P('shard'), may hold values from -0.125 to 0.125
- output_down: bfloat16 [2048, 2, 16], P('shard'), may hold values from -0.125 to 0.125
- query_lift: bfloat16 [2048, 2, 16], P('shard'), may hold values from -0.75 to 0.75
- key_lift: bfloat16 [2048, 2, 16], P('shard'), may hold values from -0.75 to 0.75
- value_lift: bfloat16 [2048, 2, 16], P('shard'), may hold values from -0.75 to 0.75
- output_lift: bfloat16 [2048, 2, 16], P('shard'), may hold values from -1.5 to 1.5
- expert_gate: bfloat16 [16, 2048, 1024], P('shard'), may hold values from -0.125 to 0.125
- expert_upper: bfloat16 [16, 2048, 1024], P('shard'), may hold values from -0.125 to 0.125
- expert_lower: bfloat16 [16, 1024, 2048], P('shard'), may hold values from -0.1875 to 0.1875
- gate_down: bfloat16 [16, 2048, 2, 16], P('shard'), may hold values from -0.125 to 0.125
- gate_lift: bfloat16 [16, 1024, 2, 16], P('shard'), may hold values from -0.75 to 0.75
- upper_down: bfloat16 [16, 2048, 2, 16], P('shard'), may hold values from -0.125 to 0.125
- upper_lift: bfloat16 [16, 1024, 2, 16], P('shard'), may hold values from -0.75 to 0.75
- lower_down: bfloat16 [16, 1024, 2, 16], P('shard'), may hold values from -0.1875 to 0.1875
- lower_lift: bfloat16 [16, 2048, 2, 16], P('shard'), may hold values from -0.75 to 0.75
Outputs:
- output: bfloat16 [8192, 2048], P(('rep', 'shard'))
- input_grad: bfloat16 [8192, 2048], P(('rep', 'shard'))
- query_down_grad: float32 [2048, 2, 16], P('shard')
- key_down_grad: float32 [2048, 2, 16], P('shard')
- value_down_grad: float32 [2048, 2, 16], P('shard')
- output_down_grad: float32 [2048, 2, 16], P('shard')
- query_lift_grad: float32 [2048, 2, 16], P('shard')
- key_lift_grad: float32 [2048, 2, 16], P('shard')
- value_lift_grad: float32 [2048, 2, 16], P('shard')
- output_lift_grad: float32 [2048, 2, 16], P('shard')
- gate_down_grad: float32 [16, 2048, 2, 16], P('shard')
- gate_lift_grad: float32 [16, 1024, 2, 16], P('shard')
- upper_down_grad: float32 [16, 2048, 2, 16], P('shard')
- upper_lift_grad: float32 [16, 1024, 2, 16], P('shard')
- lower_down_grad: float32 [16, 1024, 2, 16], P('shard')
- lower_lift_grad: float32 [16, 2048, 2, 16], P('shard')
Inputs may be any that keep to these rules, and one draw needn't show every extreme that they name: `routes`: in the 256 rows of one sequence no expert is named by more than 160 rows, a bound that some block reaches; a row's 8 experts differ. `segments`: within a sequence the entries never fall. `padding`: each row of 256 is 1 up to some position and 0 after it, with at most 64 zeros.
All inputs are finite; a program needn't handle non-finite values.
Results may differ from a plain program's by a relative error of at most 0.023.
Values may be sent and summed in bfloat16 or wider, within the bound.
No kernel may reach another device: no remote copies, remote signals or barrier semaphores. Data moves between devices by JAX's collectives and lax.ppermute only.
A program may use at most 384 MiB of HBM per device.

v0:
```python
import jax
import jax.numpy as jnp
from jax import lax
from jax.sharding import PartitionSpec as P

HEADS = 16
HEAD = 128
TOP = 8
EXPERTS = 16
RANK = 16
SETS = 2
MOST = 160


epsilon = 1e-06
adapter_scale = 2.0
masked_score = -1e30


def rms_forward(values, gain_vec):
    inverse = lax.rsqrt(jnp.mean(values * values, axis=-1, keepdims=True) + epsilon)
    return values * inverse * gain_vec


def rms_backward(values, gain_vec, grad_norm):
    inverse = lax.rsqrt(jnp.mean(values * values, axis=-1, keepdims=True) + epsilon)
    weighted = grad_norm * gain_vec
    cubed = inverse * inverse * inverse
    return inverse * weighted - values * cubed * jnp.mean(values * weighted, axis=-1, keepdims=True)


def route_slots(routes, route_weights):
    expert_ids = jnp.arange(EXPERTS, dtype=jnp.int32)
    picked = (routes[:, :, None] == expert_ids[None, None, :]).astype(jnp.int32)
    member = jnp.sum(picked, axis=1)
    before = jnp.cumsum(member, axis=0) - member
    slot_of = jnp.sum(picked * (expert_ids[None, None, :] * MOST + before[:, None, :]), axis=2)
    slot_ids = jnp.arange(MOST, dtype=jnp.int32)
    chosen = member.T[:, None, :] * (before.T[:, None, :] == slot_ids[None, :, None]).astype(
        jnp.int32
    )
    token_ids = jnp.arange(routes.shape[0], dtype=jnp.int32)
    token_of = jnp.sum(chosen * token_ids[None, None, :], axis=2)
    per_expert = jnp.sum(picked.astype(jnp.float32) * route_weights[:, :, None], axis=1)
    slot_weight = jnp.sum(chosen.astype(jnp.float32) * per_expert.T[:, None, :], axis=2)
    return (slot_of, token_of, slot_weight)


def adapt_plain(block_of_rows, dense_weight, down_pack, raise_bundle, retain_mask):
    narrowed_rows = (
        jnp.dot(block_of_rows, down_pack, preferred_element_type=jnp.float32) * retain_mask
    ).astype(jnp.bfloat16)
    final_output = jnp.dot(block_of_rows, dense_weight, preferred_element_type=jnp.float32)
    final_output = final_output + adapter_scale * jnp.einsum(
        "sj,oj->so", narrowed_rows, raise_bundle, preferred_element_type=jnp.float32
    )
    return (final_output, narrowed_rows)


def adapt_plain_back(
    block_of_rows,
    output_gradient,
    dense_weight,
    down_pack,
    raise_bundle,
    narrowed_rows,
    retain_mask,
):
    grad_reduced = (
        adapter_scale
        * jnp.dot(output_gradient, raise_bundle, preferred_element_type=jnp.float32)
        * retain_mask
    ).astype(jnp.bfloat16)
    lift_gradient = adapter_scale * jnp.einsum(
        "so,sj->oj", output_gradient, narrowed_rows, preferred_element_type=jnp.float32
    )
    grad_down = jnp.einsum(
        "si,sj->ij", block_of_rows, grad_reduced, preferred_element_type=jnp.float32
    )
    grad_rows = jnp.einsum(
        "so,io->si", output_gradient, dense_weight, preferred_element_type=jnp.float32
    )
    grad_rows = grad_rows + jnp.einsum(
        "sj,ij->si", grad_reduced, down_pack, preferred_element_type=jnp.float32
    )
    return (grad_rows, grad_down, lift_gradient)


def batch_adapt(block_of_rows, dense_weight, down, raise_matrix, retain_mask):
    how_many = down.shape[0]
    down_pack = down.reshape(how_many, down.shape[1], -1)
    raise_bundle = raise_matrix.reshape(how_many, raise_matrix.shape[1], -1)
    narrowed_rows = (
        jnp.einsum("nci,nij->ncj", block_of_rows, down_pack, preferred_element_type=jnp.float32)
        * retain_mask
    ).astype(jnp.bfloat16)
    final_output = jnp.einsum(
        "nci,nio->nco", block_of_rows, dense_weight, preferred_element_type=jnp.float32
    )
    final_output = final_output + adapter_scale * jnp.einsum(
        "ncj,noj->nco", narrowed_rows, raise_bundle, preferred_element_type=jnp.float32
    )
    return (final_output, narrowed_rows)


def batch_adapt_back(
    block_of_rows, output_gradient, dense_weight, down, raise_matrix, narrowed_rows, retain_mask
):
    how_many = down.shape[0]
    down_pack = down.reshape(how_many, down.shape[1], -1)
    raise_bundle = raise_matrix.reshape(how_many, raise_matrix.shape[1], -1)
    grad_reduced = (
        adapter_scale
        * jnp.einsum(
            "nco,noj->ncj", output_gradient, raise_bundle, preferred_element_type=jnp.float32
        )
        * retain_mask
    ).astype(jnp.bfloat16)
    lift_gradient = adapter_scale * jnp.einsum(
        "nco,ncj->noj", output_gradient, narrowed_rows, preferred_element_type=jnp.float32
    )
    grad_down = jnp.einsum(
        "nci,ncj->nij", block_of_rows, grad_reduced, preferred_element_type=jnp.float32
    )
    grad_rows = jnp.einsum(
        "nco,nio->nci", output_gradient, dense_weight, preferred_element_type=jnp.float32
    )
    grad_rows = grad_rows + jnp.einsum(
        "ncj,nij->nci", grad_reduced, down_pack, preferred_element_type=jnp.float32
    )
    return (grad_rows, grad_down.reshape(down.shape), lift_gradient.reshape(raise_matrix.shape))


def expert_forward(block_of_rows, set_mask, params):
    (
        expert_gate,
        expert_upper,
        expert_lower,
        gate_down,
        gate_lift,
        upper_down,
        upper_lift,
        lower_down,
        lower_lift,
    ) = params
    retain_mask = jnp.repeat(set_mask.astype(jnp.float32), RANK, axis=-1)
    gate_val, gate_reduced = batch_adapt(
        block_of_rows, expert_gate, gate_down, gate_lift, retain_mask
    )
    upper_val, upper_reduced = batch_adapt(
        block_of_rows, expert_upper, upper_down, upper_lift, retain_mask
    )
    hidden = (jax.nn.silu(gate_val) * upper_val).astype(jnp.bfloat16)
    final_output, lower_reduced = batch_adapt(
        hidden, expert_lower, lower_down, lower_lift, retain_mask
    )
    return final_output.astype(jnp.bfloat16)


def expert_backward(block_of_rows, set_mask, output_gradient, params):
    (
        expert_gate,
        expert_upper,
        expert_lower,
        gate_down,
        gate_lift,
        upper_down,
        upper_lift,
        lower_down,
        lower_lift,
    ) = params
    retain_mask = jnp.repeat(set_mask.astype(jnp.float32), RANK, axis=-1)
    gate_val, gate_reduced = batch_adapt(
        block_of_rows, expert_gate, gate_down, gate_lift, retain_mask
    )
    upper_val, upper_reduced = batch_adapt(
        block_of_rows, expert_upper, upper_down, upper_lift, retain_mask
    )
    sigmoid_gate = jax.nn.sigmoid(gate_val)
    act_gate = gate_val * sigmoid_gate
    hidden = (act_gate * upper_val).astype(jnp.bfloat16)
    lower_pack = lower_down.reshape(lower_down.shape[0], lower_down.shape[1], -1)
    lower_reduced = (
        jnp.einsum("nci,nij->ncj", hidden, lower_pack, preferred_element_type=jnp.float32)
        * retain_mask
    ).astype(jnp.bfloat16)
    grad_hidden, grad_lower_down, grad_lower_lift = batch_adapt_back(
        hidden, output_gradient, expert_lower, lower_down, lower_lift, lower_reduced, retain_mask
    )
    grad_gate = (
        grad_hidden * upper_val * sigmoid_gate * (1.0 + gate_val * (1.0 - sigmoid_gate))
    ).astype(jnp.bfloat16)
    grad_upper = (grad_hidden * act_gate).astype(jnp.bfloat16)
    from_gate, grad_gate_down, grad_gate_lift = batch_adapt_back(
        block_of_rows, grad_gate, expert_gate, gate_down, gate_lift, gate_reduced, retain_mask
    )
    from_upper, grad_upper_down, grad_upper_lift = batch_adapt_back(
        block_of_rows, grad_upper, expert_upper, upper_down, upper_lift, upper_reduced, retain_mask
    )
    grad_rows = (from_gate + from_upper).astype(jnp.bfloat16)
    return (
        grad_rows,
        grad_gate_down,
        grad_gate_lift,
        grad_upper_down,
        grad_upper_lift,
        grad_lower_down,
        grad_lower_lift,
    )


def attention_logits(heads_q, heads_k, allowed):
    logits = jnp.einsum(
        "qhd,khd->hqk", heads_q, heads_k, preferred_element_type=jnp.float32
    ) * HEAD ** (-0.5)
    return jnp.where(allowed[None], logits, masked_score)


def flatten_last(table):
    return table.reshape(table.shape[0], -1)


def local(
    tokens,
    cotangent,
    segments,
    padding,
    routes,
    route_weights,
    adapter_set,
    norm_one,
    norm_two,
    query_weight,
    key_weight,
    value_weight,
    output_weight,
    query_down,
    key_down,
    value_down,
    output_down,
    query_lift,
    key_lift,
    value_lift,
    output_lift,
    expert_gate,
    expert_upper,
    expert_lower,
    gate_down,
    gate_lift,
    upper_down,
    upper_lift,
    lower_down,
    lower_lift,
):
    seq_len = tokens.shape[0]
    score_scale = HEAD ** (-0.5)
    chosen_set = adapter_set[0]
    set_flags = (jnp.arange(SETS, dtype=jnp.int32) == chosen_set).astype(jnp.float32)
    keep_attn = jnp.repeat(set_flags, RANK)
    positions = jnp.arange(seq_len, dtype=jnp.int32)
    allowed = (segments[0][:, None] == segments[0][None, :]) & (
        (padding[0][None, :] == 1) | (positions[:, None] == positions[None, :])
    )
    gathered = (
        lax.all_gather(query_weight, "shard", axis=1, tiled=True),
        lax.all_gather(key_weight, "shard", axis=1, tiled=True),
        lax.all_gather(value_weight, "shard", axis=1, tiled=True),
        lax.all_gather(output_weight, "shard", axis=1, tiled=True),
        lax.all_gather(query_down, "shard", axis=0, tiled=True),
        lax.all_gather(key_down, "shard", axis=0, tiled=True),
        lax.all_gather(value_down, "shard", axis=0, tiled=True),
        lax.all_gather(output_down, "shard", axis=0, tiled=True),
        lax.all_gather(query_lift, "shard", axis=0, tiled=True),
        lax.all_gather(key_lift, "shard", axis=0, tiled=True),
        lax.all_gather(value_lift, "shard", axis=0, tiled=True),
        lax.all_gather(output_lift, "shard", axis=0, tiled=True),
    )
    residual = tokens.astype(jnp.float32)
    normed_one = rms_forward(residual, norm_one).astype(jnp.bfloat16)
    projected = []
    reduced_list = []
    for number in range(3):
        final_output, narrowed_rows = adapt_plain(
            normed_one,
            gathered[number],
            flatten_last(gathered[4 + number]),
            flatten_last(gathered[8 + number]),
            keep_attn,
        )
        projected.append(final_output.astype(jnp.bfloat16).reshape(seq_len, HEADS, HEAD))
        reduced_list.append(narrowed_rows)
    logits = attention_logits(projected[0], projected[1], allowed)
    top_score = jnp.max(logits, axis=-1, keepdims=True)
    exp_scores = jnp.exp(logits - top_score)
    exp_total = jnp.sum(exp_scores, axis=-1, keepdims=True)
    attn_probs = exp_scores / exp_total
    log_total = top_score + jnp.log(exp_total)
    attn_mixed = (
        jnp.einsum(
            "hqk,khd->qhd",
            attn_probs.astype(jnp.bfloat16),
            projected[2],
            preferred_element_type=jnp.float32,
        )
        .reshape(seq_len, -1)
        .astype(jnp.bfloat16)
    )
    attn_out, reduced_out = adapt_plain(
        attn_mixed, gathered[3], flatten_last(gathered[7]), flatten_last(gathered[11]), keep_attn
    )
    after_attn = residual + attn_out
    normed_two = rms_forward(after_attn, norm_two).astype(jnp.bfloat16)
    slot_of, token_of, slot_weight = route_slots(routes, route_weights)
    dispatched = jnp.take(normed_two, token_of.reshape(-1), axis=0).reshape(EXPERTS, MOST, -1)
    row_sets = jnp.broadcast_to(set_flags.astype(jnp.bfloat16), (EXPERTS, MOST, SETS))
    arrived, arrived_sets = (
        lax.all_to_all(dispatched, "shard", split_axis=0, concat_axis=1, tiled=True),
        lax.all_to_all(row_sets, "shard", split_axis=0, concat_axis=1, tiled=True),
    )
    local_out = expert_forward(
        arrived,
        arrived_sets,
        (
            expert_gate,
            expert_upper,
            expert_lower,
            gate_down,
            gate_lift,
            upper_down,
            upper_lift,
            lower_down,
            lower_lift,
        ),
    )
    expert_out = lax.all_to_all(local_out, "shard", split_axis=1, concat_axis=0, tiled=True)
    taken_out = jnp.take(
        expert_out.reshape(EXPERTS * MOST, -1), slot_of.reshape(-1), axis=0
    ).reshape(seq_len, TOP, -1)
    combined = jnp.sum(taken_out.astype(jnp.float32) * route_weights[:, :, None], axis=1)
    output = (after_attn + combined).astype(jnp.bfloat16)
    grad_after = cotangent.astype(jnp.float32)
    taken_grad = jnp.take(grad_after, token_of.reshape(-1), axis=0).reshape(EXPERTS, MOST, -1)
    slot_grad = (taken_grad * slot_weight[:, :, None]).astype(jnp.bfloat16)
    sent_grad = lax.all_to_all(slot_grad, "shard", split_axis=0, concat_axis=1, tiled=True)
    local_back = expert_backward(
        arrived,
        arrived_sets,
        sent_grad,
        (
            expert_gate,
            expert_upper,
            expert_lower,
            gate_down,
            gate_lift,
            upper_down,
            upper_lift,
            lower_down,
            lower_lift,
        ),
    )
    slot_dx = lax.all_to_all(local_back[0], "shard", split_axis=1, concat_axis=0, tiled=True)
    expert_grads = local_back[1:]
    taken_dx = jnp.take(slot_dx.reshape(EXPERTS * MOST, -1), slot_of.reshape(-1), axis=0).reshape(
        seq_len, TOP, -1
    )
    grad_normed_two = jnp.sum(taken_dx.astype(jnp.float32), axis=1)
    grad_mid = grad_after + rms_backward(after_attn, norm_two, grad_normed_two)
    grad_attn = grad_mid.astype(jnp.bfloat16)
    params_back = (
        lax.all_gather(query_weight, "shard", axis=1, tiled=True),
        lax.all_gather(key_weight, "shard", axis=1, tiled=True),
        lax.all_gather(value_weight, "shard", axis=1, tiled=True),
        lax.all_gather(output_weight, "shard", axis=1, tiled=True),
        lax.all_gather(query_down, "shard", axis=0, tiled=True),
        lax.all_gather(key_down, "shard", axis=0, tiled=True),
        lax.all_gather(value_down, "shard", axis=0, tiled=True),
        lax.all_gather(output_down, "shard", axis=0, tiled=True),
        lax.all_gather(query_lift, "shard", axis=0, tiled=True),
        lax.all_gather(key_lift, "shard", axis=0, tiled=True),
        lax.all_gather(value_lift, "shard", axis=0, tiled=True),
        lax.all_gather(output_lift, "shard", axis=0, tiled=True),
    )
    grad_mixed, grad_out_down, grad_out_lift = adapt_plain_back(
        attn_mixed,
        grad_attn,
        params_back[3],
        flatten_last(params_back[7]),
        flatten_last(params_back[11]),
        reduced_out,
        keep_attn,
    )
    grad_heads = grad_mixed.astype(jnp.bfloat16).reshape(seq_len, HEADS, HEAD)
    logits_again = attention_logits(projected[0], projected[1], allowed)
    probs_again = jnp.exp(logits_again - log_total)
    grad_probs = jnp.einsum(
        "qhd,khd->hqk", grad_heads, projected[2], preferred_element_type=jnp.float32
    )
    row_delta = jnp.sum(grad_probs * probs_again, axis=-1, keepdims=True)
    grad_logits = (probs_again * (grad_probs - row_delta)).astype(jnp.bfloat16)
    grad_query = (
        jnp.einsum("hqk,khd->qhd", grad_logits, projected[1], preferred_element_type=jnp.float32)
        * score_scale
    )
    grad_key = (
        jnp.einsum("hqk,qhd->khd", grad_logits, projected[0], preferred_element_type=jnp.float32)
        * score_scale
    )
    grad_value = jnp.einsum(
        "hqk,qhd->khd",
        probs_again.astype(jnp.bfloat16),
        grad_heads,
        preferred_element_type=jnp.float32,
    )
    grad_proj = [grad_query, grad_key, grad_value]
    grad_normed_one = jnp.zeros((seq_len, normed_one.shape[1]), jnp.float32)
    down_grads = []
    lift_grads = []
    for number in range(3):
        grad_rounded = grad_proj[number].reshape(seq_len, -1).astype(jnp.bfloat16)
        grad_rows, grad_down, lift_gradient = adapt_plain_back(
            normed_one,
            grad_rounded,
            params_back[number],
            flatten_last(params_back[4 + number]),
            flatten_last(params_back[8 + number]),
            reduced_list[number],
            keep_attn,
        )
        grad_normed_one = grad_normed_one + grad_rows
        down_grads.append(grad_down.reshape(grad_down.shape[0], SETS, RANK))
        lift_grads.append(lift_gradient.reshape(lift_gradient.shape[0], SETS, RANK))
    input_grad = (grad_mid + rms_backward(residual, norm_one, grad_normed_one)).astype(jnp.bfloat16)
    out_down_grad = grad_out_down.reshape(grad_out_down.shape[0], SETS, RANK)
    out_lift_grad = grad_out_lift.reshape(grad_out_lift.shape[0], SETS, RANK)
    attn_sums = (
        lax.psum_scatter(
            down_grads[0].astype(jnp.bfloat16), "shard", scatter_dimension=0, tiled=True
        ).astype(jnp.float32),
        lax.psum_scatter(
            down_grads[1].astype(jnp.bfloat16), "shard", scatter_dimension=0, tiled=True
        ).astype(jnp.float32),
        lax.psum_scatter(
            down_grads[2].astype(jnp.bfloat16), "shard", scatter_dimension=0, tiled=True
        ).astype(jnp.float32),
        lax.psum_scatter(
            out_down_grad.astype(jnp.bfloat16), "shard", scatter_dimension=0, tiled=True
        ).astype(jnp.float32),
        lax.psum_scatter(
            lift_grads[0].astype(jnp.bfloat16), "shard", scatter_dimension=0, tiled=True
        ).astype(jnp.float32),
        lax.psum_scatter(
            lift_grads[1].astype(jnp.bfloat16), "shard", scatter_dimension=0, tiled=True
        ).astype(jnp.float32),
        lax.psum_scatter(
            lift_grads[2].astype(jnp.bfloat16), "shard", scatter_dimension=0, tiled=True
        ).astype(jnp.float32),
        lax.psum_scatter(
            out_lift_grad.astype(jnp.bfloat16), "shard", scatter_dimension=0, tiled=True
        ).astype(jnp.float32),
    )
    totals = (
        lax.psum(attn_sums[0].astype(jnp.bfloat16), "rep").astype(jnp.float32),
        lax.psum(attn_sums[1].astype(jnp.bfloat16), "rep").astype(jnp.float32),
        lax.psum(attn_sums[2].astype(jnp.bfloat16), "rep").astype(jnp.float32),
        lax.psum(attn_sums[3].astype(jnp.bfloat16), "rep").astype(jnp.float32),
        lax.psum(attn_sums[4].astype(jnp.bfloat16), "rep").astype(jnp.float32),
        lax.psum(attn_sums[5].astype(jnp.bfloat16), "rep").astype(jnp.float32),
        lax.psum(attn_sums[6].astype(jnp.bfloat16), "rep").astype(jnp.float32),
        lax.psum(attn_sums[7].astype(jnp.bfloat16), "rep").astype(jnp.float32),
        lax.psum(expert_grads[0].astype(jnp.bfloat16), "rep").astype(jnp.float32),
        lax.psum(expert_grads[1].astype(jnp.bfloat16), "rep").astype(jnp.float32),
        lax.psum(expert_grads[2].astype(jnp.bfloat16), "rep").astype(jnp.float32),
        lax.psum(expert_grads[3].astype(jnp.bfloat16), "rep").astype(jnp.float32),
        lax.psum(expert_grads[4].astype(jnp.bfloat16), "rep").astype(jnp.float32),
        lax.psum(expert_grads[5].astype(jnp.bfloat16), "rep").astype(jnp.float32),
    )
    return (
        output,
        input_grad,
        totals[0],
        totals[1],
        totals[2],
        totals[3],
        totals[4],
        totals[5],
        totals[6],
        totals[7],
        totals[8],
        totals[9],
        totals[10],
        totals[11],
        totals[12],
        totals[13],
    )


def solution(mesh):
    placed = (
        P(("rep", "shard"), None),
        P(("rep", "shard"), None),
        P(("rep", "shard"), None),
        P(("rep", "shard"), None),
        P(("rep", "shard"), None),
        P(("rep", "shard"), None),
        P(("rep", "shard")),
        P(),
        P(),
        P(None, "shard"),
        P(None, "shard"),
        P(None, "shard"),
        P(None, "shard"),
        P("shard", None, None),
        P("shard", None, None),
        P("shard", None, None),
        P("shard", None, None),
        P("shard", None, None),
        P("shard", None, None),
        P("shard", None, None),
        P("shard", None, None),
        P("shard", None, None),
        P("shard", None, None),
        P("shard", None, None),
        P("shard", None, None, None),
        P("shard", None, None, None),
        P("shard", None, None, None),
        P("shard", None, None, None),
        P("shard", None, None, None),
        P("shard", None, None, None),
    )
    return jax.shard_map(
        local,
        mesh=mesh,
        in_specs=placed,
        out_specs=(
            P(("rep", "shard"), None),
            P(("rep", "shard"), None),
            P("shard", None, None),
            P("shard", None, None),
            P("shard", None, None),
            P("shard", None, None),
            P("shard", None, None),
            P("shard", None, None),
            P("shard", None, None),
            P("shard", None, None),
            P("shard", None, None, None),
            P("shard", None, None, None),
            P("shard", None, None, None),
            P("shard", None, None, None),
            P("shard", None, None, None),
            P("shard", None, None, None),
        ),
        check_vma=False,
    )
```

profile of v0, /device:TPU:0, one launch (start us, length us, event | category | flops | bytes accessed | tf_op | source)
XLA Modules:
  0.0 2025.1 jit_solution(16924291386358086777)
XLA Ops:
  54.0 464.9 %all_gather.55 = bf16[2048,2,16]{0,2,1:T(8,128)(2,1)S(1)} all-gather(bf16[512,2,16]{0,2,1:T(8,128)(2,1)S(1)} %copy-done.75), channel_id=1, replica_groups=mesh['rep'=8,'shard'=4] {'shard'}, dimensions={0}, use_global_device_ids=true | all-gather | bytes 163840 | tf_op jit(solution)/shard_map/all_gather | solution.py:270
  532.3 19.2 all_gather.52
  551.5 15.4 all_gather.53
  566.9 17.6 all_gather.49
  584.5 19.9 all_gather.50
  604.4 17.4 all_gather.58
  621.8 20.1 all_gather.59
  663.2 21.7 %all-gather.5.cloned.1.call-done = bf16[2048,2048]{1,0:T(8,128)(2,1)} async-done(((bf16[2048,512]{1,0:T(8,128)(2,1)}), bf16[2048,2048]{1,0:T(8,128)(2,1)}) %all-gather.5.cloned.1.call-update) | async-done | bytes 8388624 | tf_op jit(solution)/shard_map/all_gather | solution.py:267
  694.5 139.9 %all-gather.11.cloned.1.call-done = bf16[2048,2048]{1,0:T(8,128)(2,1)} async-done(((bf16[2048,512]{1,0:T(8,128)(2,1)}), bf16[2048,2048]{1,0:T(8,128)(2,1)}) %all-gather.11.cloned.1.call-update) | async-done | bytes 8388624 | tf_op jit(solution)/shard_map/all_gather | solution.py:268
  893.5 18.7 fusion.95
  912.2 186.2 %all-to-all-done = bf16[16,160,2048]{2,1,0:T(8,128)(2,1)} async-done(((bf16[16,160,2048]{2,1,0:T(8,128)(2,1)}), bf16[16,160,2048]{2,1,0:T(8,128)(2,1)}, u32[]{:S(2)}, u32[]{:S(2)}) %all-to-all-start) | async-done | bytes 10485792 | tf_op jit(solution)/shard_map/all_to_all | solution.py:317
  1119.3 19.9 fusion.91
  1150.2 33.1 %multiply_convert_fusion.3 = (bf16[4,640,1024]{2,1,0:T(8,128)(2,1)}, bf16[4,640,1024]{2,1,0:T(8,128)(2,1)}, bf16[4,640,1024]{2,1,0:T(8,128)(2,1)}) fusion(f32[4,640,1024]{2,1,0:T(8,128)} %fusion.93, f32[4,640,1024]{2,1,0:T(8,128)} %fusion.91, f32[4,640,1024]{2,1,0:T(8,128)} %fusion.92, f32[4,640,1024]{2,1,0:T(8,128)} %fusion.95, ...), kind=kOutput, calls=%fused_computation.12 | convolution fusion | flops 10789847040 | bytes 95420416 | tf_op jit(solution)/shard_map/nci,nio->nco/dot_general | solution.py:97
  1187.6 18.5 fusion.94
  1218.0 14.7 copy.148
  1256.1 19.4 fusion.97
  1275.4 19.5 fusion.99
  1295.0 20.2 add_convert_fusion
  1315.1 25.4 %copy.152 = bf16[4,640,2048]{2,0,1:T(4,128)(2,1)} copy(bf16[4,640,2048]{2,1,0:T(8,128)(2,1)S(1)} %add_convert_fusion) | data formatting | bytes 20971520 | tf_op jit(solution)/shard_map/convert_element_type | solution.py:200
  1340.5 126.2 %all-to-all-done.2 = bf16[4,640,2048]{2,0,1:T(4,128)(2,1)} async-done(((bf16[4,640,2048]{2,0,1:T(4,128)(2,1)}), bf16[4,640,2048]{2,0,1:T(4,128)(2,1)}, u32[]{:S(2)}, u32[]{:S(2)}) %all-to-all-start.2) | async-done | bytes 10485792 | tf_op jit(solution)/shard_map/all_to_all | solution.py:335
  1499.5 65.1 %all-reduce.7.cloned.1.call-done = (bf16[4,2048,2,16]{1,3,2,0:T(8,128)(2,1)}, bf16[4,1024,2,16]{1,3,2,0:T(8,128)(2,1)}, bf16[4,2048,2,16]{1,3,2,0:T(8,128)(2,1)}...) async-done(((bf16[4,2048,2,16]{1,3,2,0:T(8,128)(2,1)}, bf16[4,1024,2,16]{1,3,2,0:T(8,128)(2,1)}, ...) | async-done | bytes 2359312 | tf_op jit(solution)/shard_map/psum | solution.py:470
  1587.2 113.0 %all-to-all-done.4 = bf16[4,640,2048]{2,0,1:T(4,128)(2,1)} async-done(((bf16[4,640,2048]{2,0,1:T(4,128)(2,1)}), bf16[4,640,2048]{2,0,1:T(4,128)(2,1)}, u32[]{:S(2)}, u32[]{:S(2)}) %all-to-all-start.4) | async-done | bytes 10485792 | tf_op jit(solution)/shard_map/all_to_all | solution.py:361
  1700.2 13.9 copy.153
  1714.1 21.6 %gather_fusion.2 = bf16[2048,2048]{1,0:T(8,128)(2,1)} fusion(bf16[2560,2048]{1,0:T(8,128)(2,1)} %bitcast.226, s32[2048]{0:T(1024)S(1)} %fusion.71), kind=kCustom, calls=%fused_computation.clone | custom fusion | bytes 16785408 | tf_op jit(solution)/shard_map/jit(_take)/gather | solution.py:336
  1735.8 21.6 %gather_fusion.3 = bf16[2048,2048]{1,0:T(8,128)(2,1)} fusion(bf16[2560,2048]{1,0:T(8,128)(2,1)} %bitcast.227, s32[2048]{0:T(1024)S(1)} %fusion.71), kind=kCustom, calls=%fused_computation.1.clone | custom fusion | bytes 16785408 | tf_op jit(solution)/shard_map/jit(_take)/gather | solution.py:363
  1757.4 17.3 convert_reduce_fusion
  1850.8 19.7 reduce-scatter.23.cloned.1.call-done
  1870.5 19.6 reduce-scatter.11.cloned.1.call-done
  1890.0 19.7 reduce-scatter.19.cloned.1.call-done
  1909.7 19.6 reduce-scatter.9.cloned.1.call-done
  1929.3 20.2 reduce-scatter.17.cloned.1.call-done
  1953.0 54.0 %all-reduce.5.cloned.1.call-done = (bf16[512,2,16]{0,2,1:T(8,128)(2,1)}, bf16[512,2,16]{0,2,1:T(8,128)(2,1)}, bf16[512,2,16]{0,2,1:T(8,128)(2,1)}, bf16[512,2,16...) async-done(((bf16[512,2,16]{0,2,1:T(8,128)(2,1)}, ...) | async-done | bytes 262160 | tf_op jit(solution)/shard_map/psum | solution.py:462
  (379 shorter events, 365.5 us)
Async XLA Ops:
  7.2 873.0 %copy-start = (bf16[4,2048,2,16]{1,3,2,0:T(8,128)(2,1)S(1)}, bf16[4,2048,2,16]{1,3,2,0:T(8,128)(2,1)}, u32[]{:S(2)}) copy-start(bf16[4,2048,2,16]{1,3,2,0:T(8,128)(2,1)} %param.61) | copy-start | bytes 1572868
  7.2 637.2 %all-gather.9.cloned.1.call-start = ((), (), s32[]{:S(2)}) async-start(), calls=%async_computation.15 | async-start | bytes 10485760 | tf_op jit(solution)/shard_map/all_gather | solution.py:266
  7.9 645.4 %all-gather.7.cloned.1.call-start = ((), (), s32[]{:S(2)}) async-start(), calls=%async_computation.14 | async-start | bytes 10485760 | tf_op jit(solution)/shard_map/all_gather | solution.py:265
  8.7 676.1 %all-gather.5.cloned.1.call-start = ((), (), s32[]{:S(2)}) async-start(), calls=%async_computation.13 | async-start | bytes 10485760 | tf_op jit(solution)/shard_map/all_gather | solution.py:267
  10.8 36.4 %all-to-all-start.1 = ((bf16[16,160,2]{1,2,0:T(2,128)(2,1)}), bf16[16,160,2]{1,2,0:T(2,128)(2,1)S(1)}, u32[]{:S(2)}, u32[]{:S(2)}) async-start(bf16[16,160,2]{1,2,0:T(2,128)(2,1)} %broadcast_in_dim.54), calls=%async_computation.1 | async-start | bytes 32768 | tf_op jit(solution)/shard_map/all_to_all | solution.py:318
  47.0 471.9 %copy-start.76 = (bf16[512,2,16]{0,2,1:T(8,128)(2,1)S(1)}, bf16[512,2,16]{0,2,1:T(8,128)(2,1)}, u32[]{:S(2)}) copy-start(bf16[512,2,16]{0,2,1:T(8,128)(2,1)} %param.50) | copy-start | bytes 98308
  47.0 485.2 %copy-start.77 = (bf16[512,2,16]{0,2,1:T(8,128)(2,1)S(1)}, bf16[512,2,16]{0,2,1:T(8,128)(2,1)}, u32[]{:S(2)}) copy-start(bf16[512,2,16]{0,2,1:T(8,128)(2,1)} %param.45) | copy-start | bytes 98308
  47.1 504.5 %copy-start.78 = (bf16[512,2,16]{0,2,1:T(8,128)(2,1)S(1)}, bf16[512,2,16]{0,2,1:T(8,128)(2,1)}, u32[]{:S(2)}) copy-start(bf16[512,2,16]{0,2,1:T(8,128)(2,1)} %param.49) | copy-start | bytes 98308
  47.1 519.8 %copy-start.79 = (bf16[512,2,16]{0,2,1:T(8,128)(2,1)S(1)}, bf16[512,2,16]{0,2,1:T(8,128)(2,1)}, u32[]{:S(2)}) copy-start(bf16[512,2,16]{0,2,1:T(8,128)(2,1)} %param.47) | copy-start | bytes 98308
  47.1 537.4 %copy-start.80 = (bf16[512,2,16]{0,2,1:T(8,128)(2,1)S(1)}, bf16[512,2,16]{0,2,1:T(8,128)(2,1)}, u32[]{:S(2)}) copy-start(bf16[512,2,16]{0,2,1:T(8,128)(2,1)} %param.51) | copy-start | bytes 98308
  47.1 557.3 %copy-start.81 = (bf16[512,2,16]{0,2,1:T(8,128)(2,1)S(1)}, bf16[512,2,16]{0,2,1:T(8,128)(2,1)}, u32[]{:S(2)}) copy-start(bf16[512,2,16]{0,2,1:T(8,128)(2,1)} %param.48) | copy-start | bytes 98308
  47.1 574.7 %copy-start.82 = (bf16[512,2,16]{0,2,1:T(8,128)(2,1)S(1)}, bf16[512,2,16]{0,2,1:T(8,128)(2,1)}, u32[]{:S(2)}) copy-start(bf16[512,2,16]{0,2,1:T(8,128)(2,1)} %param.52) | copy-start | bytes 98308
  47.1 594.8 %copy-start.98 = (s32[1,256]{1,0:T(1,128)S(1)}, s32[1,256]{1,0:T(1,128)}, u32[]{:S(2)}) copy-start(s32[1,256]{1,0:T(1,128)} %param.35) | copy-start | bytes 3076
  47.1 594.8 %copy-start.8 = (bf16[256,2048]{1,0:T(8,128)(2,1)S(1)}, bf16[256,2048]{1,0:T(8,128)(2,1)}, u32[]{:S(2)}) copy-start(bf16[256,2048]{1,0:T(8,128)(2,1)} %param.32) | copy-start | bytes 3145732
  47.1 816.4 %all-to-all-start.3 = ((bf16[16,160,2048]{2,1,0:T(8,128)(2,1)}), bf16[16,160,2048]{2,1,0:T(8,128)(2,1)}, u32[]{:S(2)}, u32[]{:S(2)}) async-start(bf16[16,160,2048]{2,1,0:T(8,128)(2,1)} %multiply_convert_fusion), calls=%async_computation.3 | async-start | bytes 20971520 | tf_op jit(solution)/shard_map/all_to_all | solution.py:344
  53.3 589.5 %copy-start.94 = (s32[1,256]{1,0:T(1,128)S(1)}, s32[1,256]{1,0:T(1,128)}, u32[]{:S(2)}) copy-start(s32[1,256]{1,0:T(1,128)} %param.34) | copy-start | bytes 3076
  53.3 589.6 %copy-start.89 = (f32[2048]{0:T(1024)S(1)}, f32[2048]{0:T(1024)}, u32[]{:S(2)}) copy-start(f32[2048]{0:T(1024)} %param.39) | copy-start | bytes 24580
  53.3 781.1 %all-gather.11.cloned.1.call-start = ((), (), s32[]{:S(2)}) async-start(), calls=%async_computation.16 | async-start | bytes 10485760 | tf_op jit(solution)/shard_map/all_gather | solution.py:268
  54.0 640.2 %copy-start.96 = (f32[32]{0:T(128)}, f32[32]{0:T(128)S(1)}, u32[]{:S(2)}) copy-start(f32[32]{0:T(128)S(1)} %mul.389) | copy-start | bytes 388
  863.5 234.9 %all-to-all-start = ((bf16[16,160,2048]{2,1,0:T(8,128)(2,1)}), bf16[16,160,2048]{2,1,0:T(8,128)(2,1)}, u32[]{:S(2)}, u32[]{:S(2)}) async-start(bf16[16,160,2048]{2,1,0:T(8,128)(2,1)} %broadcast_select_fusion), calls=%async_computation | async-start | bytes 20971520 | tf_op jit(solution)/shard_map/all_to_all | solution.py:317
  1232.6 234.1 %all-to-all-start.2 = ((bf16[4,640,2048]{2,0,1:T(4,128)(2,1)}), bf16[4,640,2048]{2,0,1:T(4,128)(2,1)}, u32[]{:S(2)}, u32[]{:S(2)}) async-start(bf16[4,640,2048]{2,0,1:T(4,128)(2,1)} %copy.148), calls=%async_computation.2 | async-start | bytes 20971520 | tf_op jit(solution)/shard_map/all_to_all | solution.py:335
  1466.7 233.5 %all-to-all-start.4 = ((bf16[4,640,2048]{2,0,1:T(4,128)(2,1)}), bf16[4,640,2048]{2,0,1:T(4,128)(2,1)}, u32[]{:S(2)}, u32[]{:S(2)}) async-start(bf16[4,640,2048]{2,0,1:T(4,128)(2,1)} %copy.152), calls=%async_computation.4 | async-start | bytes 20971520 | tf_op jit(solution)/shard_map/all_to_all | solution.py:361
  1472.7 91.8 %all-reduce.7.cloned.1.call-start = ((), (), s32[]{:S(2)}) async-start(), calls=%async_computation.26 | async-start | bytes 4718592 | tf_op jit(solution)/shard_map/psum | solution.py:470
  1498.5 349.6 %reduce-scatter.13.cloned.1.call-start = ((), (), s32[]{:S(2)}) async-start(), calls=%async_computation.19 | async-start | bytes 163840 | tf_op jit(solution)/shard_map/reduce_scatter | solution.py:442
  1793.0 55.1 %reduce-scatter.21.cloned.1.call-start = ((), (), s32[]{:S(2)}) async-start(), calls=%async_computation.23 | async-start | bytes 163840 | tf_op jit(solution)/shard_map/reduce_scatter | solution.py:454
  1799.9 50.9 %reduce-scatter.15.cloned.1.call-start = ((), (), s32[]{:S(2)}) async-start(), calls=%async_computation.20 | async-start | bytes 163840 | tf_op jit(solution)/shard_map/reduce_scatter | solution.py:445
  1808.6 61.8 %reduce-scatter.23.cloned.1.call-start = ((), (), s32[]{:S(2)}) async-start(), calls=%async_computation.24 | async-start | bytes 163840 | tf_op jit(solution)/shard_map/reduce_scatter | solution.py:457
  1809.7 80.4 %reduce-scatter.11.cloned.1.call-start = ((), (), s32[]{:S(2)}) async-start(), calls=%async_computation.18 | async-start | bytes 163840 | tf_op jit(solution)/shard_map/reduce_scatter | solution.py:439
  1813.7 96.0 %reduce-scatter.19.cloned.1.call-start = ((), (), s32[]{:S(2)}) async-start(), calls=%async_computation.22 | async-start | bytes 163840 | tf_op jit(solution)/shard_map/reduce_scatter | solution.py:451
  1819.4 109.9 %reduce-scatter.9.cloned.1.call-start = ((), (), s32[]{:S(2)}) async-start(), calls=%async_computation.17 | async-start | bytes 163840 | tf_op jit(solution)/shard_map/reduce_scatter | solution.py:436
  1823.3 126.2 %reduce-scatter.17.cloned.1.call-start = ((), (), s32[]{:S(2)}) async-start(), calls=%async_computation.21 | async-start | bytes 163840 | tf_op jit(solution)/shard_map/reduce_scatter | solution.py:448
  1832.5 174.5 %all-reduce.5.cloned.1.call-start = ((), (), s32[]{:S(2)}) async-start(), calls=%async_computation.25 | async-start | bytes 524288 | tf_op jit(solution)/shard_map/psum | solution.py:462
  (92 other events, 2312.2 us)
Sparse Core Ops, SparseCore 0:
  9.6 261.9 all-gather.8
  273.2 251.0 all-gather.6
  525.9 158.9 all-gather.4
  686.2 148.0 all-gather.10
  1498.6 65.8 all-reduce.6
  1793.1 18.2 reduce-scatter.12
  1813.6 17.3 reduce-scatter.20
  1833.4 17.3 reduce-scatter.14
  1853.0 17.3 reduce-scatter.22
  1872.6 17.3 reduce-scatter.10
  1892.3 17.3 reduce-scatter.18
  1911.9 17.3 reduce-scatter.8
  1932.1 17.3 reduce-scatter.16
  1953.6 53.2 all-reduce.4
where the time goes:
time: 2030 us
  waiting for transfers between devices  810 us (40%)
  blocking collectives  588 us (29%)
  matrix products  333 us (16%)
  local copies, waits for them, and re-layouts  169 us (8%)
  other arithmetic  76.4 us (4%)
  starting transfers between devices  32.6 us (2%)
    all_gather x1, blocking collectives, local(): lax.all_gather(key_down, 'shard', axis=0, tiled=True)  465 us
    all_to_all x1, waiting for transfers between devices, local(): lax.all_to_all(dispatched, 'shard', split_axis=0, concat_axis=1, tiled=True)  186 us
    all_gather x1, waiting for transfers between devices, local(): lax.all_gather(output_weight, 'shard', axis=1, tiled=True)  140 us
    all_to_all x1, waiting for transfers between devices, local(): lax.all_to_all(local_out, 'shard', split_axis=1, concat_axis=0, tiled=True)  126 us
    all_to_all x1, waiting for transfers between devices, local(): lax.all_to_all(local_back[0], 'shard', split_axis=1, concat_axis=0, tiled...  113 us
    dot_general x3, matrix products, batch_adapt(): jnp.einsum('nci,nio->nco', block_of_rows, dense_weight, preferred_element...  71.6 us
    psum x1, waiting for transfers between devices, local(): lax.psum(expert_grads[0].astype(jnp.bfloat16), 'rep').astype(jnp.float32)  65.1 us
    dot_general x3, matrix products, batch_adapt_back(): jnp.einsum('nco,nio->nci', output_gradient, dense_weight, preferred_eleme...  57.6 us
  transfers between devices with their start and end apart: 19, of which 13 were waited for; matrix products, arithmetic and copies ran while one was open for 17% of the time, Pallas kernels for 0%

commit v1 on v0

v1 whole, which is shorter than its diff:
```python
import functools

import jax
import jax.numpy as jnp
from jax import lax
from jax.experimental import pallas as pl
from jax.experimental.pallas import tpu as pltpu
from jax.sharding import PartitionSpec as P

HEADS = 16
HEAD = 128
TOP = 8
EXPERTS = 16
RANK = 16
SETS = 2
MOST = 160
PACK = SETS * RANK

epsilon = 1e-06
adapter_scale = 2.0
masked_score = -1e30
score_scale = HEAD ** (-0.5)

BF = jnp.bfloat16
F32 = jnp.float32
VMEM = 56 * 1024 * 1024


def dot_nn(a, b):
    return jnp.dot(a, b, preferred_element_type=F32)


def dot_nt(a, b):
    return lax.dot_general(a, b, (((1,), (1,)), ((), ())), preferred_element_type=F32)


def dot_tn(a, b):
    return lax.dot_general(a, b, (((0,), (0,)), ((), ())), preferred_element_type=F32)


def rms_forward(values, gain_vec):
    inverse = lax.rsqrt(jnp.mean(values * values, axis=-1, keepdims=True) + epsilon)
    return values * inverse * gain_vec


def rms_backward(values, gain_vec, grad_norm):
    inverse = lax.rsqrt(jnp.mean(values * values, axis=-1, keepdims=True) + epsilon)
    weighted = grad_norm * gain_vec
    cubed = inverse * inverse * inverse
    return inverse * weighted - values * cubed * jnp.mean(values * weighted, axis=-1, keepdims=True)


def scores(q, k, allowed):
    s = dot_nt(q, k) * score_scale
    s = jnp.where(allowed, s, masked_score)
    e = jnp.exp(s - jnp.max(s, axis=-1, keepdims=True))
    return e / jnp.sum(e, axis=-1, keepdims=True)


def allowed_mask(seg_row, seg_col, pad_row):
    rows = lax.broadcasted_iota(jnp.int32, (seg_col.shape[0], seg_row.shape[1]), 0)
    cols = lax.broadcasted_iota(jnp.int32, (seg_col.shape[0], seg_row.shape[1]), 1)
    return (seg_col == seg_row) & ((pad_row == 1) | (rows == cols))


def attention_kernel(seg_row, seg_col, pad_row, q, k, v, o):
    allowed = allowed_mask(seg_row[...], seg_col[...], pad_row[...])
    for h in range(q.shape[1] // HEAD):
        at = slice(h * HEAD, (h + 1) * HEAD)
        p = scores(q[:, at], k[:, at], allowed)
        o[:, at] = dot_nn(p.astype(BF), v[:, at]).astype(BF)


def attention(masks, q, k, v):
    rows, width = q.shape
    full = pl.BlockSpec(memory_space=pltpu.VMEM)
    return pl.pallas_call(
        attention_kernel,
        in_specs=[full] * 6,
        out_specs=full,
        out_shape=jax.ShapeDtypeStruct((rows, width), BF),
        compiler_params=pltpu.CompilerParams(vmem_limit_bytes=32 * 1024 * 1024),
        cost_estimate=pl.CostEstimate(
            flops=4 * rows * rows * width,
            bytes_accessed=8 * rows * width,
            transcendentals=rows * rows * width // HEAD,
        ),
    )(*masks, q, k, v)


def attention_back_kernel(seg_row, seg_col, pad_row, q, k, v, do, dq, dk, dv):
    allowed = allowed_mask(seg_row[...], seg_col[...], pad_row[...])
    for h in range(q.shape[1] // HEAD):
        at = slice(h * HEAD, (h + 1) * HEAD)
        p = scores(q[:, at], k[:, at], allowed)
        dp = dot_nt(do[:, at], v[:, at])
        delta = jnp.sum(dp * p, axis=-1, keepdims=True)
        ds = (p * (dp - delta)).astype(BF)
        dq[:, at] = (dot_nn(ds, k[:, at]) * score_scale).astype(BF)
        dk[:, at] = (dot_tn(ds, q[:, at]) * score_scale).astype(BF)
        dv[:, at] = dot_tn(p.astype(BF), do[:, at]).astype(BF)


def attention_back(masks, q, k, v, do):
    rows, width = q.shape
    full = pl.BlockSpec(memory_space=pltpu.VMEM)
    return pl.pallas_call(
        attention_back_kernel,
        in_specs=[full] * 7,
        out_specs=[full] * 3,
        out_shape=[jax.ShapeDtypeStruct((rows, width), BF)] * 3,
        compiler_params=pltpu.CompilerParams(vmem_limit_bytes=32 * 1024 * 1024),
        cost_estimate=pl.CostEstimate(
            flops=10 * rows * rows * width,
            bytes_accessed=14 * rows * width,
            transcendentals=rows * rows * width // HEAD,
        ),
    )(*masks, q, k, v, do)


def expert_kernel(
    n_exp,
    n_ff,
    has_sum,
    h2,
    cot,
    place,
    weight,
    mask,
    w_gate,
    w_up,
    w_low,
    d_gu,
    l_gate,
    l_up,
    d_low,
    l_low,
    *refs,
):
    if has_sum:
        refs = refs[5:]
    (out, dh2, g_gu, g_lg, g_lu, g_dl, g_ll) = refs[:7]
    (x_s, dy_s, rgu_s, drl_s, sw_s, y_acc, dx_acc, rl_acc, drgu_acc, sel, y_all, dx_all) = refs[7:]
    e = pl.program_id(0)
    f = pl.program_id(1)
    keep = mask[...]
    keep_one = keep[:, :PACK]
    base = pl.multiple_of(e * MOST, MOST)

    @pl.when(f == 0)
    def _():
        slots = lax.broadcasted_iota(jnp.int32, (MOST, place.shape[2]), 0)
        hit = slots == place[0]
        pick = jnp.where(hit, 1.0, 0.0).astype(BF)
        sel[pl.ds(base, MOST), :] = pick
        sw = jnp.sum(jnp.where(hit, weight[0], 0.0), axis=1, keepdims=True)
        sw_s[...] = sw
        x = dot_nn(pick, h2[...]).astype(BF)
        dy = (dot_nn(pick, cot[...]) * sw).astype(BF)
        x_s[...] = x
        dy_s[...] = dy
        rgu_s[...] = (dot_nt(x, d_gu[0]) * keep).astype(BF)
        drl_s[...] = (adapter_scale * dot_nt(dy, l_low[0]) * keep_one).astype(BF)
        y_acc[...] = jnp.zeros_like(y_acc)
        dx_acc[...] = jnp.zeros_like(dx_acc)
        rl_acc[...] = jnp.zeros_like(rl_acc)
        drgu_acc[...] = jnp.zeros_like(drgu_acc)

    x = x_s[...]
    dy = dy_s[...]
    r_g = rgu_s[:, :PACK]
    r_u = rgu_s[:, PACK:]
    gate = dot_nn(x, w_gate[0]) + adapter_scale * dot_nn(r_g, l_gate[0])
    up = dot_nn(x, w_up[0]) + adapter_scale * dot_nn(r_u, l_up[0])
    sig = 1.0 / (1.0 + jnp.exp(-gate))
    act = gate * sig
    hidden = (act * up).astype(BF)
    rl_acc[...] += dot_nt(hidden, d_low[0])
    y_acc[...] += dot_nn(hidden, w_low[0])
    d_hidden = dot_nt(dy, w_low[0]) + dot_nn(drl_s[...], d_low[0])
    d_gate = (d_hidden * up * sig * (1.0 + gate * (1.0 - sig))).astype(BF)
    d_up = (d_hidden * act).astype(BF)
    drgu_acc[:, :PACK] += dot_nt(d_gate, l_gate[0])
    drgu_acc[:, PACK:] += dot_nt(d_up, l_up[0])
    dx_acc[...] += dot_nt(d_gate, w_gate[0]) + dot_nt(d_up, w_up[0])
    g_lg[0] = adapter_scale * dot_tn(r_g, d_gate)
    g_lu[0] = adapter_scale * dot_tn(r_u, d_up)
    g_dl[0] = dot_tn(drl_s[...], hidden)

    @pl.when(f == n_ff - 1)
    def _():
        x = x_s[...]
        dy = dy_s[...]
        r_low = (rl_acc[...] * keep_one).astype(BF)
        y = y_acc[...] + adapter_scale * dot_nn(r_low, l_low[0])
        y_all[pl.ds(base, MOST), :] = (y * sw_s[...]).astype(BF)
        dr = (adapter_scale * drgu_acc[...] * keep).astype(BF)
        dx_all[pl.ds(base, MOST), :] = (dx_acc[...] + dot_nn(dr, d_gu[0])).astype(BF)
        g_ll[0] = adapter_scale * dot_tn(r_low, dy)
        g_gu[0] = dot_tn(dr, x)

    @pl.when((f == n_ff - 1) & (e == n_exp - 1))
    def _():
        out[...] = dot_tn(sel[...], y_all[...]).astype(out.dtype)
        dh2[...] = dot_tn(sel[...], dx_all[...]).astype(dh2.dtype)


def expert_chunk(h2, cot, place, weight, mask, params, out_type, ff_block=512):
    w_gate, w_up, w_low, d_gu, l_gate, l_up, d_low, l_low = params
    n_exp, width, ff = w_gate.shape
    rows = h2.shape[0]
    n_ff = ff // ff_block
    whole = lambda e, f: (0, 0)
    per_e = lambda e, f: (e, 0, 0)
    cols = lambda e, f: (e, 0, f)
    grads = [
        (2 * PACK, width, per_e, width),
        (PACK, ff, cols, ff_block),
        (PACK, ff, cols, ff_block),
        (PACK, ff, cols, ff_block),
        (PACK, width, per_e, width),
    ]
    return pl.pallas_call(
        functools.partial(expert_kernel, n_exp, n_ff, False),
        grid=(n_exp, n_ff),
        in_specs=[
            pl.BlockSpec((rows, width), whole),
            pl.BlockSpec((rows, width), whole),
            pl.BlockSpec((1, 1, rows), per_e),
            pl.BlockSpec((1, 1, rows), per_e),
            pl.BlockSpec((1, 2 * PACK), whole),
            pl.BlockSpec((1, width, ff_block), cols),
            pl.BlockSpec((1, width, ff_block), cols),
            pl.BlockSpec((1, ff_block, width), lambda e, f: (e, f, 0)),
            pl.BlockSpec((1, 2 * PACK, width), per_e),
            pl.BlockSpec((1, PACK, ff_block), cols),
            pl.BlockSpec((1, PACK, ff_block), cols),
            pl.BlockSpec((1, PACK, ff_block), cols),
            pl.BlockSpec((1, PACK, width), per_e),
        ],
        out_specs=[
            pl.BlockSpec((rows, width), whole),
            pl.BlockSpec((rows, width), whole),
        ]
        + [pl.BlockSpec((1, g[0], g[3]), g[2]) for g in grads],
        out_shape=[
            jax.ShapeDtypeStruct((rows, width), out_type),
            jax.ShapeDtypeStruct((rows, width), out_type),
        ]
        + [jax.ShapeDtypeStruct((n_exp, g[0], g[1]), F32) for g in grads],
        scratch_shapes=[
            pltpu.VMEM((MOST, width), BF),
            pltpu.VMEM((MOST, width), BF),
            pltpu.VMEM((MOST, 2 * PACK), BF),
            pltpu.VMEM((MOST, PACK), BF),
            pltpu.VMEM((MOST, 1), F32),
            pltpu.VMEM((MOST, width), F32),
            pltpu.VMEM((MOST, width), F32),
            pltpu.VMEM((MOST, PACK), F32),
            pltpu.VMEM((MOST, 2 * PACK), F32),
            pltpu.VMEM((n_exp * MOST, rows), BF),
            pltpu.VMEM((n_exp * MOST, width), BF),
            pltpu.VMEM((n_exp * MOST, width), BF),
        ],
        compiler_params=pltpu.CompilerParams(
            vmem_limit_bytes=VMEM, dimension_semantics=("arbitrary", "arbitrary")
        ),
        cost_estimate=pl.CostEstimate(
            flops=20 * n_exp * MOST * width * ff,
            bytes_accessed=6 * n_exp * width * ff,
            transcendentals=n_exp * MOST * ff,
        ),
    )(h2, cot, place, weight, mask, w_gate, w_up, w_low, d_gu, l_gate, l_up, d_low, l_low)


def local(
    n_rep,
    n_shard,
    tokens,
    cotangent,
    segments,
    padding,
    routes,
    route_weights,
    adapter_set,
    norm_one,
    norm_two,
    query_weight,
    key_weight,
    value_weight,
    output_weight,
    query_down,
    key_down,
    value_down,
    output_down,
    query_lift,
    key_lift,
    value_lift,
    output_lift,
    expert_gate,
    expert_upper,
    expert_lower,
    gate_down,
    gate_lift,
    upper_down,
    upper_lift,
    lower_down,
    lower_lift,
):
    seq_len, width = tokens.shape
    n_exp = expert_gate.shape[0]
    cols = query_weight.shape[1]
    team = min(cols // HEAD, n_rep // 2)
    half = width // 2
    plane = lax.axis_index("shard")
    rep = lax.axis_index("rep")
    core = rep % 2
    chip = (rep // 2) % team

    def rep_swap(x, bits):
        return lax.ppermute(x, "rep", [(a, a ^ bits) for a in range(n_rep)])

    def line_gather(x):
        from_up, from_down = [x], [x]
        for _ in range(1, n_shard):
            from_up.append(
                lax.ppermute(from_up[-1], "shard", [(a, a - 1) for a in range(1, n_shard)])
            )
            from_down.append(
                lax.ppermute(from_down[-1], "shard", [(a, a + 1) for a in range(n_shard - 1)])
            )
        return [x] + [from_up[k] + from_down[n_shard - k] for k in range(1, n_shard)]

    def line_send(x, k):
        return lax.ppermute(x, "shard", [(a, (a + k) % n_shard) for a in range(n_shard)])

    def in_order(parts):
        return jnp.roll(jnp.stack(parts), plane, axis=0)

    def chip_gather(x):
        return [x] + [rep_swap(x, j << 1) for j in range(1, team)]

    def flat(table):
        return table.reshape(table.shape[0], PACK).T

    packed = jnp.concatenate(
        [
            flat(t)
            for t in (
                query_down,
                key_down,
                value_down,
                output_down,
                query_lift,
                key_lift,
                value_lift,
                output_lift,
            )
        ],
        axis=0,
    )
    groups = 2 * team
    group = chip * 2 + core
    pack_rows = 8 * PACK // groups
    pack_own = lax.dynamic_slice(packed, (group * pack_rows, 0), (pack_rows, cols))
    pack_line = in_order(line_gather(pack_own))
    pack_line = pack_line.transpose(1, 0, 2).reshape(pack_rows, width)
    pack_same = jnp.stack(chip_gather(pack_line))
    pack_other = rep_swap(pack_same, 1)
    pack_all = jnp.stack([pack_same, pack_other], axis=1).reshape(groups, pack_rows, width)
    pack_all = jnp.take(pack_all, jnp.arange(groups) ^ group, axis=0).reshape(8, PACK, width)
    downs, lifts = pack_all[:4], pack_all[4:]

    def own_block(weight):
        block = lax.dynamic_slice(weight, (core * half, chip * HEAD), (half, HEAD))
        block = in_order(line_gather(block))
        return block.transpose(1, 0, 2).reshape(half, n_shard * HEAD)

    def share(block):
        same = chip_gather(block)
        return same, [rep_swap(b, 1) for b in same]

    blocks = [share(own_block(w)) for w in (query_weight, key_weight, value_weight)]
    out_rows = output_weight.reshape(2, n_shard // 2, cols // HEAD, HEAD, cols)
    out_own = lax.dynamic_slice(
        out_rows, (core, 0, chip, 0, 0), (1, n_shard // 2, 1, HEAD, cols)
    ).reshape(n_shard // 2 * HEAD, cols)
    out_own = in_order(line_gather(out_own)).transpose(1, 0, 2).reshape(-1, width)
    out_same, out_other = share(out_own)

    def chip_cols(table, j):
        parts = table.reshape(table.shape[0], n_shard, team, HEAD)
        return lax.dynamic_index_in_dim(parts, chip ^ j, 2, keepdims=False).reshape(
            table.shape[0], n_shard * HEAD
        )

    def pick_half(x, which):
        size = x.shape[1] // 2
        return lax.dynamic_slice(x, (0, which * size), (x.shape[0], size))

    chosen_set = adapter_set[0]
    set_flags = (jnp.arange(SETS, dtype=jnp.int32) == chosen_set).astype(F32)
    keep = jnp.repeat(set_flags, RANK)[None]
    masks = (segments, segments.reshape(seq_len, 1), padding)
    residual = tokens.astype(F32)
    normed_one = rms_forward(residual, norm_one).astype(BF)
    near, far = pick_half(normed_one, core), pick_half(normed_one, 1 - core)
    reduced = [(dot_nt(normed_one, downs[a]) * keep).astype(BF) for a in range(3)]

    def project(a, j):
        same, other = blocks[a]
        y = dot_nn(near, same[j]) + dot_nn(far, other[j])
        y = y + adapter_scale * dot_nn(reduced[a], chip_cols(lifts[a], j))
        return y.astype(BF)

    heads = [[project(a, j) for a in range(3)] for j in range(team)]
    mixed = [attention(masks, *heads[j]) for j in range(team)]
    reduced_out = sum(dot_nt(mixed[j], chip_cols(downs[3], j)) for j in range(team))
    reduced_out = (reduced_out * keep).astype(BF)
    attn_out = adapter_scale * dot_nn(reduced_out, lifts[3])
    for j in range(team):
        attn_out = attn_out + dot_nn(pick_half(mixed[j], core), out_same[j])
        attn_out = attn_out + dot_nn(pick_half(mixed[j], 1 - core), out_other[j])
    after_attn = residual + attn_out
    normed_two = rms_forward(after_attn, norm_two).astype(BF)

    expert_ids = jnp.arange(EXPERTS, dtype=jnp.int32)
    picked = routes[:, :, None] == expert_ids[None, None, :]
    member = jnp.sum(picked.astype(jnp.int32), axis=1)
    before = jnp.cumsum(member, axis=0) - member
    place = jnp.where(member == 1, before, -1).T
    per_expert = jnp.sum(jnp.where(picked, route_weights[:, :, None], 0.0), axis=1).T
    info = jnp.concatenate(
        [
            place.astype(F32),
            per_expert,
            jnp.broadcast_to(chosen_set.astype(F32), (8, seq_len)),
        ],
        axis=0,
    )
    info_line = line_gather(info)
    cot_line = line_gather(cotangent)
    rows_line = line_gather(normed_two)
    params = (
        expert_gate,
        expert_upper,
        expert_lower,
        jnp.concatenate(
            [t.reshape(n_exp, width, PACK).transpose(0, 2, 1) for t in (gate_down, upper_down)],
            axis=1,
        ),
        gate_lift.reshape(n_exp, -1, PACK).transpose(0, 2, 1),
        upper_lift.reshape(n_exp, -1, PACK).transpose(0, 2, 1),
        lower_down.reshape(n_exp, -1, PACK).transpose(0, 2, 1),
        lower_lift.reshape(n_exp, width, PACK).transpose(0, 2, 1),
    )

    def chunk(k):
        line = info_line[k]
        at = plane * n_exp
        spot = lax.dynamic_slice(line, (at, 0), (n_exp, seq_len)).astype(jnp.int32)
        share_of = lax.dynamic_slice(line, (EXPERTS + at, 0), (n_exp, seq_len))
        row_set = line[2 * EXPERTS, 0].astype(jnp.int32)
        flags = (jnp.arange(SETS, dtype=jnp.int32) == row_set).astype(F32)
        mask = jnp.tile(jnp.repeat(flags, RANK), 2)[None]
        return expert_chunk(
            rows_line[k],
            cot_line[k],
            spot[:, None, :],
            share_of[:, None, :],
            mask,
            params,
            F32 if k == 0 else BF,
        )

    order = sorted(range(n_shard), key=lambda k: (k != 0, abs(2 * k - n_shard), k))
    results = {k: chunk(k) for k in order}
    dh2 = results[0][1]
    for k in order[1:]:
        dh2 = dh2 + line_send(results[k][1], k).astype(F32)
    output = after_attn + results[0][0]
    for k in order[1:]:
        output = output + line_send(results[k][0], k).astype(F32)
    output = output.astype(BF)
    expert_sums = [sum(results[k][2 + a] for k in order) for a in range(5)]
    expert_flat = jnp.concatenate(
        [g.astype(BF).reshape(-1, width) for g in expert_sums], axis=0
    )
    expert_flat = lax.psum(expert_flat, "rep")

    grad_after = cotangent.astype(F32)
    grad_mid = grad_after + rms_backward(after_attn, norm_two, dh2)
    grad_attn = grad_mid.astype(BF)
    d_reduced_out = (adapter_scale * dot_nt(grad_attn, lifts[3]) * keep).astype(BF)
    grad_out_lift = adapter_scale * dot_tn(reduced_out, grad_attn)

    def halves(a, b):
        return jnp.where(
            core == 0, jnp.concatenate([a, b], axis=1), jnp.concatenate([b, a], axis=1)
        )

    def grad_heads(j):
        g = halves(dot_nt(grad_attn, out_same[j]), dot_nt(grad_attn, out_other[j]))
        return (g + dot_nn(d_reduced_out, chip_cols(downs[3], j))).astype(BF)

    back = [attention_back(masks, *heads[j], grad_heads(j)) for j in range(team)]

    def from_chips(parts):
        stacked = jnp.stack([p.reshape(p.shape[0], n_shard, HEAD) for p in parts])
        stacked = jnp.take(stacked, jnp.arange(team) ^ chip, axis=0)
        return stacked.transpose(1, 2, 0, 3).reshape(parts[0].shape[0], width)

    down_grads, lift_grads = [], []
    near_grad = jnp.zeros((seq_len, half), F32)
    far_grad = jnp.zeros((seq_len, half), F32)
    low_grad = jnp.zeros((seq_len, width), F32)
    for a in range(3):
        dr = sum(dot_nt(back[j][a], chip_cols(lifts[a], j)) for j in range(team))
        dr = (adapter_scale * dr * keep).astype(BF)
        lift_grads.append(
            from_chips([adapter_scale * dot_tn(reduced[a], back[j][a]) for j in range(team)])
        )
        down_grads.append(dot_tn(dr, normed_one))
        low_grad = low_grad + dot_nn(dr, downs[a])
        for j in range(team):
            near_grad = near_grad + dot_nt(back[j][a], blocks[a][0][j])
            far_grad = far_grad + dot_nt(back[j][a], blocks[a][1][j])
    down_grads.append(from_chips([dot_tn(d_reduced_out, mixed[j]) for j in range(team)]))
    lift_grads.append(grad_out_lift)
    grad_normed_one = low_grad + halves(near_grad, far_grad)
    input_grad = (grad_mid + rms_backward(residual, norm_one, grad_normed_one)).astype(BF)
    attn_flat = jnp.stack(down_grads + lift_grads).astype(BF)
    attn_flat = attn_flat.reshape(8 * PACK, n_shard, cols).transpose(1, 0, 2)
    attn_flat = lax.psum_scatter(attn_flat, "shard", scatter_dimension=0, tiled=True)
    attn_flat = lax.psum(attn_flat.reshape(8 * PACK, cols), "rep").astype(F32)

    def unflat(g):
        return g.T.reshape(cols, SETS, RANK)

    attn_outs = [unflat(attn_flat[a * PACK : (a + 1) * PACK]) for a in range(8)]

    ff = expert_gate.shape[2]
    sizes = [(2 * PACK, width), (PACK, ff), (PACK, ff), (PACK, ff), (PACK, width)]
    parts, start = [], 0
    for height, long in sizes:
        count = n_exp * height * long // width
        parts.append(expert_flat[start : start + count].astype(F32).reshape(n_exp, height, long))
        start += count

    def restore(g):
        return g.transpose(0, 2, 1).reshape(n_exp, -1, SETS, RANK)

    expert_outs = [
        restore(parts[0][:, :PACK]),
        restore(parts[1]),
        restore(parts[0][:, PACK:]),
        restore(parts[2]),
        restore(parts[3]),
        restore(parts[4]),
    ]
    return (output, input_grad, *attn_outs, *expert_outs)


def solution(mesh):
    rows = P(("rep", "shard"), None)
    second = P(None, "shard")
    three = P("shard", None, None)
    four = P("shard", None, None, None)
    placed = (rows,) * 6 + (P(("rep", "shard")), P(), P()) + (second,) * 4
    placed = placed + (three,) * 11 + (four,) * 6
    return jax.shard_map(
        functools.partial(local, mesh.shape["rep"], mesh.shape["shard"]),
        mesh=mesh,
        in_specs=placed,
        out_specs=(rows, rows) + (three,) * 8 + (four,) * 6,
        check_vma=False,
    )
```

time: 2030 us -> 1040 us (0.51)
  blocking collectives: 588 us -> 0 us
  waiting for transfers between devices: 810 us -> 319 us
  matrix products: 333 us -> 82.2 us
  starting transfers between devices: 32.6 us -> 256 us
  Pallas kernels: 0 us -> 188 us
  local copies, waits for them, and re-layouts: 169 us -> 86.6 us
    all_gather x8 -> x0, blocking collectives: 588 us -> none  [the longest x1 465 us: local(): lax.all_gather(key_down, 'shard', axis=0, tiled=True)]
    all_to_all x5 -> x0, waiting for transfers between devices: 425 us -> none  [the longest x1 186 us: local(): lax.all_to_all(dispatched, 'shard', split_axis=0, concat_axis=1, tiled=True)]
    ppermute x0 -> x86, starting transfers between devices: none -> 256 us  [the longest x24 112 us: line_gather(): lax.ppermute(from_down[-1], 'shard', [(a, a + 1) for a in range(n_shard -...]
    ppermute x0 -> x86, waiting for transfers between devices: none -> 255 us  [the longest x32 157 us: rep_swap(): return lax.ppermute(x, 'rep', [(a, a ^ bits) for a in range(n_rep)])]
    dot_general x62 -> x124, matrix products: 333 us -> 82.2 us  [the longest x52 42 us: dot_nt(): lax.dot_general(a, b, (((1,), (1,)), ((), ())), preferred_element_type=F32)]
    pallas_call x0 -> x12, Pallas kernels: none -> 188 us  [the longest x4 174 us: expert_chunk(): pl.pallas_call(functools.partial(expert_kernel, n_exp, n_ff, False), grid...]
    all_gather x4 -> x0, waiting for transfers between devices: 162 us -> none  [the longest x1 140 us: local(): lax.all_gather(output_weight, 'shard', axis=1, tiled=True)]
    reduce_scatter x8 -> x1, waiting for transfers between devices: 101 us -> 2.9 us  [local(): lax.psum_scatter(attn_flat, 'shard', scatter_dimension=0, tiled=True)]
  transfers between devices with their start and end apart: 19 -> 88, of which waited for: 13 -> 22; matrix products, arithmetic and copies ran while one was open for 17% -> 13% of each run, Pallas kernels for 0% -> 17%
where the time goes in v1:
time: 1040 us; the launch traced here: 1030 us
  waiting for transfers between devices  319 us (31%)
  starting transfers between devices  256 us (25%)
  Pallas kernels  188 us (18%)
  local copies, waits for them, and re-layouts  86.6 us (8%)
  matrix products  82.2 us (8%)
  other arithmetic  73.7 us (7%)
  between operations  20.9 us (2%)
    pallas_call x4, Pallas kernels, expert_chunk(): pl.pallas_call(functools.partial(expert_kernel, n_exp, n_ff, False), grid...  174 us
    ppermute x32, waiting for transfers between devices, rep_swap(): return lax.ppermute(x, 'rep', [(a, a ^ bits) for a in range(n_rep)])  157 us
    ppermute x24, starting transfers between devices, line_gather(): lax.ppermute(from_down[-1], 'shard', [(a, a + 1) for a in range(n_shard -...  112 us
    ppermute x6, starting transfers between devices, line_send(): lax.ppermute(x, 'shard', [(a, (a + k) % n_shard) for a in range(n_shard)])  87.4 us
    psum x1, waiting for transfers between devices, local(): attn_flat = lax.psum(attn_flat.reshape(8 * PACK, cols), 'rep').astype(F32)  61.2 us
    ppermute x6, waiting for transfers between devices, line_send(): lax.ppermute(x, 'shard', [(a, (a + k) % n_shard) for a in range(n_shard)])  49.7 us
    dot_general x52, matrix products, dot_nt(): lax.dot_general(a, b, (((1,), (1,)), ((), ())), preferred_element_type=F32)  42 us
    ppermute x24, starting transfers between devices, line_gather(): lax.ppermute(from_up[-1], 'shard', [(a, a - 1) for a in range(1, n_shard)])  32 us
  transfers between devices with their start and end apart: 88, of which 22 were waited for; matrix products, arithmetic and copies ran while one was open for 13% of the time, Pallas kernels for 17%

profile of v1, /device:TPU:0, one launch (start us, length us, event | category | flops | bytes accessed | tf_op | source)
XLA Modules:
  0.0 1026.6 jit_solution(9926787292581831405)
XLA Ops:
  14.2 4.9 collective-permute-start.8
  24.5 5.9 collective-permute-start.25
  42.8 4.8 collective-permute-start.10
  64.7 5.3 collective-permute-start.18
  73.6 5.3 collective-permute-start.1
  80.2 5.3 collective-permute-start.26
  86.7 5.3 collective-permute-start.19
  98.2 5.2 collective-permute-start.2
  108.3 5.3 collective-permute-start.51
  116.9 5.9 collective-permute-start.27
  136.8 9.0 collective-permute-done.29
  188.4 9.6 collective-permute-done.35
  200.0 20.5 %collective-permute-done.33 = bf16[1024,512]{0,1:T(8,128)(2,1)S(1)} collective-permute-done((bf16[1024,512]{0,1:T(8,128)(2,1)S(1)}, bf16[1024,512]{0,1:T(8,128)(2,1)S(1)}, u32[]{:S(2)}, u32[]{:S(2)}) %collective-permute-start.33) | collective-permute-done | bytes 1048608 | tf_op jit(solution)/shard_map/ppermute | solution.py:321
  222.4 19.6 %collective-permute-done.31 = bf16[1024,512]{0,1:T(8,128)(2,1)S(1)} collective-permute-done((bf16[1024,512]{0,1:T(8,128)(2,1)S(1)}, bf16[1024,512]{0,1:T(8,128)(2,1)S(1)}, u32[]{:S(2)}, u32[]{:S(2)}) %collective-permute-start.31) | collective-permute-done | bytes 1048608 | tf_op jit(solution)/shard_map/ppermute | solution.py:321
  249.1 72.7 %collective-permute-done.37 = bf16[1024,512]{0,1:T(8,128)(2,1)S(1)} collective-permute-done((bf16[1024,512]{0,1:T(8,128)(2,1)S(1)}, bf16[1024,512]{0,1:T(8,128)(2,1)S(1)}, u32[]{:S(2)}, u32[]{:S(2)}) %collective-permute-start.37) | collective-permute-done | bytes 1048608 | tf_op jit(solution)/shard_map/ppermute | solution.py:321
  345.2 12.7 %collective-permute-done.56 = bf16[256,2048]{0,1:T(8,128)(2,1)S(1)} collective-permute-done((bf16[256,2048]{0,1:T(8,128)(2,1)S(1)}, bf16[256,2048]{0,1:T(8,128)(2,1)S(1)}, u32[]{:S(2)}, u32[]{:S(2)}) %collective-permute-start.56) | collective-permute-done | bytes 1048608 | tf_op jit(solution)/shard_map/ppermute | solution.py:321
  358.0 5.5 collective-permute-start.68
  364.0 18.7 %collective-permute-done.58 = bf16[256,2048]{0,1:T(8,128)(2,1)S(1)} collective-permute-done((bf16[256,2048]{0,1:T(8,128)(2,1)S(1)}, bf16[256,2048]{0,1:T(8,128)(2,1)S(1)}, u32[]{:S(2)}, u32[]{:S(2)}) %collective-permute-start.58) | collective-permute-done | bytes 1048608 | tf_op jit(solution)/shard_map/ppermute | solution.py:321
  387.6 6.8 collective-permute-start.69
  409.9 29.7 %collective-permute-done.72 = f32[40,256]{1,0:T(8,128)S(1)} collective-permute-done((f32[40,256]{1,0:T(8,128)S(1)}, f32[40,256]{1,0:T(8,128)S(1)}, u32[]{:S(2)}, u32[]{:S(2)}) %collective-permute-start.72) | collective-permute-done | bytes 40992 | tf_op jit(solution)/shard_map/ppermute | solution.py:330
  440.9 5.0 collective-permute-done.71
  477.5 5.2 collective-permute-start.65
  482.7 43.9 %shard_map.409 = (f32[256,2048]{1,0:T(8,128)}, f32[256,2048]{1,0:T(8,128)}, f32[4,64,2048]{2,1,0:T(8,128)}, f32[4,32,1024]{2,1,0:T(8,128)}, f32[4,32,1024]{2,1,0...) custom-call(bf16[256,2048]{1,0:T(8,128)(2,1)} %multiply_convert_fusion.h2, bf16[256,2048]{1,0:T(8,128)(2,1)} %cot.1, ...), custom_call_target="tpu_custom_call" | custom-call | flops 26843545600 | bytes 50331648 | tf_op jit(solution)/shard_map/pallas_call | solution.py:223
  537.2 43.3 %shard_map.410 = (bf16[256,2048]{1,0:T(8,128)(2,1)}, bf16[256,2048]{1,0:T(8,128)(2,1)}, f32[4,64,2048]{2,1,0:T(8,128)}, f32[4,32,1024]{2,1,0:T(8,128)}, f32[4,32...) custom-call(bf16[256,2048]{1,0:T(8,128)(2,1)} %add.615.h2, bf16[256,2048]{1,0:T(8,128)(2,1)} %add.616.cot, ...), custom_call_target="tpu_custom_call" | custom-call | flops 26843545600 | bytes 50331648 | tf_op jit(solution)/shard_map/pallas_call | solution.py:223
  587.5 43.4 %shard_map.411 = (bf16[256,2048]{1,0:T(8,128)(2,1)}, bf16[256,2048]{1,0:T(8,128)(2,1)}, f32[4,64,2048]{2,1,0:T(8,128)}, f32[4,32,1024]{2,1,0:T(8,128)}, f32[4,32...) custom-call(bf16[256,2048]{1,0:T(8,128)(2,1)} %add.619.h2, bf16[256,2048]{1,0:T(8,128)(2,1)} %add.620.cot, ...), custom_call_target="tpu_custom_call" | custom-call | flops 26843545600 | bytes 50331648 | tf_op jit(solution)/shard_map/pallas_call | solution.py:223
  635.0 43.4 %shard_map.412 = (bf16[256,2048]{1,0:T(8,128)(2,1)}, bf16[256,2048]{1,0:T(8,128)(2,1)}, f32[4,64,2048]{2,1,0:T(8,128)}, f32[4,32,1024]{2,1,0:T(8,128)}, f32[4,32...) custom-call(bf16[256,2048]{1,0:T(8,128)(2,1)} %add.623.h2, bf16[256,2048]{1,0:T(8,128)(2,1)} %add.624.cot, ...), custom_call_target="tpu_custom_call" | custom-call | flops 26843545600 | bytes 50331648 | tf_op jit(solution)/shard_map/pallas_call | solution.py:223
  678.4 20.0 %collective-permute-start.85 = (bf16[256,2048]{1,0:T(8,128)(2,1)}, bf16[256,2048]{1,0:T(8,128)(2,1)}, u32[]{:S(2)}, u32[]{:S(2)}) collective-permute-start(bf16[256,2048]{1,0:T(8,128)(2,1)} %get-tuple-element.65), channel_id=1, source_target_pairs={{0,3},{1,0},{2,1},{3,2},{4,7},{5,4},{6,5},{7,6},{8,11},{9,8},{10,9... | collective-permute-start | bytes 3145736 | tf_op jit(solution)/shard_map/ppermute | solution.py:335
  698.4 61.1 %collective-permute-start.78 = (bf16[256,2048]{1,0:T(8,128)(2,1)}, bf16[256,2048]{1,0:T(8,128)(2,1)}, u32[]{:S(2)}, u32[]{:S(2)}) collective-permute-start(bf16[256,2048]{1,0:T(8,128)(2,1)} %get-tuple-element.60), channel_id=1, source_target_pairs={{0,1},{1,2},{2,3},{3,0},{4,5},{5,6},{6,7},{7,4},{8,9},{9,10},{10,1... | collective-permute-start | bytes 3145736 | tf_op jit(solution)/shard_map/ppermute | solution.py:335
  775.2 30.6 %collective-permute-done.85 = bf16[256,2048]{1,0:T(8,128)(2,1)} collective-permute-done((bf16[256,2048]{1,0:T(8,128)(2,1)}, bf16[256,2048]{1,0:T(8,128)(2,1)}, u32[]{:S(2)}, u32[]{:S(2)}) %collective-permute-start.85) | collective-permute-done | bytes 1048608 | tf_op jit(solution)/shard_map/ppermute | solution.py:335
  808.3 19.1 %collective-permute-done.82 = bf16[256,2048]{1,0:T(8,128)(2,1)S(1)} collective-permute-done((bf16[256,2048]{1,0:T(8,128)(2,1)}, bf16[256,2048]{1,0:T(8,128)(2,1)S(1)}, u32[]{:S(2)}, u32[]{:S(2)}) %collective-permute-start.82) | collective-permute-done | bytes 1048608 | tf_op jit(solution)/shard_map/ppermute | solution.py:335
  827.4 6.6 fusion.226
  946.7 61.2 %all-reduce.3.cloned.1.call-done = (bf16[256,512]{1,0:T(8,128)(2,1)}, bf16[576,2048]{1,0:T(8,128)(2,1)}) async-done(((bf16[256,512]{1,0:T(8,128)(2,1)}, bf16[576,2048]{1,0:T(8,128)(2,1)}), (bf16[256,512]{1,0:T(8,128)(2,1)}, bf16[576,2048]{1,0:T(8,128)(2,1)})) %all-reduce.3.cloned.1.call-update) | async-done | bytes 2621456 | tf_op jit(solution)/shard_map/psum | solution.py:535
  (866 shorter events, 365.1 us)
Async XLA Ops:
  7.2 933.5 %reduce-scatter.2.cloned.1.call-start = ((), (), s32[]{:S(2)}) async-start(), calls=%async_computation.1 | async-start | bytes 1310720 | tf_op jit(solution)/shard_map/reduce_scatter | solution.py:534
  23.2 50.4 %collective-permute-start.24 = (bf16[1024,128]{0,1:T(8,128)(2,1)S(1)}, bf16[1024,128]{0,1:T(8,128)(2,1)}, u32[]{:S(2)}, u32[]{:S(2)}) collective-permute-start(bf16[1024,128]{0,1:T(8,128)(2,1)S(1)} %copy.306), channel_id=1, source_target_pairs={{1,0},{2,1},{3,2},{5,4},{6,5},{7,6},{9,8},{10,9},{11,10},{13,12},{... | collective-permute-start | bytes 786440 | tf_op jit(solution)/shard_map/ppermute | solution.py:327
  24.5 54.4 %collective-permute-start.25 = (bf16[1024,128]{0,1:T(8,128)(2,1)S(1)}, bf16[1024,128]{0,1:T(8,128)(2,1)}, u32[]{:S(2)}, u32[]{:S(2)}) collective-permute-start(bf16[1024,128]{0,1:T(8,128)(2,1)S(1)} %copy.306), channel_id=1, source_target_pairs={{0,1},{1,2},{2,3},{4,5},{5,6},{6,7},{8,9},{9,10},{10,11},{12,13},{... | collective-permute-start | bytes 786440 | tf_op jit(solution)/shard_map/ppermute | solution.py:330
  107.0 277.7 %collective-permute-start.66 = (bf16[256,2048]{1,0:T(8,128)(2,1)}, bf16[256,2048]{1,0:T(8,128)(2,1)}, u32[]{:S(2)}, u32[]{:S(2)}) collective-permute-start(bf16[256,2048]{1,0:T(8,128)(2,1)} %cot.1), channel_id=1, source_target_pairs={{1,0},{2,1},{3,2},{5,4},{6,5},{7,6},{9,8},{10,9},{11,10},{13,12},{... | collective-permute-start | bytes 3145736 | tf_op jit(solution)/shard_map/ppermute | solution.py:327
  108.3 49.9 %collective-permute-start.51 = (bf16[256,512]{0,1:T(8,128)(2,1)S(1)}, bf16[256,512]{0,1:T(8,128)(2,1)}, u32[]{:S(2)}, u32[]{:S(2)}) collective-permute-start(bf16[256,512]{0,1:T(8,128)(2,1)S(1)} %collective-permute-done.50), channel_id=1, source_target_pairs={{0,1},{1,2},{2,3},{4,5},{5,6},{6,7},{8,9},{9,10},{10,11},{12,13},{... | collective-permute-start | bytes 786440 | tf_op jit(solution)/shard_map/ppermute | solution.py:330
  113.5 49.3 %collective-permute-start.53 = (bf16[256,512]{0,1:T(8,128)(2,1)}, bf16[256,512]{0,1:T(8,128)(2,1)}, u32[]{:S(2)}, u32[]{:S(2)}) collective-permute-start(bf16[256,512]{0,1:T(8,128)(2,1)} %collective-permute-done.49), channel_id=1, source_target_pairs={{1,0},{2,1},{3,2},{5,4},{6,5},{7,6},{9,8},{10,9},{11,10},{13,12},{... | collective-permute-start | bytes 786440 | tf_op jit(solution)/shard_map/ppermute | solution.py:327
  182.5 59.5 %collective-permute-start.31 = (bf16[1024,512]{0,1:T(8,128)(2,1)S(1)}, bf16[1024,512]{0,1:T(8,128)(2,1)S(1)}, u32[]{:S(2)}, u32[]{:S(2)}) collective-permute-start(bf16[1024,512]{0,1:T(8,128)(2,1)S(1)} %bitcast.543), channel_id=1, source_target_pairs={{0,8},{4,12},{8,0},{12,4},{16,24},{20,28},{24,16},{28,20},{1,9},{5... | collective-permute-start | bytes 3145736 | tf_op jit(solution)/shard_map/ppermute | solution.py:321
  184.6 60.4 %collective-permute-start.41 = (bf16[1024,512]{0,1:T(8,128)(2,1)S(1)}, bf16[1024,512]{0,1:T(8,128)(2,1)S(1)}, u32[]{:S(2)}, u32[]{:S(2)}) collective-permute-start(bf16[1024,512]{0,1:T(8,128)(2,1)S(1)} %bitcast.532), channel_id=1, source_target_pairs={{0,16},{4,20},{8,24},{12,28},{16,0},{20,4},{24,8},{28,12},{1,17},{... | collective-permute-start | bytes 3145736 | tf_op jit(solution)/shard_map/ppermute | solution.py:321
  198.0 48.0 %collective-permute-start.39 = (bf16[1024,512]{0,1:T(8,128)(2,1)S(1)}, bf16[1024,512]{0,1:T(8,128)(2,1)S(1)}, u32[]{:S(2)}, u32[]{:S(2)}) collective-permute-start(bf16[1024,512]{0,1:T(8,128)(2,1)S(1)} %bitcast.538), channel_id=1, source_target_pairs={{0,16},{4,20},{8,24},{12,28},{16,0},{20,4},{24,8},{28,12},{1,17},{... | collective-permute-start | bytes 3145736 | tf_op jit(solution)/shard_map/ppermute | solution.py:321
  220.5 101.3 %collective-permute-start.37 = (bf16[1024,512]{0,1:T(8,128)(2,1)S(1)}, bf16[1024,512]{0,1:T(8,128)(2,1)S(1)}, u32[]{:S(2)}, u32[]{:S(2)}) collective-permute-start(bf16[1024,512]{0,1:T(8,128)(2,1)S(1)} %bitcast.544), channel_id=1, source_target_pairs={{0,16},{4,20},{8,24},{12,28},{16,0},{20,4},{24,8},{28,12},{1,17},{... | collective-permute-start | bytes 3145736 | tf_op jit(solution)/shard_map/ppermute | solution.py:321
  242.0 80.2 %collective-permute-start.47 = (bf16[1024,512]{0,1:T(8,128)(2,1)S(1)}, bf16[1024,512]{0,1:T(8,128)(2,1)S(1)}, u32[]{:S(2)}, u32[]{:S(2)}) collective-permute-start(bf16[1024,512]{0,1:T(8,128)(2,1)S(1)} %bitcast.533), channel_id=1, source_target_pairs={{0,24},{4,28},{8,16},{12,20},{16,8},{20,12},{24,0},{28,4},{1,25},{... | collective-permute-start | bytes 3145736 | tf_op jit(solution)/shard_map/ppermute | solution.py:321
  245.0 78.4 %collective-permute-start.45 = (bf16[1024,512]{0,1:T(8,128)(2,1)S(1)}, bf16[1024,512]{0,1:T(8,128)(2,1)S(1)}, u32[]{:S(2)}, u32[]{:S(2)}) collective-permute-start(bf16[1024,512]{0,1:T(8,128)(2,1)S(1)} %bitcast.539), channel_id=1, source_target_pairs={{0,24},{4,28},{8,16},{12,20},{16,8},{20,12},{24,0},{28,4},{1,25},{... | collective-permute-start | bytes 3145736 | tf_op jit(solution)/shard_map/ppermute | solution.py:321
  246.0 77.9 %collective-permute-start.43 = (bf16[1024,512]{0,1:T(8,128)(2,1)S(1)}, bf16[1024,512]{0,1:T(8,128)(2,1)S(1)}, u32[]{:S(2)}, u32[]{:S(2)}) collective-permute-start(bf16[1024,512]{0,1:T(8,128)(2,1)S(1)} %bitcast.545), channel_id=1, source_target_pairs={{0,24},{4,28},{8,16},{12,20},{16,8},{20,12},{24,0},{28,4},{1,25},{... | collective-permute-start | bytes 3145736 | tf_op jit(solution)/shard_map/ppermute | solution.py:321
  334.9 47.7 %collective-permute-start.58 = (bf16[256,2048]{0,1:T(8,128)(2,1)S(1)}, bf16[256,2048]{0,1:T(8,128)(2,1)S(1)}, u32[]{:S(2)}, u32[]{:S(2)}) collective-permute-start(bf16[256,2048]{0,1:T(8,128)(2,1)S(1)} %bitcast.550), channel_id=1, source_target_pairs={{0,16},{4,20},{8,24},{12,28},{16,0},{20,4},{24,8},{28,12},{1,17},{... | collective-permute-start | bytes 3145736 | tf_op jit(solution)/shard_map/ppermute | solution.py:321
  337.0 45.6 %collective-permute-start.60 = (bf16[256,2048]{0,1:T(8,128)(2,1)S(1)}, bf16[256,2048]{0,1:T(8,128)(2,1)S(1)}, u32[]{:S(2)}, u32[]{:S(2)}) collective-permute-start(bf16[256,2048]{0,1:T(8,128)(2,1)S(1)} %bitcast.551), channel_id=1, source_target_pairs={{0,24},{4,28},{8,16},{12,20},{16,8},{20,12},{24,0},{28,4},{1,25},{... | collective-permute-start | bytes 3145736 | tf_op jit(solution)/shard_map/ppermute | solution.py:321
  386.3 85.7 %collective-permute-start.67 = (bf16[256,2048]{1,0:T(8,128)(2,1)}, bf16[256,2048]{1,0:T(8,128)(2,1)}, u32[]{:S(2)}, u32[]{:S(2)}) collective-permute-start(bf16[256,2048]{1,0:T(8,128)(2,1)} %collective-permute-done.66), channel_id=1, source_target_pairs={{1,0},{2,1},{3,2},{5,4},{6,5},{7,6},{9,8},{10,9},{11,10},{13,12},{... | collective-permute-start | bytes 3145736 | tf_op jit(solution)/shard_map/ppermute | solution.py:327
  387.6 80.5 %collective-permute-start.69 = (bf16[256,2048]{1,0:T(8,128)(2,1)}, bf16[256,2048]{1,0:T(8,128)(2,1)}, u32[]{:S(2)}, u32[]{:S(2)}) collective-permute-start(bf16[256,2048]{1,0:T(8,128)(2,1)} %collective-permute-done.68), channel_id=1, source_target_pairs={{0,1},{1,2},{2,3},{4,5},{5,6},{6,7},{8,9},{9,10},{10,11},{12,13},{... | collective-permute-start | bytes 3145736 | tf_op jit(solution)/shard_map/ppermute | solution.py:330
  400.1 76.1 %collective-permute-start.62 = (bf16[256,2048]{1,0:T(8,128)(2,1)}, bf16[256,2048]{1,0:T(8,128)(2,1)}, u32[]{:S(2)}, u32[]{:S(2)}) collective-permute-start(bf16[256,2048]{1,0:T(8,128)(2,1)} %multiply_convert_fusion.h2), channel_id=1, source_target_pairs={{1,0},{2,1},{3,2},{5,4},{6,5},{7,6},{9,8},{10,9},{11,10},{13,12},{... | collective-permute-start | bytes 3145736 | tf_op jit(solution)/shard_map/ppermute | solution.py:327
  401.3 76.1 %collective-permute-start.64 = (bf16[256,2048]{1,0:T(8,128)(2,1)}, bf16[256,2048]{1,0:T(8,128)(2,1)S(1)}, u32[]{:S(2)}, u32[]{:S(2)}) collective-permute-start(bf16[256,2048]{1,0:T(8,128)(2,1)} %multiply_convert_fusion.h2), channel_id=1, source_target_pairs={{0,1},{1,2},{2,3},{4,5},{5,6},{6,7},{8,9},{9,10},{10,11},{12,13},{... | collective-permute-start | bytes 3145736 | tf_op jit(solution)/shard_map/ppermute | solution.py:330
  468.0 58.6 %collective-permute-start.76 = (bf16[256,2048]{1,0:T(8,128)(2,1)}, bf16[256,2048]{1,0:T(8,128)(2,1)S(1)}, u32[]{:S(2)}, u32[]{:S(2)}) collective-permute-start(bf16[256,2048]{1,0:T(8,128)(2,1)} %collective-permute-done.69), channel_id=1, source_target_pairs={{0,1},{1,2},{2,3},{4,5},{5,6},{6,7},{8,9},{9,10},{10,11},{12,13},{... | collective-permute-start | bytes 3145736 | tf_op jit(solution)/shard_map/ppermute | solution.py:330
  474.9 54.4 %collective-permute-start.80 = (bf16[256,2048]{1,0:T(8,128)(2,1)}, bf16[256,2048]{1,0:T(8,128)(2,1)S(1)}, u32[]{:S(2)}, u32[]{:S(2)}) collective-permute-start(bf16[256,2048]{1,0:T(8,128)(2,1)} %collective-permute-done.67), channel_id=1, source_target_pairs={{1,0},{2,1},{3,2},{5,4},{6,5},{7,6},{9,8},{10,9},{11,10},{13,12},{... | collective-permute-start | bytes 3145736 | tf_op jit(solution)/shard_map/ppermute | solution.py:327
  476.2 59.7 %collective-permute-start.63 = (bf16[256,2048]{1,0:T(8,128)(2,1)}, bf16[256,2048]{1,0:T(8,128)(2,1)S(1)}, u32[]{:S(2)}, u32[]{:S(2)}) collective-permute-start(bf16[256,2048]{1,0:T(8,128)(2,1)} %collective-permute-done.62), channel_id=1, source_target_pairs={{1,0},{2,1},{3,2},{5,4},{6,5},{7,6},{9,8},{10,9},{11,10},{13,12},{... | collective-permute-start | bytes 3145736 | tf_op jit(solution)/shard_map/ppermute | solution.py:327
  477.5 54.4 %collective-permute-start.65 = (bf16[256,2048]{1,0:T(8,128)(2,1)S(1)}, bf16[256,2048]{1,0:T(8,128)(2,1)S(1)}, u32[]{:S(2)}, u32[]{:S(2)}) collective-permute-start(bf16[256,2048]{1,0:T(8,128)(2,1)S(1)} %collective-permute-done.64), channel_id=1, source_target_pairs={{0,1},{1,2},{2,3},{4,5},{5,6},{6,7},{8,9},{9,10},{10,11},{12,13},{... | collective-permute-start | bytes 3145736 | tf_op jit(solution)/shard_map/ppermute | solution.py:330
  531.9 53.0 %collective-permute-start.75 = (bf16[256,2048]{1,0:T(8,128)(2,1)S(1)}, bf16[256,2048]{1,0:T(8,128)(2,1)S(1)}, u32[]{:S(2)}, u32[]{:S(2)}) collective-permute-start(bf16[256,2048]{1,0:T(8,128)(2,1)S(1)} %collective-permute-done.65), channel_id=1, source_target_pairs={{0,1},{1,2},{2,3},{4,5},{5,6},{6,7},{8,9},{9,10},{10,11},{12,13},{... | collective-permute-start | bytes 3145736 | tf_op jit(solution)/shard_map/ppermute | solution.py:330
  580.4 192.5 %collective-permute-start.83 = (bf16[256,2048]{1,0:T(8,128)(2,1)}, bf16[256,2048]{1,0:T(8,128)(2,1)S(1)}, u32[]{:S(2)}, u32[]{:S(2)}) collective-permute-start(bf16[256,2048]{1,0:T(8,128)(2,1)} %get-tuple-element.63), channel_id=1, source_target_pairs={{0,2},{1,3},{2,0},{3,1},{4,6},{5,7},{6,4},{7,5},{8,10},{9,11},{10,... | collective-permute-start | bytes 3145736 | tf_op jit(solution)/shard_map/ppermute | solution.py:335
  581.9 226.5 %collective-permute-start.74 = (bf16[256,2048]{1,0:T(8,128)(2,1)}, bf16[256,2048]{1,0:T(8,128)(2,1)}, u32[]{:S(2)}, u32[]{:S(2)}) collective-permute-start(bf16[256,2048]{1,0:T(8,128)(2,1)} %get-tuple-element.59), channel_id=1, source_target_pairs={{0,2},{1,3},{2,0},{3,1},{4,6},{5,7},{6,4},{7,5},{8,10},{9,11},{10,... | collective-permute-start | bytes 3145736 | tf_op jit(solution)/shard_map/ppermute | solution.py:335
  583.4 50.2 %collective-permute-start.79 = (bf16[256,2048]{1,0:T(8,128)(2,1)S(1)}, bf16[256,2048]{1,0:T(8,128)(2,1)S(1)}, u32[]{:S(2)}, u32[]{:S(2)}) collective-permute-start(bf16[256,2048]{1,0:T(8,128)(2,1)S(1)} %collective-permute-done.63), channel_id=1, source_target_pairs={{1,0},{2,1},{3,2},{5,4},{6,5},{7,6},{9,8},{10,9},{11,10},{13,12},{... | collective-permute-start | bytes 3145736 | tf_op jit(solution)/shard_map/ppermute | solution.py:327
  630.9 144.3 %collective-permute-start.84 = (bf16[256,2048]{1,0:T(8,128)(2,1)}, bf16[256,2048]{1,0:T(8,128)(2,1)}, u32[]{:S(2)}, u32[]{:S(2)}) collective-permute-start(bf16[256,2048]{1,0:T(8,128)(2,1)} %get-tuple-element.64), channel_id=1, source_target_pairs={{0,1},{1,2},{2,3},{3,0},{4,5},{5,6},{6,7},{7,4},{8,9},{9,10},{10,1... | collective-permute-start | bytes 3145736 | tf_op jit(solution)/shard_map/ppermute | solution.py:335
  678.4 127.4 %collective-permute-start.85 = (bf16[256,2048]{1,0:T(8,128)(2,1)}, bf16[256,2048]{1,0:T(8,128)(2,1)}, u32[]{:S(2)}, u32[]{:S(2)}) collective-permute-start(bf16[256,2048]{1,0:T(8,128)(2,1)} %get-tuple-element.65), channel_id=1, source_target_pairs={{0,3},{1,0},{2,1},{3,2},{4,7},{5,4},{6,5},{7,6},{8,11},{9,8},{10,9... | collective-permute-start | bytes 3145736 | tf_op jit(solution)/shard_map/ppermute | solution.py:335
  698.4 109.9 %collective-permute-start.78 = (bf16[256,2048]{1,0:T(8,128)(2,1)}, bf16[256,2048]{1,0:T(8,128)(2,1)}, u32[]{:S(2)}, u32[]{:S(2)}) collective-permute-start(bf16[256,2048]{1,0:T(8,128)(2,1)} %get-tuple-element.60), channel_id=1, source_target_pairs={{0,1},{1,2},{2,3},{3,0},{4,5},{5,6},{6,7},{7,4},{8,9},{9,10},{10,1... | collective-permute-start | bytes 3145736 | tf_op jit(solution)/shard_map/ppermute | solution.py:335
  773.0 54.4 %collective-permute-start.82 = (bf16[256,2048]{1,0:T(8,128)(2,1)}, bf16[256,2048]{1,0:T(8,128)(2,1)S(1)}, u32[]{:S(2)}, u32[]{:S(2)}) collective-permute-start(bf16[256,2048]{1,0:T(8,128)(2,1)} %get-tuple-element.61), channel_id=1, source_target_pairs={{0,3},{1,0},{2,1},{3,2},{4,7},{5,4},{6,5},{7,6},{8,11},{9,8},{10,9... | collective-permute-start | bytes 3145736 | tf_op jit(solution)/shard_map/ppermute | solution.py:335
  915.0 92.9 %all-reduce.3.cloned.1.call-start = ((), (), s32[]{:S(2)}) async-start(), calls=%async_computation.2 | async-start | bytes 5242880 | tf_op jit(solution)/shard_map/psum | solution.py:535
  (240 other events, 4405.2 us)
Sparse Core Ops, SparseCore 0:
  915.1 25.6 reduce-scatter.1
  944.4 63.3 all-reduce.2

commit v2 on v1

v2 whole, which is shorter than its diff:
```python
import functools

import jax
import jax.numpy as jnp
from jax import lax
from jax.experimental import pallas as pl
from jax.experimental.pallas import tpu as pltpu
from jax.sharding import PartitionSpec as P

HEADS = 16
HEAD = 128
TOP = 8
EXPERTS = 16
RANK = 16
SETS = 2
MOST = 160
PACK = SETS * RANK

epsilon = 1e-06
adapter_scale = 2.0
masked_score = -1e30
score_scale = HEAD ** (-0.5)

BF = jnp.bfloat16
F32 = jnp.float32
VMEM = 56 * 1024 * 1024


def dot_nn(a, b):
    return jnp.dot(a, b, preferred_element_type=F32)


def dot_nt(a, b):
    return lax.dot_general(a, b, (((1,), (1,)), ((), ())), preferred_element_type=F32)


def dot_tn(a, b):
    return lax.dot_general(a, b, (((0,), (0,)), ((), ())), preferred_element_type=F32)


def rms_forward(values, gain_vec):
    inverse = lax.rsqrt(jnp.mean(values * values, axis=-1, keepdims=True) + epsilon)
    return values * inverse * gain_vec


def rms_backward(values, gain_vec, grad_norm):
    inverse = lax.rsqrt(jnp.mean(values * values, axis=-1, keepdims=True) + epsilon)
    weighted = grad_norm * gain_vec
    cubed = inverse * inverse * inverse
    return inverse * weighted - values * cubed * jnp.mean(values * weighted, axis=-1, keepdims=True)


def scores(q, k, allowed):
    s = dot_nt(q, k) * score_scale
    s = jnp.where(allowed, s, masked_score)
    e = jnp.exp(s - jnp.max(s, axis=-1, keepdims=True))
    return e / jnp.sum(e, axis=-1, keepdims=True)


def allowed_mask(seg_row, seg_col, pad_row):
    shape = (seg_col.shape[0], seg_row.shape[1])
    rows = lax.broadcasted_iota(jnp.int32, shape, 0)
    cols = lax.broadcasted_iota(jnp.int32, shape, 1)
    return (seg_col == seg_row) & ((pad_row == 1) | (rows == cols))


def project_kernel(sizes, ids, h, flags, near1, near2, far1, far2, downs, lifts, *refs):
    team, n_line, rows, width = sizes
    outs, (r_own, w_s, r_s) = refs[:team], refs[team:]
    core = ids[2]
    half = width // 2
    span = n_line * HEAD
    here = pl.multiple_of(core * half, half)
    there = pl.multiple_of((1 - core) * half, half)
    for j in range(team):
        at = slice(j * rows, (j + 1) * rows)
        keep = flags[j, :1, : 3 * PACK].astype(F32)
        r_s[at, :] = (dot_nt(h[at, :], downs[: 3 * PACK, :]) * keep).astype(BF)
    for a in range(3):
        r_own[a] = r_s[:rows, a * PACK : (a + 1) * PACK]
    for a, (near, far, start) in enumerate(((near1, far1, 0), (near2, far2, 0), (near2, far2, half))):
        for z in range(n_line):
            at = slice(z * HEAD, (z + 1) * HEAD)
            w_s[a, pl.ds(here, half), at] = near[z, start : start + half, :]
            w_s[a, pl.ds(there, half), at] = far[z, start : start + half, :]
    tile = min(256, span)
    per = span // tile

    def step(i, carry):
        a = i // per
        at = pl.multiple_of((i % per) * tile, tile)
        y = dot_nn(h[...], w_s[a, :, pl.ds(at, tile)])
        y = y + adapter_scale * dot_nn(r_s[...], lifts[a, :, pl.ds(at, tile)])
        y = y.astype(BF)
        for j in range(team):
            outs[j][:, pl.ds(pl.multiple_of(i * tile, tile), tile)] = y[j * rows : (j + 1) * rows]
        return carry

    lax.fori_loop(0, 3 * per, step, 0)


def project(ids, h, flags, near, far, downs, lifts, sizes):
    team, n_line, rows, width = sizes
    span = n_line * HEAD
    full = pl.BlockSpec(memory_space=pltpu.VMEM)
    got = pl.pallas_call(
        functools.partial(project_kernel, sizes),
        in_specs=[pl.BlockSpec(memory_space=pltpu.SMEM)] + [full] * 8,
        out_specs=[full] * (team + 1),
        out_shape=[jax.ShapeDtypeStruct((rows, 3 * span), BF)] * team
        + [jax.ShapeDtypeStruct((3, rows, PACK), BF)],
        scratch_shapes=[
            pltpu.VMEM((3, width, span), BF),
            pltpu.VMEM((team * rows, 3 * PACK), BF),
        ],
        compiler_params=pltpu.CompilerParams(vmem_limit_bytes=VMEM),
        cost_estimate=pl.CostEstimate(
            flops=6 * team * rows * width * span, bytes_accessed=12 * width * span, transcendentals=0
        ),
    )(ids, h, flags, *near, *far, downs, lifts)
    return got[:team], got[team]


def chip_columns(ref, chip, n_line, cols):
    parts = []
    for z in range(n_line):
        parts.append(ref[:, pl.ds(pl.multiple_of(z * cols + chip * HEAD, HEAD), HEAD)])
    return jnp.concatenate(parts, axis=1)


def mix_kernel(sizes, ids, seg_row, seg_col, pad_row, tokens, gain, d_out, l_out, keep, *refs):
    team, n_line, rows, width, cols = sizes
    qkv, refs = refs[:team], refs[team:]
    near, refs = refs[:team], refs[team:]
    far, refs = refs[:team], refs[team:]
    mixed, r_out, x1, h2, acc = refs
    chip, core = ids[1], ids[2]
    span = n_line * HEAD
    side = span // 2
    allowed = allowed_mask(seg_row[...], seg_col[...], pad_row[...])
    reduced = jnp.zeros((rows, PACK), F32)
    for j in range(team):
        for z in range(n_line):
            q, k, v = (
                qkv[j][:, a * span + z * HEAD : a * span + (z + 1) * HEAD] for a in range(3)
            )
            p = scores(q, k, allowed)
            mixed[:, j * span + z * HEAD : j * span + (z + 1) * HEAD] = dot_nn(
                p.astype(BF), v
            ).astype(BF)
        o = mixed[:, j * span : (j + 1) * span]
        reduced = reduced + dot_nt(o, chip_columns(d_out, chip ^ j, n_line, cols))
        mine = mixed[:, pl.ds(pl.multiple_of(j * span + core * side, HEAD), side)]
        other = mixed[:, pl.ds(pl.multiple_of(j * span + (1 - core) * side, HEAD), side)]
        part = dot_nn(mine, near[j][...]) + dot_nn(other, far[j][...])
        if j == 0:
            acc[...] = part
        else:
            acc[...] += part
    low = (reduced * keep[...]).astype(BF)
    r_out[...] = low
    total = tokens[...].astype(F32) + (acc[...] + adapter_scale * dot_nn(low, l_out[...]))
    x1[...] = total
    h2[...] = rms_forward(total, gain[...]).astype(BF)


def mix(ids, masks, tokens, gain, d_out, l_out, keep, qkv, near, far, sizes):
    team, n_line, rows, width, cols = sizes
    full = pl.BlockSpec(memory_space=pltpu.VMEM)
    return pl.pallas_call(
        functools.partial(mix_kernel, sizes),
        in_specs=[pl.BlockSpec(memory_space=pltpu.SMEM)] + [full] * (8 + 3 * team),
        out_specs=[full] * 4,
        out_shape=[
            jax.ShapeDtypeStruct((rows, width), BF),
            jax.ShapeDtypeStruct((rows, PACK), BF),
            jax.ShapeDtypeStruct((rows, width), F32),
            jax.ShapeDtypeStruct((rows, width), BF),
        ],
        scratch_shapes=[pltpu.VMEM((rows, width), F32)],
        compiler_params=pltpu.CompilerParams(vmem_limit_bytes=VMEM),
        cost_estimate=pl.CostEstimate(
            flops=2 * rows * width * width + 4 * rows * rows * width,
            bytes_accessed=2 * width * width + 12 * rows * width,
            transcendentals=rows * rows * HEADS,
        ),
    )(ids, *masks, tokens, gain, d_out, l_out, keep, *qkv, *near, *far)


def back_kernel(sizes, ids, *refs):
    team, n_line, rows, width, cols = sizes
    (seg_row, seg_col, pad_row, tokens, cot, x1, gain1, gain2, own, downs, l_out, keep) = refs[:12]
    refs = refs[12:]
    parts, refs = refs[: n_line - 1], refs[n_line - 1 :]
    mixed, r_own, r_out = refs[:3]
    refs = refs[3:]
    qkv, refs = refs[:team], refs[team:]
    near_o, refs = refs[:team], refs[team:]
    far_o, refs = refs[:team], refs[team:]
    weights, in_grad, grads, near_s, far_s, sems, dx1_s, da_s, do_s, do_b, dp_s, acc, h1_s, dr, lift_s = refs
    chip, core = ids[1], ids[2]
    span = n_line * HEAD
    side = span // 2
    half = width // 2
    lift_gap = 3 * PACK // 2
    lift_end = half + lift_gap
    slots = near_s.shape[0]

    def fetch(j):
        copies = []
        for side_at, buf in ((core, near_s), (1 - core, far_s)):
            source = ids[3] + (chip ^ j) * 2 + side_at
            number = 0 if buf is near_s else 1
            for z in range(n_line):
                copies.append(
                    pltpu.make_async_copy(
                        weights.at[source, z],
                        buf.at[j % slots, :, z * HEAD : (z + 1) * HEAD],
                        sems.at[j % slots, number, z],
                    )
                )
        return copies

    for copy in fetch(0):
        copy.start()
    mask = keep[...]
    dh2 = own[...]
    for part in parts:
        dh2 = dh2 + part[...].astype(F32)
    dx1 = cot[...].astype(F32) + rms_backward(x1[...], gain2[...], dh2)
    dx1_s[...] = dx1
    da_s[...] = dx1.astype(BF)
    h1_s[...] = rms_forward(tokens[...].astype(F32), gain1[...]).astype(BF)
    da = da_s[...]
    d_low = (adapter_scale * dot_nt(da, l_out[...]) * mask).astype(BF)

    def put_all(row, block):
        for z in range(n_line):
            grads[z, row : row + PACK, :] = block[:, z * cols : (z + 1) * cols].astype(BF)

    put_all(7 * PACK, adapter_scale * dot_tn(r_out[...], da))
    allowed = allowed_mask(seg_row[...], seg_col[...], pad_row[...])
    dr[...] = jnp.zeros_like(dr)
    here = pl.multiple_of(core * half, half)
    there = pl.multiple_of((1 - core) * half, half)
    acc[...] = jnp.zeros_like(acc)
    for j in range(team):
        ahead = j + slots - 1
        if 0 < ahead < team:
            for copy in fetch(ahead):
                copy.start()
        spot = chip ^ j

        def put(row, block):
            for z in range(n_line):
                at = pl.multiple_of(spot * HEAD, HEAD)
                grads[z, pl.ds(row, PACK), pl.ds(at, HEAD)] = block[
                    :, z * HEAD : (z + 1) * HEAD
                ].astype(BF)

        do_s[:, pl.ds(pl.multiple_of(core * side, HEAD), side)] = dot_nt(da, near_o[j][...])
        do_s[:, pl.ds(pl.multiple_of((1 - core) * side, HEAD), side)] = dot_nt(da, far_o[j][...])
        do = do_s[...] + dot_nn(
            d_low, chip_columns(downs.at[3 * PACK :, :], spot, n_line, cols)
        )
        do = do.astype(BF)
        put(3 * PACK, dot_tn(d_low, mixed[:, j * span : (j + 1) * span]))
        do_b[...] = do

        def head(z, carry):
            at = pl.multiple_of(z * HEAD, HEAD)
            q, k, v = (
                qkv[j][:, pl.ds(pl.multiple_of(a * span + at, HEAD), HEAD)] for a in range(3)
            )
            p = scores(q, k, allowed)
            do_h = do_b[:, pl.ds(at, HEAD)]
            dp = dot_nt(do_h, v)
            delta = jnp.sum(dp * p, axis=-1, keepdims=True)
            ds = (p * (dp - delta)).astype(BF)
            heads = (
                dot_nn(ds, k) * score_scale,
                dot_tn(ds, q) * score_scale,
                dot_tn(p.astype(BF), do_h),
            )
            for a in range(3):
                dp_s[:, pl.ds(pl.multiple_of(a * span + at, HEAD), HEAD)] = heads[a].astype(BF)
            return carry

        lax.fori_loop(0, n_line, head, 0, unroll=2)
        for copy in fetch(j):
            copy.wait()
        slot = j % slots
        packs = jnp.where(
            core == 0,
            jnp.concatenate([near_s[slot, half:lift_end, :], far_s[slot, half:lift_end, :]]),
            jnp.concatenate([far_s[slot, half:lift_end, :], near_s[slot, half:lift_end, :]]),
        )
        for a in range(3):
            lift_s[a] = packs[a * PACK : (a + 1) * PACK]

        def grad(a, carry):
            g = dp_s[:, pl.ds(pl.multiple_of(a * span, HEAD), span)]
            lift = lift_s[a]
            dr[a] += dot_nt(g, lift)
            put(
                pl.multiple_of((4 + a) * PACK, PACK), adapter_scale * dot_tn(r_own[a], g)
            )
            rows_a = pl.ds(pl.multiple_of(a * half + lift_gap * jnp.minimum(a, 1), 16), half)
            acc[:, pl.ds(here, half)] += dot_nt(g, near_s[slot, rows_a, :])
            acc[:, pl.ds(there, half)] += dot_nt(g, far_s[slot, rows_a, :])
            return carry

        lax.fori_loop(0, 3, grad, 0)
    h1 = h1_s[...]
    for a in range(3):
        low = (adapter_scale * dr[a] * mask).astype(BF)
        put_all(a * PACK, dot_tn(low, h1))
        acc[...] += dot_nn(low, downs[a * PACK : (a + 1) * PACK, :])
    total = dx1_s[...] + rms_backward(tokens[...].astype(F32), gain1[...], acc[...])
    in_grad[...] = total.astype(BF)


def attention_back(ids, small, parts, kept, qkv, near_o, far_o, weights, sizes):
    team, n_line, rows, width, cols = sizes
    span = n_line * HEAD
    full = pl.BlockSpec(memory_space=pltpu.VMEM)
    count = len(small) + len(parts) + len(kept) + 3 * team
    slots = 2 if span <= 512 else 1
    return pl.pallas_call(
        functools.partial(back_kernel, sizes),
        in_specs=[pl.BlockSpec(memory_space=pltpu.SMEM)]
        + [full] * count
        + [pl.BlockSpec(memory_space=pl.ANY)],
        out_specs=[full] * 2,
        out_shape=[
            jax.ShapeDtypeStruct((rows, width), BF),
            jax.ShapeDtypeStruct((n_line, 8 * PACK, cols), BF),
        ],
        scratch_shapes=[
            pltpu.VMEM((slots, weights.shape[2], span), BF),
            pltpu.VMEM((slots, weights.shape[2], span), BF),
            pltpu.SemaphoreType.DMA((slots, 2, n_line)),
            pltpu.VMEM((rows, width), F32),
            pltpu.VMEM((rows, width), BF),
            pltpu.VMEM((rows, span), F32),
            pltpu.VMEM((rows, span), BF),
            pltpu.VMEM((rows, 3 * span), BF),
            pltpu.VMEM((rows, width), F32),
            pltpu.VMEM((rows, width), BF),
            pltpu.VMEM((3, rows, PACK), F32),
            pltpu.VMEM((3, PACK, span), BF),
        ],
        compiler_params=pltpu.CompilerParams(vmem_limit_bytes=VMEM),
        cost_estimate=pl.CostEstimate(
            flops=8 * rows * width * width + 10 * rows * rows * width,
            bytes_accessed=8 * width * width + 20 * rows * width,
            transcendentals=rows * rows * HEADS,
        ),
    )(ids, *small, *parts, *kept, *qkv, *near_o, *far_o, weights)


def expert_kernel(
    n_exp,
    n_ff,
    has_sum,
    source,
    h2,
    cot,
    place,
    weight,
    mask,
    w_gate,
    w_up,
    w_low,
    d_gu,
    l_gate,
    l_up,
    d_low,
    l_low,
    *refs,
):
    prior = (None,) * 5
    if has_sum:
        prior, refs = refs[:5], refs[5:]

    def emit(number, ref, value):
        if has_sum:
            value = value + prior[number][0].astype(F32)
        ref[0] = value.astype(ref.dtype)

    (out, dh2, g_gu, g_lg, g_lu, g_dl, g_ll) = refs[:7]
    (x_s, dy_s, rgu_s, drl_s, sw_s, y_acc, dx_acc, rl_acc, drgu_acc, sel, y_all, dx_all) = refs[7:]
    e = pl.program_id(0)
    f = pl.program_id(1)
    keep = mask[...]
    keep_one = keep[:, :PACK]
    base = pl.multiple_of(e * MOST, MOST)

    @pl.when(f == 0)
    def _():
        slots = lax.broadcasted_iota(jnp.int32, (MOST, place.shape[2]), 0)
        hit = slots == place[0]
        pick = jnp.where(hit, 1.0, 0.0).astype(BF)
        sel[pl.ds(base, MOST), :] = pick
        sw = jnp.sum(jnp.where(hit, weight[0], 0.0), axis=1, keepdims=True)
        sw_s[...] = sw
        x = dot_nn(pick, h2[...]).astype(BF)
        dy = (dot_nn(pick, cot[0]) * sw).astype(BF)
        x_s[...] = x
        dy_s[...] = dy
        rgu_s[...] = (dot_nt(x, d_gu[0]) * keep).astype(BF)
        drl_s[...] = (adapter_scale * dot_nt(dy, l_low[0]) * keep_one).astype(BF)
        y_acc[...] = jnp.zeros_like(y_acc)
        dx_acc[...] = jnp.zeros_like(dx_acc)
        rl_acc[...] = jnp.zeros_like(rl_acc)
        drgu_acc[...] = jnp.zeros_like(drgu_acc)

    x = x_s[...]
    dy = dy_s[...]
    r_g = rgu_s[:, :PACK]
    r_u = rgu_s[:, PACK:]
    gate = dot_nn(x, w_gate[0]) + adapter_scale * dot_nn(r_g, l_gate[0])
    up = dot_nn(x, w_up[0]) + adapter_scale * dot_nn(r_u, l_up[0])
    sig = 1.0 / (1.0 + jnp.exp(-gate))
    act = gate * sig
    hidden = (act * up).astype(BF)
    rl_acc[...] += dot_nt(hidden, d_low[0])
    y_acc[...] += dot_nn(hidden, w_low[0])
    d_hidden = dot_nt(dy, w_low[0]) + dot_nn(drl_s[...], d_low[0])
    d_gate = (d_hidden * up * sig * (1.0 + gate * (1.0 - sig))).astype(BF)
    d_up = (d_hidden * act).astype(BF)
    drgu_acc[:, :PACK] += dot_nt(d_gate, l_gate[0])
    drgu_acc[:, PACK:] += dot_nt(d_up, l_up[0])
    dx_acc[...] += dot_nt(d_gate, w_gate[0]) + dot_nt(d_up, w_up[0])
    emit(1, g_lg, adapter_scale * dot_tn(r_g, d_gate))
    emit(2, g_lu, adapter_scale * dot_tn(r_u, d_up))
    emit(3, g_dl, dot_tn(drl_s[...], hidden))

    @pl.when(f == n_ff - 1)
    def _():
        x = x_s[...]
        dy = dy_s[...]
        r_low = (rl_acc[...] * keep_one).astype(BF)
        y = y_acc[...] + adapter_scale * dot_nn(r_low, l_low[0])
        y_all[pl.ds(base, MOST), :] = (y * sw_s[...]).astype(BF)
        dr = (adapter_scale * drgu_acc[...] * keep).astype(BF)
        dx_all[pl.ds(base, MOST), :] = (dx_acc[...] + dot_nn(dr, d_gu[0])).astype(BF)
        emit(4, g_ll, adapter_scale * dot_tn(r_low, dy))
        emit(0, g_gu, dot_tn(dr, x))

    @pl.when((f == n_ff - 1) & (e == n_exp - 1))
    def _():
        out[...] = dot_tn(sel[...], y_all[...]).astype(out.dtype)
        dh2[...] = dot_tn(sel[...], dx_all[...]).astype(dh2.dtype)


def expert_chunk(source, h2, cot, place, weight, mask, params, prior, out_type, ff_block=512):
    w_gate, w_up, w_low, d_gu, l_gate, l_up, d_low, l_low = params
    n_exp, width, ff = w_gate.shape
    rows = h2.shape[0]
    n_ff = ff // ff_block
    whole = lambda e, f, s: (0, 0)
    per_e = lambda e, f, s: (e, 0, 0)
    cols = lambda e, f, s: (e, 0, f)
    grads = [
        (2 * PACK, width, per_e, width),
        (PACK, ff, cols, ff_block),
        (PACK, ff, cols, ff_block),
        (PACK, ff, cols, ff_block),
        (PACK, width, per_e, width),
    ]
    grad_specs = [pl.BlockSpec((1, g[0], g[3]), g[2]) for g in grads]
    grad_type = F32
    return pl.pallas_call(
        functools.partial(expert_kernel, n_exp, n_ff, prior is not None),
        grid_spec=pltpu.PrefetchScalarGridSpec(
            num_scalar_prefetch=1,
            grid=(n_exp, n_ff),
            in_specs=[
                pl.BlockSpec((rows, width), whole),
                pl.BlockSpec((1, rows, width), lambda e, f, s: (s[0], 0, 0)),
                pl.BlockSpec((1, 1, rows), per_e),
                pl.BlockSpec((1, 1, rows), per_e),
                pl.BlockSpec((1, 2 * PACK), whole),
                pl.BlockSpec((1, width, ff_block), cols),
                pl.BlockSpec((1, width, ff_block), cols),
                pl.BlockSpec((1, ff_block, width), lambda e, f, s: (e, f, 0)),
                pl.BlockSpec((1, 2 * PACK, width), per_e),
                pl.BlockSpec((1, PACK, ff_block), cols),
                pl.BlockSpec((1, PACK, ff_block), cols),
                pl.BlockSpec((1, PACK, ff_block), cols),
                pl.BlockSpec((1, PACK, width), per_e),
            ]
            + (grad_specs if prior is not None else []),
            out_specs=[
                pl.BlockSpec((rows, width), whole),
                pl.BlockSpec((rows, width), whole),
            ]
            + grad_specs,
            scratch_shapes=[
                pltpu.VMEM((MOST, width), BF),
                pltpu.VMEM((MOST, width), BF),
                pltpu.VMEM((MOST, 2 * PACK), BF),
                pltpu.VMEM((MOST, PACK), BF),
                pltpu.VMEM((MOST, 1), F32),
                pltpu.VMEM((MOST, width), F32),
                pltpu.VMEM((MOST, width), F32),
                pltpu.VMEM((MOST, PACK), F32),
                pltpu.VMEM((MOST, 2 * PACK), F32),
                pltpu.VMEM((n_exp * MOST, rows), BF),
                pltpu.VMEM((n_exp * MOST, width), BF),
                pltpu.VMEM((n_exp * MOST, width), BF),
            ],
        ),
        out_shape=[
            jax.ShapeDtypeStruct((rows, width), out_type),
            jax.ShapeDtypeStruct((rows, width), out_type),
        ]
        + [jax.ShapeDtypeStruct((n_exp, g[0], g[1]), grad_type) for g in grads],
        compiler_params=pltpu.CompilerParams(
            vmem_limit_bytes=VMEM, dimension_semantics=("arbitrary", "arbitrary")
        ),
        cost_estimate=pl.CostEstimate(
            flops=20 * n_exp * MOST * width * ff,
            bytes_accessed=6 * n_exp * width * ff,
            transcendentals=n_exp * MOST * ff,
        ),
    )(
        source,
        h2,
        cot,
        place,
        weight,
        mask,
        w_gate,
        w_up,
        w_low,
        d_gu,
        l_gate,
        l_up,
        d_low,
        l_low,
        *(prior or ()),
    )


def local(
    n_rep,
    n_shard,
    tokens,
    cotangent,
    segments,
    padding,
    routes,
    route_weights,
    adapter_set,
    norm_one,
    norm_two,
    query_weight,
    key_weight,
    value_weight,
    output_weight,
    query_down,
    key_down,
    value_down,
    output_down,
    query_lift,
    key_lift,
    value_lift,
    output_lift,
    expert_gate,
    expert_upper,
    expert_lower,
    gate_down,
    gate_lift,
    upper_down,
    upper_lift,
    lower_down,
    lower_lift,
):
    seq_len, width = tokens.shape
    n_exp, _, ff = expert_gate.shape
    cols = query_weight.shape[1]
    team = min(cols // HEAD, n_rep // 2)
    tiles = cols // HEAD
    half = width // 2
    plane = lax.axis_index("shard")
    rep = lax.axis_index("rep")
    core = rep % 2
    chip = (rep // 2) % team
    ids = jnp.stack([plane, chip, core, rep - rep % (2 * team)]).astype(jnp.int32)

    def rep_swap(x, bits):
        return lax.ppermute(x, "rep", [(a, a ^ bits) for a in range(n_rep)])

    def line_steps(x):
        from_up, from_down = [x], [x]
        for _ in range(1, n_shard):
            from_up.append(
                lax.ppermute(from_up[-1], "shard", [(a, a - 1) for a in range(1, n_shard)])
            )
            from_down.append(
                lax.ppermute(from_down[-1], "shard", [(a, a + 1) for a in range(n_shard - 1)])
            )
        return from_up, from_down

    def line_gather(x):
        up, down = line_steps(x)
        return [x] + [up[k] + down[n_shard - k] for k in range(1, n_shard)]

    def line_send(x, k):
        return lax.ppermute(x, "shard", [(a, (a + k) % n_shard) for a in range(n_shard)])

    def in_order(parts):
        buf = jnp.zeros((n_shard,) + parts[0].shape, parts[0].dtype)
        for k, part in enumerate(parts):
            buf = lax.dynamic_update_index_in_dim(buf, part, (plane + k) % n_shard, 0)
        return buf

    def chip_gather(x):
        return [x] + [rep_swap(x, j << 1) for j in range(1, team)]

    def after(x, *others):
        return lax.optimization_barrier((x,) + others)[0]

    chosen_set = adapter_set[0]
    set_flags = (jnp.arange(SETS, dtype=jnp.int32) == chosen_set).astype(F32)
    keep = jnp.repeat(set_flags, RANK)[None]
    masks = (segments, segments.reshape(seq_len, 1), padding)
    gain_one, gain_two = norm_one[None], norm_two[None]
    normed_one = rms_forward(tokens.astype(F32), gain_one).astype(BF)
    flag_rows = jnp.pad(jnp.tile(keep, (16, 3)), ((0, 0), (0, width - 3 * PACK))).astype(BF)
    sent_h = chip_gather(jnp.concatenate([normed_one, flag_rows], axis=0))
    flags = jnp.stack([h[seq_len:, :HEAD] for h in sent_h])
    hs = jnp.concatenate([h[:seq_len] for h in sent_h])

    def flat(table):
        return table.reshape(table.shape[0], PACK).T

    def pieces(x):
        return x.reshape(x.shape[0], tiles, HEAD).transpose(1, 0, 2).reshape(-1, HEAD)

    def whole_rows(x, height):
        x = x.reshape(n_shard, tiles, height, HEAD)
        return x.transpose(2, 0, 1, 3).reshape(height, width)

    def both(a, b, axis=0):
        return jnp.where(
            core == 0, jnp.concatenate([a, b], axis=axis), jnp.concatenate([b, a], axis=axis)
        )

    def slice_of(weight):
        return lax.dynamic_slice(weight, (core * half, chip * HEAD), (half, HEAD))

    def core_rows(table, height):
        return lax.dynamic_slice(table, (core * height, 0), (height, table.shape[1]))

    lift_rows = 3 * PACK // 2
    down_rows = 4 * PACK // 2
    last_rows = PACK // 2
    lift_pack = jnp.concatenate([flat(t) for t in (query_lift, key_lift, value_lift)], axis=0)
    down_pack = jnp.concatenate(
        [flat(t) for t in (query_down, key_down, value_down, output_down)], axis=0
    )
    out_rows = output_weight.reshape(2, n_shard // 2, tiles, HEAD, cols)
    out_own = lax.dynamic_slice(
        out_rows, (core, 0, chip, 0, 0), (1, n_shard // 2, 1, HEAD, cols)
    ).reshape(n_shard // 2 * HEAD, cols)
    first = [
        slice_of(query_weight),
        lax.dynamic_slice(lift_pack, (core * lift_rows, chip * HEAD), (lift_rows, HEAD)),
        pieces(core_rows(down_pack, down_rows)),
        pieces(core_rows(flat(output_lift), last_rows)),
        pieces(out_own),
    ]
    marks = [0]
    for piece in first:
        marks.append(marks[-1] + piece.shape[0])
    line1 = line_gather(jnp.concatenate(first, axis=0))
    near1 = in_order(line1)
    second = jnp.concatenate([slice_of(key_weight), slice_of(value_weight)], axis=0)
    line2 = line_gather(after(second, *line1, *sent_h))
    near2 = in_order(line2)
    far1 = rep_swap(near1[:, : marks[4]], 1)
    far2 = rep_swap(near2, 1)
    lifts = both(
        *(
            g[:, marks[1] : marks[2]].transpose(1, 0, 2).reshape(lift_rows, -1)
            for g in (near1, far1)
        )
    )
    lifts = jnp.stack(
        [
            jnp.pad(lifts[a * PACK : (a + 1) * PACK], ((a * PACK, (2 - a) * PACK), (0, 0)))
            for a in range(3)
        ]
    )
    downs = both(*(whole_rows(g[:, marks[2] : marks[3]], down_rows) for g in (near1, far1)))
    lift_out = both(*(whole_rows(g[:, marks[3] : marks[4]], last_rows) for g in (near1, far1)))
    out_block = whole_rows(near1[:, marks[4] :], n_shard // 2 * HEAD)
    near_o = chip_gather(out_block)
    far_o = [rep_swap(b, 1) for b in near_o]

    sizes = (team, n_shard, seq_len, width)
    made, r_own = project(ids, after(hs, *near_o), flags, (near1, near2), (far1, far2), downs, lifts, sizes)
    qkv = [made[0]] + [rep_swap(made[j], j << 1) for j in range(1, team)]
    sizes = sizes + (cols,)
    mixed, r_out, after_attn, normed_two = mix(
        ids, masks, tokens, gain_two, downs[3 * PACK :], lift_out, keep, qkv, near_o, far_o, sizes
    )

    expert_ids = jnp.arange(EXPERTS, dtype=jnp.int32)
    picked = routes[:, :, None] == expert_ids[None, None, :]
    member = jnp.sum(picked.astype(jnp.int32), axis=1)
    before = jnp.cumsum(member, axis=0) - member
    place = jnp.where(member == 1, before, -1).T.astype(F32)
    per_expert = jnp.sum(jnp.where(picked, route_weights[:, :, None], 0.0), axis=1).T
    high = lax.reduce_precision(per_expert, 8, 7)
    mid = lax.reduce_precision(per_expert - high, 8, 7)
    low = per_expert - high - mid
    flag = jnp.broadcast_to(chosen_set.astype(F32), (EXPERTS, seq_len))
    info = jnp.concatenate([place, high, mid, low, flag], axis=0).astype(BF)
    info_rows = 16
    info = info.reshape(-1, width)
    info = jnp.pad(info, ((0, info_rows - info.shape[0]), (0, 0)))
    cot_info = after(jnp.concatenate([cotangent, info], axis=0), *line2, *near_o)
    cot_line = lax.all_gather(cot_info, "shard")
    sent_w = jnp.concatenate([near1[:, : marks[2]], near2], axis=1)
    all_w = lax.all_gather(after(sent_w, normed_two), "rep")
    order = sorted(range(n_shard), key=lambda k: (k != 0, abs(2 * k - n_shard), k))
    rows_line = {0: normed_two}
    for k in order[1:]:
        rows_line[k] = line_send(normed_two, n_shard - k)
    params = (
        expert_gate,
        expert_upper,
        expert_lower,
        jnp.concatenate(
            [t.reshape(n_exp, width, PACK).transpose(0, 2, 1) for t in (gate_down, upper_down)],
            axis=1,
        ),
        gate_lift.reshape(n_exp, -1, PACK).transpose(0, 2, 1),
        upper_lift.reshape(n_exp, -1, PACK).transpose(0, 2, 1),
        lower_down.reshape(n_exp, -1, PACK).transpose(0, 2, 1),
        lower_lift.reshape(n_exp, width, PACK).transpose(0, 2, 1),
    )

    def read(facts):
        mine = lax.dynamic_slice_in_dim(facts.astype(F32), plane * n_exp, n_exp, 2)
        flags = (jnp.arange(SETS, dtype=F32) == mine[:, 4, 0, :1]).astype(F32)
        mask = jnp.tile(jnp.repeat(flags, RANK, axis=1), (1, 2))
        return mine[:, 0].astype(jnp.int32), mine[:, 1] + mine[:, 2] + mine[:, 3], mask

    fact_rows = 5 * EXPERTS * seq_len // width
    own_facts = read(info[:fact_rows].reshape(1, 5, EXPERTS, seq_len))
    line_facts = read(
        cot_line[:, seq_len : seq_len + fact_rows].reshape(n_shard, 5, EXPERTS, seq_len)
    )

    def chunk(k, prior):
        if k == 0:
            spot, share_of, mask = (f[0] for f in own_facts)
            cot, source = cotangent[None], jnp.zeros((1,), jnp.int32)
        else:
            source = (plane + k) % n_shard
            spot, share_of, mask = (
                lax.dynamic_index_in_dim(f, source, 0, keepdims=False) for f in line_facts
            )
            cot, source = cot_line, source.reshape(1).astype(jnp.int32)
        return expert_chunk(
            source,
            rows_line[k],
            cot,
            spot[:, None, :],
            share_of[:, None, :],
            mask[None],
            params,
            prior,
            F32 if k == 0 else BF,
        )

    results, prior = {}, None
    for k in order:
        results[k] = chunk(k, prior)
        prior = results[k][2:]
    back_parts = [line_send(results[k][1], k) for k in order[1:]]
    out_parts = [line_send(results[k][0], k) for k in order[1:]]
    expert_sums = [g.astype(BF) for g in prior]
    expert_sums = lax.psum(tuple(expert_sums), "rep")

    input_grad, attn_flat = attention_back(
        ids,
        (*masks, tokens, cotangent, after_attn, gain_one, gain_two, results[0][1])
        + (downs, lift_out, keep),
        back_parts,
        (mixed, r_own, r_out),
        qkv,
        near_o,
        far_o,
        all_w,
        sizes,
    )
    attn_flat = after(attn_flat, *out_parts)
    output = after_attn + results[0][0]
    for part in out_parts:
        output = output + part.astype(F32)
    output = output.astype(BF)

    def block_of(k):
        return lax.dynamic_index_in_dim(attn_flat, (plane + k) % n_shard, 0, keepdims=False)

    total = block_of(0).astype(F32)
    for k in range(1, n_shard):
        total = total + line_send(block_of(k), k).astype(F32)
    bits = n_rep.bit_length() - 1
    stages = [[1], [2, 4, 6]] if bits > 2 else [[1 << b] for b in range(bits)]
    stages = stages + [[1 << b] for b in range(3, bits)]
    for stage in stages:
        rounded = total.astype(BF)
        total = rounded.astype(F32)
        for swap in stage:
            total = total + rep_swap(rounded, swap).astype(F32)
    attn_flat = total

    def unflat(g):
        return g.T.reshape(cols, SETS, RANK)

    attn_outs = [unflat(attn_flat[a * PACK : (a + 1) * PACK]) for a in range(8)]

    parts = [g.astype(F32) for g in expert_sums]

    def restore(g):
        return g.transpose(0, 2, 1).reshape(n_exp, -1, SETS, RANK)

    expert_outs = [
        restore(parts[0][:, :PACK]),
        restore(parts[1]),
        restore(parts[0][:, PACK:]),
        restore(parts[2]),
        restore(parts[3]),
        restore(parts[4]),
    ]
    return (output, input_grad, *attn_outs, *expert_outs)


def solution(mesh):
    rows = P(("rep", "shard"), None)
    second = P(None, "shard")
    three = P("shard", None, None)
    four = P("shard", None, None, None)
    placed = (rows,) * 6 + (P(("rep", "shard")), P(), P()) + (second,) * 4
    placed = placed + (three,) * 11 + (four,) * 6
    return jax.shard_map(
        functools.partial(local, mesh.shape["rep"], mesh.shape["shard"]),
        mesh=mesh,
        in_specs=placed,
        out_specs=(rows, rows) + (three,) * 8 + (four,) * 6,
        check_vma=False,
    )
```

time: 1040 us -> 666 us (0.64)
  starting transfers between devices: 256 us -> 68.7 us
  waiting for transfers between devices: 319 us -> 235 us
  matrix products: 82.2 us -> 0 us
  Pallas kernels: 188 us -> 244 us
  local copies, waits for them, and re-layouts: 86.6 us -> 45.6 us
  other arithmetic: 73.7 us -> 49.5 us
    ppermute x48 -> x12, starting transfers between devices: 144 us -> 37.6 us  [the longest x6 29.9 us: line_steps(): lax.ppermute(from_down[-1], 'shard', [(a, a + 1) for a in range(n_shard -...]
    ppermute x32 -> x19, waiting for transfers between devices: 157 us -> 60.7 us  [rep_swap(): return lax.ppermute(x, 'rep', [(a, a ^ bits) for a in range(n_rep)])]
    dot_general x124 -> x0, matrix products: 82.2 us -> none  [the longest x52 42 us: dot_nt(): lax.dot_general(a, b, (((1,), (1,)), ((), ())), preferred_element_type=F32)]
    ppermute x6 -> x12, waiting for transfers between devices: 49.7 us -> 126 us  [line_send(): lax.ppermute(x, 'shard', [(a, (a + k) % n_shard) for a in range(n_shard)])]
    ppermute x6 -> x12, starting transfers between devices: 87.4 us -> 14.8 us  [line_send(): lax.ppermute(x, 'shard', [(a, (a + k) % n_shard) for a in range(n_shard)])]
    psum x1, waiting for transfers between devices: 61.2 us -> 0.01 us  [local(): expert_sums = lax.psum(tuple(expert_sums), 'rep')]
    pallas_call x12 -> x7, Pallas kernels: 188 us -> 244 us  [the longest x4 176 us: expert_chunk(): pl.pallas_call(functools.partial(expert_kernel, n_exp, n_ff, prior is not...]
    unnamed x390 -> x88, local copies, waits for them, and re-layouts: 28.9 us -> 4.91 us
  transfers between devices with their start and end apart: 88 -> 46, of which waited for: 22 -> 23; matrix products, arithmetic and copies ran while one was open for 13% -> 13% of each run, Pallas kernels for 17% -> 37%
where the time goes in v2:
time: 666 us; the launch traced here: 659 us
  Pallas kernels  244 us (37%)
  waiting for transfers between devices  235 us (35%)
  starting transfers between devices  68.7 us (10%)
  other arithmetic  49.5 us (7%)
  local copies, waits for them, and re-layouts  45.6 us (7%)
  between operations  15.7 us (2%)
    pallas_call x4, Pallas kernels, expert_chunk(): pl.pallas_call(functools.partial(expert_kernel, n_exp, n_ff, prior is not...  176 us
    ppermute x12, waiting for transfers between devices, line_send(): lax.ppermute(x, 'shard', [(a, (a + k) % n_shard) for a in range(n_shard)])  126 us
    ppermute x19, waiting for transfers between devices, rep_swap(): return lax.ppermute(x, 'rep', [(a, a ^ bits) for a in range(n_rep)])  60.7 us
    pallas_call x1, Pallas kernels, attention_back(): pl.pallas_call(functools.partial(back_kernel, sizes), in_specs=[pl.BlockS...  37.3 us
    ppermute x6, waiting for transfers between devices, line_steps(): lax.ppermute(from_down[-1], 'shard', [(a, a + 1) for a in range(n_shard -...  35.5 us
    ppermute x6, starting transfers between devices, line_steps(): lax.ppermute(from_down[-1], 'shard', [(a, a + 1) for a in range(n_shard -...  29.9 us
    pallas_call x1, Pallas kernels, project(): pl.pallas_call(functools.partial(project_kernel, sizes), in_specs=[pl.Blo...  16.9 us
    ppermute x19, starting transfers between devices, rep_swap(): return lax.ppermute(x, 'rep', [(a, a ^ bits) for a in range(n_rep)])  15.8 us
  transfers between devices with their start and end apart: 46, of which 23 were waited for; matrix products, arithmetic and copies ran while one was open for 13% of the time, Pallas kernels for 37%

profile of v2, /device:TPU:0, one launch (start us, length us, event | category | flops | bytes accessed | tf_op | source)
XLA Modules:
  0.0 658.5 jit_solution(5447904617736304230)
XLA Ops:
  12.5 5.6 collective-permute-start.1
  25.8 5.4 collective-permute-done.1
  31.2 5.2 collective-permute-start.2
  39.5 8.5 %collective-permute-done.2 = bf16[2416,128]{1,0:T(8,128)(2,1)} collective-permute-done((bf16[2416,128]{1,0:T(8,128)(2,1)S(1)}, bf16[2416,128]{1,0:T(8,128)(2,1)}, u32[]{:S(2)}, u32[]{:S(2)}) %collective-permute-start.2) | collective-permute-done | bytes 618528 | tf_op jit(solution)/shard_map/ppermute | solution.py:603
  48.0 4.5 collective-permute-start.3
  56.2 8.1 %collective-permute-done.3 = bf16[2416,128]{1,0:T(8,128)(2,1)S(1)} collective-permute-done((bf16[2416,128]{1,0:T(8,128)(2,1)}, bf16[2416,128]{1,0:T(8,128)(2,1)S(1)}, u32[]{:S(2)}, u32[]{:S(2)}) %collective-permute-start.3) | collective-permute-done | bytes 618528 | tf_op jit(solution)/shard_map/ppermute | solution.py:603
  67.0 3.6 collective-permute-done.5
  73.6 4.2 collective-permute-start.14
  80.4 8.2 %collective-permute-done.14 = bf16[2048,128]{1,0:T(8,128)(2,1)} collective-permute-done((bf16[2048,128]{1,0:T(8,128)(2,1)}, bf16[2048,128]{1,0:T(8,128)(2,1)}, u32[]{:S(2)}, u32[]{:S(2)}) %collective-permute-start.14) | collective-permute-done | bytes 524320 | tf_op jit(solution)/shard_map/ppermute | solution.py:603
  88.6 5.2 collective-permute-start.15
  98.3 5.4 collective-permute-done.15
  103.7 5.2 collective-permute-start.16
  127.2 7.3 %collective-permute-done.18 = bf16[2048,128]{1,0:T(8,128)(2,1)S(1)} collective-permute-done((bf16[2048,128]{1,0:T(8,128)(2,1)}, bf16[2048,128]{1,0:T(8,128)(2,1)S(1)}, u32[]{:S(2)}, u32[]{:S(2)}) %collective-permute-start.18) | collective-permute-done | bytes 524320 | tf_op jit(solution)/shard_map/ppermute | solution.py:600
  136.5 4.4 collective-permute-done.10.refs_5_.refs_23_
  140.9 18.6 %collective-permute-done.11.refs_6_.refs_24_ = bf16[256,2048]{1,0:T(8,128)(2,1)} collective-permute-done((bf16[256,2048]{1,0:T(8,128)(2,1)S(1)}, bf16[256,2048]{1,0:T(8,128)(2,1)}, u32[]{:S(2)}, u32[]{:S(2)}) %collective-permute-start.11) | collective-permute-done | bytes 1048608 | tf_op jit(solution)/shard_map/ppermute | solution.py:594
  181.9 16.9 %shard_map.405 = (bf16[256,1536]{1,0:T(8,128)(2,1)}, bf16[256,1536]{1,0:T(8,128)(2,1)}, bf16[256,1536]{1,0:T(8,128)(2,1)}, bf16[256,1536]{1,0:T(8,128)(2,1)}, bf16[3,256,32]{2,1,0:T(8,128)(2,1)}) custom-call(s32[4]{0:T(128)} %pad_add_fusion.ids, bf16[1024,2048]{1,0:T(8,128)(2,1)} %pad_maximum_fusion.h, bf16[4,16,128]{2,1,0:T(8,128)(2,1)} %pad_maximum_fusion.6.flags, ...), custom_call_target="tpu_custom_call" | custom-call | flops 6442450944 | bytes 12582912 | tf_op jit(solution)/shard_map/pallas_call | solution.py:106
  212.6 6.9 %collective-permute-done.20.refs_1_.refs_19_ = bf16[256,1536]{1,0:T(8,128)(2,1)} collective-permute-done((bf16[256,1536]{1,0:T(8,128)(2,1)}, bf16[256,1536]{1,0:T(8,128)(2,1)}, u32[]{:S(2)}, u32[]{:S(2)}) %collective-permute-start.20) | collective-permute-done | bytes 786464 | tf_op jit(solution)/shard_map/ppermute | solution.py:594
  219.5 16.1 %collective-permute-done.21.refs_2_.refs_20_ = bf16[256,1536]{1,0:T(8,128)(2,1)S(1)} collective-permute-done((bf16[256,1536]{1,0:T(8,128)(2,1)}, bf16[256,1536]{1,0:T(8,128)(2,1)S(1)}, u32[]{:S(2)}, u32[]{:S(2)}) %collective-permute-start.21) | collective-permute-done | bytes 786464 | tf_op jit(solution)/shard_map/ppermute | solution.py:594
  236.4 13.3 %shard_map.406 = (bf16[256,2048]{1,0:T(8,128)(2,1)}, bf16[256,32]{1,0:T(8,128)(2,1)}, f32[256,2048]{1,0:T(8,128)}, bf16[256,2048]{1,0:T(8,128)(2,1)}) custom-call(s32[4]{0:T(128)} %pad_add_fusion.ids, s32[1,256]{1,0:T(1,128)} %refs_0_.1, s32[256,1]{1,0:T(8,128)} %copy.146.seg_col.refs_1_, s32[1,256]{1,0:T(1,128)} %refs_2_.1, bf16[256,2048]{1,0:T(8,128)(2,1)} %refs_3_.1, ...), custom_call_target="tpu_custom_call" | custom-call | flops 2684354560 | bytes 14680064 | tf_op jit(solution)/shard_map/pallas_call | solution.py:170
  258.8 46.5 %shard_map.407 = (f32[256,2048]{1,0:T(8,128)}, f32[256,2048]{1,0:T(8,128)}, f32[4,64,2048]{2,1,0:T(8,128)}, f32[4,32,1024]{2,1,0:T(8,128)}, f32[4,32,1024]{2,1,0...) custom-call(s32[1]{0:T(128)} %constant.193.clone.1.source, bf16[256,2048]{1,0:T(8,128)(2,1)} %get-tuple-element.67.h2, ...), custom_call_target="tpu_custom_call" | custom-call | flops 26843545600 | bytes 50331648 | tf_op jit(solution)/shard_map/pallas_call | solution.py:474
  308.7 38.6 %collective-permute-done.27.h2 = bf16[256,2048]{1,0:T(8,128)(2,1)} collective-permute-done((bf16[256,2048]{1,0:T(8,128)(2,1)S(1)}, bf16[256,2048]{1,0:T(8,128)(2,1)}, u32[]{:S(2)}, u32[]{:S(2)}) %collective-permute-start.27) | collective-permute-done | bytes 1048608 | tf_op jit(solution)/shard_map/ppermute | solution.py:612
  347.3 43.3 %shard_map.408 = (bf16[256,2048]{1,0:T(8,128)(2,1)}, bf16[256,2048]{1,0:T(8,128)(2,1)}, f32[4,64,2048]{2,1,0:T(8,128)}, f32[4,32,1024]{2,1,0:T(8,128)}, f32[4,32...) custom-call(s32[1]{0:T(128)} %bitcast.73.source, bf16[256,2048]{1,0:T(8,128)(2,1)} %collective-permute-done.27.h2, ...), custom_call_target="tpu_custom_call" | custom-call | flops 26843545600 | bytes 50331648 | tf_op jit(solution)/shard_map/pallas_call | solution.py:474
  394.1 43.3 %shard_map.409 = (bf16[256,2048]{1,0:T(8,128)(2,1)}, bf16[256,2048]{1,0:T(8,128)(2,1)}, f32[4,64,2048]{2,1,0:T(8,128)}, f32[4,32,1024]{2,1,0:T(8,128)}, f32[4,32...) custom-call(s32[1]{0:T(128)} %bitcast.81.source, bf16[256,2048]{1,0:T(8,128)(2,1)} %copy-done.40, ...), custom_call_target="tpu_custom_call" | custom-call | flops 26843545600 | bytes 50331648 | tf_op jit(solution)/shard_map/pallas_call | solution.py:474
  439.2 43.2 %shard_map.410 = (bf16[256,2048]{1,0:T(8,128)(2,1)}, bf16[256,2048]{1,0:T(8,128)(2,1)}, f32[4,64,2048]{2,1,0:T(8,128)}, f32[4,32,1024]{2,1,0:T(8,128)}, f32[4,32...) custom-call(s32[1]{0:T(128)} %bitcast.84.source, bf16[256,2048]{1,0:T(8,128)(2,1)} %collective-permute-done.31.h2, ...), custom_call_target="tpu_custom_call" | custom-call | flops 26843545600 | bytes 50331648 | tf_op jit(solution)/shard_map/pallas_call | solution.py:474
  493.6 15.1 %collective-permute-done.35.refs_14_ = bf16[256,2048]{1,0:T(8,128)(2,1)S(1)} collective-permute-done((bf16[256,2048]{1,0:T(8,128)(2,1)}, bf16[256,2048]{1,0:T(8,128)(2,1)S(1)}, u32[]{:S(2)}, u32[]{:S(2)}) %collective-permute-start.35) | collective-permute-done | bytes 1048608 | tf_op jit(solution)/shard_map/ppermute | solution.py:612
  509.7 37.3 %shard_map.411 = (bf16[256,2048]{1,0:T(8,128)(2,1)}, bf16[4,256,512]{2,1,0:T(8,128)(2,1)}) custom-call(s32[4]{0:T(128)} %pad_add_fusion.ids, s32[1,256]{1,0:T(1,128)} %refs_0_.1, s32[256,1]{1,0:T(8,128)} %copy.146.seg_col.refs_1_, s32[1,256]{1,0:T(1,128)} %refs_2_.1, bf16[256,2048]{1,0:T(8,128)(2,1)} %refs_3_.1, bf16[256,2048]{1,0:T(8,128)(2,1)} %refs_4_.1, ...), custom_call_target="tpu_custom_call" | custom-call | flops 9932111872 | bytes 44040192 | tf_op jit(solution)/shard_map/pallas_call | solution.py:329
  547.0 7.5 %collective-permute-done.30 = bf16[256,2048]{1,0:T(8,128)(2,1)} collective-permute-done((bf16[256,2048]{1,0:T(8,128)(2,1)}, bf16[256,2048]{1,0:T(8,128)(2,1)}, u32[]{:S(2)}, u32[]{:S(2)}) %collective-permute-start.30) | collective-permute-done | bytes 1048608 | tf_op jit(solution)/shard_map/ppermute | solution.py:612
  554.5 43.7 %collective-permute-done.28 = bf16[256,2048]{1,0:T(8,128)(2,1)} collective-permute-done((bf16[256,2048]{1,0:T(8,128)(2,1)}, bf16[256,2048]{1,0:T(8,128)(2,1)}, u32[]{:S(2)}, u32[]{:S(2)}) %collective-permute-start.28) | collective-permute-done | bytes 1048608 | tf_op jit(solution)/shard_map/ppermute | solution.py:612
  603.0 6.1 collective-permute-done.38
  609.2 14.9 %collective-permute-done.37 = bf16[256,512]{1,0:T(8,128)(2,1)S(1)} collective-permute-done((bf16[256,512]{1,0:T(8,128)(2,1)S(1)}, bf16[256,512]{1,0:T(8,128)(2,1)S(1)}, u32[]{:S(2)}, u32[]{:S(2)}) %collective-permute-start.37) | collective-permute-done | bytes 262176 | tf_op jit(solution)/shard_map/ppermute | solution.py:612
  640.7 5.0 collective-permute-done.42
  645.7 5.2 collective-permute-done.41
  (300 shorter events, 140.6 us)
Async XLA Ops:
  7.2 298.1 %all-gather.5.cloned.1.call-start = ((), (), s32[]{:S(2)}) async-start(), calls=%async_computation | async-start | bytes 5570560 | tf_op jit(solution)/shard_map/all_gather | solution.py:727
  11.2 27.0 %collective-permute-start = (bf16[2416,128]{1,0:T(8,128)(2,1)S(1)}, bf16[2416,128]{1,0:T(8,128)(2,1)}, u32[]{:S(2)}, u32[]{:S(2)}) collective-permute-start(bf16[2416,128]{1,0:T(8,128)(2,1)S(1)} %constant_dynamic-update-slice_fusion), channel_id=1, source_target_pairs={{1,0},{2,1},{3,2},{5,4},{6,5},{7,6},{9,8},{10,9},{11,10},{13,12},{... | collective-permute-start | bytes 1855496 | tf_op jit(solution)/shard_map/ppermute | solution.py:600
  12.5 18.7 %collective-permute-start.1 = (bf16[2416,128]{1,0:T(8,128)(2,1)S(1)}, bf16[2416,128]{1,0:T(8,128)(2,1)S(1)}, u32[]{:S(2)}, u32[]{:S(2)}) collective-permute-start(bf16[2416,128]{1,0:T(8,128)(2,1)S(1)} %constant_dynamic-update-slice_fusion), channel_id=1, source_target_pairs={{0,1},{1,2},{2,3},{4,5},{5,6},{6,7},{8,9},{9,10},{10,11},{12,13},{... | collective-permute-start | bytes 1855496 | tf_op jit(solution)/shard_map/ppermute | solution.py:603
  22.2 48.6 %collective-permute-start.9 = (bf16[272,2048]{1,0:T(8,128)(2,1)}, bf16[272,2048]{1,0:T(8,128)(2,1)}, u32[]{:S(2)}, u32[]{:S(2)}) collective-permute-start(bf16[272,2048]{1,0:T(8,128)(2,1)} %pad_maximum_fusion.2), channel_id=1, source_target_pairs={{0,24},{4,28},{8,16},{12,20},{16,8},{20,12},{24,0},{28,4},{1,25},{... | collective-permute-start | bytes 3342344 | tf_op jit(solution)/shard_map/ppermute | solution.py:594
  25.1 48.2 %collective-permute-start.8 = (bf16[272,2048]{1,0:T(8,128)(2,1)}, bf16[272,2048]{1,0:T(8,128)(2,1)}, u32[]{:S(2)}, u32[]{:S(2)}) collective-permute-start(bf16[272,2048]{1,0:T(8,128)(2,1)} %pad_maximum_fusion.2), channel_id=1, source_target_pairs={{0,16},{4,20},{8,24},{12,28},{16,0},{20,4},{24,8},{28,12},{1,17},{... | collective-permute-start | bytes 3342344 | tf_op jit(solution)/shard_map/ppermute | solution.py:594
  25.6 48.0 %collective-permute-start.7 = (bf16[272,2048]{1,0:T(8,128)(2,1)}, bf16[272,2048]{1,0:T(8,128)(2,1)}, u32[]{:S(2)}, u32[]{:S(2)}) collective-permute-start(bf16[272,2048]{1,0:T(8,128)(2,1)} %pad_maximum_fusion.2), channel_id=1, source_target_pairs={{0,8},{4,12},{8,0},{12,4},{16,24},{20,28},{24,16},{28,20},{1,9},{5... | collective-permute-start | bytes 3342344 | tf_op jit(solution)/shard_map/ppermute | solution.py:594
  79.1 17.9 %collective-permute-start.13 = (bf16[2048,128]{1,0:T(8,128)(2,1)}, bf16[2048,128]{1,0:T(8,128)(2,1)}, u32[]{:S(2)}, u32[]{:S(2)}) collective-permute-start(bf16[2048,128]{1,0:T(8,128)(2,1)} %pad_maximum_fusion.4), channel_id=1, source_target_pairs={{1,0},{2,1},{3,2},{5,4},{6,5},{7,6},{9,8},{10,9},{11,10},{13,12},{... | collective-permute-start | bytes 1572872 | tf_op jit(solution)/shard_map/ppermute | solution.py:600
  97.0 24.6 %collective-permute-start.17 = (bf16[2048,128]{1,0:T(8,128)(2,1)}, bf16[2048,128]{1,0:T(8,128)(2,1)}, u32[]{:S(2)}, u32[]{:S(2)}) collective-permute-start(bf16[2048,128]{1,0:T(8,128)(2,1)} %collective-permute-done.13), channel_id=1, source_target_pairs={{1,0},{2,1},{3,2},{5,4},{6,5},{7,6},{9,8},{10,9},{11,10},{13,12},{... | collective-permute-start | bytes 1572872 | tf_op jit(solution)/shard_map/ppermute | solution.py:600
  103.7 19.2 %collective-permute-start.16 = (bf16[2048,128]{1,0:T(8,128)(2,1)}, bf16[2048,128]{1,0:T(8,128)(2,1)}, u32[]{:S(2)}, u32[]{:S(2)}) collective-permute-start(bf16[2048,128]{1,0:T(8,128)(2,1)} %collective-permute-done.15), channel_id=1, source_target_pairs={{0,1},{1,2},{2,3},{4,5},{5,6},{6,7},{8,9},{9,10},{10,11},{12,13},{... | collective-permute-start | bytes 1572872 | tf_op jit(solution)/shard_map/ppermute | solution.py:603
  114.6 26.3 %collective-permute-start.10 = (bf16[256,2048]{1,0:T(8,128)(2,1)S(1)}, bf16[256,2048]{1,0:T(8,128)(2,1)}, u32[]{:S(2)}, u32[]{:S(2)}) collective-permute-start(bf16[256,2048]{1,0:T(8,128)(2,1)S(1)} %reshape.422.refs_4_.refs_22_), channel_id=1, source_target_pairs={{0,8},{4,12},{8,0},{12,4},{16,24},{20,28},{24,16},{28,20},{1,9},{5... | collective-permute-start | bytes 3145736 | tf_op jit(solution)/shard_map/ppermute | solution.py:594
  116.2 43.3 %collective-permute-start.11 = (bf16[256,2048]{1,0:T(8,128)(2,1)S(1)}, bf16[256,2048]{1,0:T(8,128)(2,1)}, u32[]{:S(2)}, u32[]{:S(2)}) collective-permute-start(bf16[256,2048]{1,0:T(8,128)(2,1)S(1)} %reshape.422.refs_4_.refs_22_), channel_id=1, source_target_pairs={{0,16},{4,20},{8,24},{12,28},{16,0},{20,4},{24,8},{28,12},{1,17},{... | collective-permute-start | bytes 3145736 | tf_op jit(solution)/shard_map/ppermute | solution.py:594
  116.4 45.0 %collective-permute-start.12 = (bf16[256,2048]{1,0:T(8,128)(2,1)S(1)}, bf16[256,2048]{1,0:T(8,128)(2,1)}, u32[]{:S(2)}, u32[]{:S(2)}) collective-permute-start(bf16[256,2048]{1,0:T(8,128)(2,1)S(1)} %reshape.422.refs_4_.refs_22_), channel_id=1, source_target_pairs={{0,24},{4,28},{8,16},{12,20},{16,8},{20,12},{24,0},{28,4},{1,25},{... | collective-permute-start | bytes 3145736 | tf_op jit(solution)/shard_map/ppermute | solution.py:594
  161.4 347.3 %all-gather.7.cloned.1.call-start = ((), (), s32[]{:S(2)}) async-start(), calls=%async_computation.1 | async-start | bytes 28753920 | tf_op jit(solution)/shard_map/all_gather | solution.py:729
  173.1 26.1 %collective-permute-start.23 = (bf16[256,2048]{1,0:T(8,128)(2,1)S(1)}, bf16[256,2048]{1,0:T(8,128)(2,1)}, u32[]{:S(2)}, u32[]{:S(2)}) collective-permute-start(bf16[256,2048]{1,0:T(8,128)(2,1)S(1)} %reshape.422.refs_4_.refs_22_), channel_id=1, source_target_pairs={{0,4},{4,0},{8,12},{12,8},{16,20},{20,16},{24,28},{28,24},{1,5},{5... | collective-permute-start | bytes 3145736 | tf_op jit(solution)/shard_map/ppermute | solution.py:594
  176.7 24.3 %collective-permute-start.24 = (bf16[256,2048]{1,0:T(8,128)(2,1)}, bf16[256,2048]{1,0:T(8,128)(2,1)S(1)}, u32[]{:S(2)}, u32[]{:S(2)}) collective-permute-start(bf16[256,2048]{1,0:T(8,128)(2,1)} %collective-permute-done.10.refs_5_.refs_23_), channel_id=1, source_target_pairs={{0,4},{4,0},{8,12},{12,8},{16,20},{20,16},{24,28},{28,24},{1,5},{5... | collective-permute-start | bytes 3145736 | tf_op jit(solution)/shard_map/ppermute | solution.py:594
  177.2 35.4 %collective-permute-start.25 = (bf16[256,2048]{1,0:T(8,128)(2,1)}, bf16[256,2048]{1,0:T(8,128)(2,1)}, u32[]{:S(2)}, u32[]{:S(2)}) collective-permute-start(bf16[256,2048]{1,0:T(8,128)(2,1)} %collective-permute-done.11.refs_6_.refs_24_), channel_id=1, source_target_pairs={{0,4},{4,0},{8,12},{12,8},{16,20},{20,16},{24,28},{28,24},{1,5},{5... | collective-permute-start | bytes 3145736 | tf_op jit(solution)/shard_map/ppermute | solution.py:594
  177.3 35.3 %collective-permute-start.26 = (bf16[256,2048]{1,0:T(8,128)(2,1)}, bf16[256,2048]{1,0:T(8,128)(2,1)}, u32[]{:S(2)}, u32[]{:S(2)}) collective-permute-start(bf16[256,2048]{1,0:T(8,128)(2,1)} %collective-permute-done.12.refs_7_.refs_25_), channel_id=1, source_target_pairs={{0,4},{4,0},{8,12},{12,8},{16,20},{20,16},{24,28},{28,24},{1,5},{5... | collective-permute-start | bytes 3145736 | tf_op jit(solution)/shard_map/ppermute | solution.py:594
  198.8 20.7 %collective-permute-start.20 = (bf16[256,1536]{1,0:T(8,128)(2,1)}, bf16[256,1536]{1,0:T(8,128)(2,1)}, u32[]{:S(2)}, u32[]{:S(2)}) collective-permute-start(bf16[256,1536]{1,0:T(8,128)(2,1)} %get-tuple-element.63), channel_id=1, source_target_pairs={{0,8},{4,12},{8,0},{12,4},{16,24},{20,28},{24,16},{28,20},{1,9},{5... | collective-permute-start | bytes 2359304 | tf_op jit(solution)/shard_map/ppermute | solution.py:594
  199.3 36.3 %collective-permute-start.21 = (bf16[256,1536]{1,0:T(8,128)(2,1)}, bf16[256,1536]{1,0:T(8,128)(2,1)S(1)}, u32[]{:S(2)}, u32[]{:S(2)}) collective-permute-start(bf16[256,1536]{1,0:T(8,128)(2,1)} %get-tuple-element.64), channel_id=1, source_target_pairs={{0,16},{4,20},{8,24},{12,28},{16,0},{20,4},{24,8},{28,12},{1,17},{... | collective-permute-start | bytes 2359304 | tf_op jit(solution)/shard_map/ppermute | solution.py:594
  201.0 34.6 %collective-permute-start.22 = (bf16[256,1536]{1,0:T(8,128)(2,1)}, bf16[256,1536]{1,0:T(8,128)(2,1)}, u32[]{:S(2)}, u32[]{:S(2)}) collective-permute-start(bf16[256,1536]{1,0:T(8,128)(2,1)} %get-tuple-element.65), channel_id=1, source_target_pairs={{0,24},{4,28},{8,16},{12,20},{16,8},{20,12},{24,0},{28,4},{1,25},{... | collective-permute-start | bytes 2359304 | tf_op jit(solution)/shard_map/ppermute | solution.py:594
  249.7 379.2 %all-reduce.7.cloned.1.call-start = ((), (), s32[]{:S(2)}) async-start(), calls=%async_computation.2 | async-start | bytes 4718592 | tf_op jit(solution)/shard_map/psum | solution.py:789
  254.8 184.4 %collective-permute-start.31 = (bf16[256,2048]{1,0:T(8,128)(2,1)S(1)}, bf16[256,2048]{1,0:T(8,128)(2,1)}, u32[]{:S(2)}, u32[]{:S(2)}) collective-permute-start(bf16[256,2048]{1,0:T(8,128)(2,1)S(1)} %copy-done.39), channel_id=1, source_target_pairs={{0,1},{1,2},{2,3},{3,0},{4,5},{5,6},{6,7},{7,4},{8,9},{9,10},{10,1... | collective-permute-start | bytes 3145736 | tf_op jit(solution)/shard_map/ppermute | solution.py:612
  256.4 136.7 %collective-permute-start.29 = (bf16[256,2048]{1,0:T(8,128)(2,1)S(1)}, bf16[256,2048]{1,0:T(8,128)(2,1)S(1)}, u32[]{:S(2)}, u32[]{:S(2)}) collective-permute-start(bf16[256,2048]{1,0:T(8,128)(2,1)S(1)} %copy-done.39), channel_id=1, source_target_pairs={{0,3},{1,0},{2,1},{3,2},{4,7},{5,4},{6,5},{7,6},{8,11},{9,8},{10,9... | collective-permute-start | bytes 3145736 | tf_op jit(solution)/shard_map/ppermute | solution.py:612
  258.6 88.8 %collective-permute-start.27 = (bf16[256,2048]{1,0:T(8,128)(2,1)S(1)}, bf16[256,2048]{1,0:T(8,128)(2,1)}, u32[]{:S(2)}, u32[]{:S(2)}) collective-permute-start(bf16[256,2048]{1,0:T(8,128)(2,1)S(1)} %copy-done.39), channel_id=1, source_target_pairs={{0,2},{1,3},{2,0},{3,1},{4,6},{5,7},{6,4},{7,5},{8,10},{9,11},{10,... | collective-permute-start | bytes 3145736 | tf_op jit(solution)/shard_map/ppermute | solution.py:612
  393.1 93.4 %collective-permute-start.33 = (bf16[256,2048]{1,0:T(8,128)(2,1)}, bf16[256,2048]{1,0:T(8,128)(2,1)S(1)}, u32[]{:S(2)}, u32[]{:S(2)}) collective-permute-start(bf16[256,2048]{1,0:T(8,128)(2,1)} %get-tuple-element.89), channel_id=1, source_target_pairs={{0,2},{1,3},{2,0},{3,1},{4,6},{5,7},{6,4},{7,5},{8,10},{9,11},{10,... | collective-permute-start | bytes 3145736 | tf_op jit(solution)/shard_map/ppermute | solution.py:612
  437.4 56.2 %collective-permute-start.34 = (bf16[256,2048]{1,0:T(8,128)(2,1)}, bf16[256,2048]{1,0:T(8,128)(2,1)S(1)}, u32[]{:S(2)}, u32[]{:S(2)}) collective-permute-start(bf16[256,2048]{1,0:T(8,128)(2,1)} %get-tuple-element.90), channel_id=1, source_target_pairs={{0,1},{1,2},{2,3},{3,0},{4,5},{5,6},{6,7},{7,4},{8,9},{9,10},{10,1... | collective-permute-start | bytes 3145736 | tf_op jit(solution)/shard_map/ppermute | solution.py:612
  482.4 26.4 %collective-permute-start.35 = (bf16[256,2048]{1,0:T(8,128)(2,1)}, bf16[256,2048]{1,0:T(8,128)(2,1)S(1)}, u32[]{:S(2)}, u32[]{:S(2)}) collective-permute-start(bf16[256,2048]{1,0:T(8,128)(2,1)} %get-tuple-element.91), channel_id=1, source_target_pairs={{0,3},{1,0},{2,1},{3,2},{4,7},{5,4},{6,5},{7,6},{8,11},{9,8},{10,9... | collective-permute-start | bytes 3145736 | tf_op jit(solution)/shard_map/ppermute | solution.py:612
  484.5 62.5 %collective-permute-start.32 = (bf16[256,2048]{1,0:T(8,128)(2,1)}, bf16[256,2048]{1,0:T(8,128)(2,1)}, u32[]{:S(2)}, u32[]{:S(2)}) collective-permute-start(bf16[256,2048]{1,0:T(8,128)(2,1)} %get-tuple-element.87), channel_id=1, source_target_pairs={{0,3},{1,0},{2,1},{3,2},{4,7},{5,4},{6,5},{7,6},{8,11},{9,8},{10,9... | collective-permute-start | bytes 3145736 | tf_op jit(solution)/shard_map/ppermute | solution.py:612
  485.1 69.4 %collective-permute-start.30 = (bf16[256,2048]{1,0:T(8,128)(2,1)}, bf16[256,2048]{1,0:T(8,128)(2,1)}, u32[]{:S(2)}, u32[]{:S(2)}) collective-permute-start(bf16[256,2048]{1,0:T(8,128)(2,1)} %get-tuple-element.81), channel_id=1, source_target_pairs={{0,1},{1,2},{2,3},{3,0},{4,5},{5,6},{6,7},{7,4},{8,9},{9,10},{10,1... | collective-permute-start | bytes 3145736 | tf_op jit(solution)/shard_map/ppermute | solution.py:612
  486.5 111.7 %collective-permute-start.28 = (bf16[256,2048]{1,0:T(8,128)(2,1)}, bf16[256,2048]{1,0:T(8,128)(2,1)}, u32[]{:S(2)}, u32[]{:S(2)}) collective-permute-start(bf16[256,2048]{1,0:T(8,128)(2,1)} %get-tuple-element.75), channel_id=1, source_target_pairs={{0,2},{1,3},{2,0},{3,1},{4,6},{5,7},{6,4},{7,5},{8,10},{9,11},{10,... | collective-permute-start | bytes 3145736 | tf_op jit(solution)/shard_map/ppermute | solution.py:612
  602.4 21.7 %collective-permute-start.37 = (bf16[256,512]{1,0:T(8,128)(2,1)S(1)}, bf16[256,512]{1,0:T(8,128)(2,1)S(1)}, u32[]{:S(2)}, u32[]{:S(2)}) collective-permute-start(bf16[256,512]{1,0:T(8,128)(2,1)S(1)} %get-tuple-element.129), channel_id=1, source_target_pairs={{0,2},{1,3},{2,0},{3,1},{4,6},{5,7},{6,4},{7,5},{8,10},{9,11},{10,... | collective-permute-start | bytes 786440 | tf_op jit(solution)/shard_map/ppermute | solution.py:612
  602.4 21.7 %collective-permute-start.36 = (bf16[256,512]{1,0:T(8,128)(2,1)S(1)}, bf16[256,512]{1,0:T(8,128)(2,1)S(1)}, u32[]{:S(2)}, u32[]{:S(2)}) collective-permute-start(bf16[256,512]{1,0:T(8,128)(2,1)S(1)} %get-tuple-element.127), channel_id=1, source_target_pairs={{0,1},{1,2},{2,3},{3,0},{4,5},{5,6},{6,7},{7,4},{8,9},{9,10},{10,1... | collective-permute-start | bytes 786440 | tf_op jit(solution)/shard_map/ppermute | solution.py:612
  (59 other events, 989.3 us)
Sparse Core Ops, SparseCore 0:
  161.5 83.9 all-gather.4
  249.9 125.8 all-gather.6
  493.7 62.7 all-reduce.6

commit v3 on v2

v3 whole, which is shorter than its diff:
```python
import functools

import jax
import jax.numpy as jnp
from jax import lax
from jax.experimental import pallas as pl
from jax.experimental.pallas import tpu as pltpu
from jax.sharding import PartitionSpec as P

HEADS = 16
HEAD = 128
TOP = 8
EXPERTS = 16
RANK = 16
SETS = 2
MOST = 160
PACK = SETS * RANK

epsilon = 1e-06
adapter_scale = 2.0
masked_score = -1e30
score_scale = HEAD ** (-0.5)

BF = jnp.bfloat16
F32 = jnp.float32
VMEM = 56 * 1024 * 1024


def dot_nn(a, b):
    return jnp.dot(a, b, preferred_element_type=F32)


def dot_nt(a, b):
    return lax.dot_general(a, b, (((1,), (1,)), ((), ())), preferred_element_type=F32)


def dot_tn(a, b):
    return lax.dot_general(a, b, (((0,), (0,)), ((), ())), preferred_element_type=F32)


def rms_forward(values, gain_vec):
    inverse = lax.rsqrt(jnp.mean(values * values, axis=-1, keepdims=True) + epsilon)
    return values * inverse * gain_vec


def rms_backward(values, gain_vec, grad_norm):
    inverse = lax.rsqrt(jnp.mean(values * values, axis=-1, keepdims=True) + epsilon)
    weighted = grad_norm * gain_vec
    cubed = inverse * inverse * inverse
    return inverse * weighted - values * cubed * jnp.mean(values * weighted, axis=-1, keepdims=True)


def scores(q, k, allowed):
    s = dot_nt(q, k) * score_scale
    s = jnp.where(allowed, s, masked_score)
    e = jnp.exp(s - jnp.max(s, axis=-1, keepdims=True))
    return e / jnp.sum(e, axis=-1, keepdims=True)


def allowed_mask(seg_row, seg_col, pad_row):
    shape = (seg_col.shape[0], seg_row.shape[1])
    rows = lax.broadcasted_iota(jnp.int32, shape, 0)
    cols = lax.broadcasted_iota(jnp.int32, shape, 1)
    return (seg_col == seg_row) & ((pad_row == 1) | (rows == cols))


def project_kernel(sizes, ids, h, downs, *refs):
    team, n_line, rows, width = sizes
    near, far, refs = refs[0], refs[1], refs[2:]
    outs, (r_own, h_s, flag_s, w_s, r_s, lift_s, sems) = refs[:team], refs[team:]
    plane, chip, core = ids[0], ids[1], ids[2]
    half = width // 2
    lift_half = 3 * PACK // 2
    copies = []
    for j in range(team):
        source = ids[3] + (chip ^ j) * 2 + core
        copies.append(
            pltpu.make_async_copy(
                h.at[source, :rows], h_s.at[j * rows : (j + 1) * rows], sems.at[0, j]
            )
        )
        copies.append(
            pltpu.make_async_copy(h.at[source, rows:, :HEAD], flag_s.at[j], sems.at[1, j])
        )
    for copy in copies:
        copy.start()
    for k in range(n_line):
        at = pl.ds(pl.multiple_of((plane + k) % n_line * HEAD, HEAD), HEAD)
        for side, ref in ((core, near), (1 - core, far)):
            for a in range(3):
                start = a * half + (lift_half if a else 0)
                w_s[a, pl.ds(pl.multiple_of(side * half, half), half), at] = ref[
                    k, start : start + half, :
                ]
            lift_s[3, pl.ds(pl.multiple_of(side * lift_half, 16), lift_half), at] = ref[
                k, half : half + lift_half, :
            ]
    lifts = lift_s[3]
    band = lax.broadcasted_iota(jnp.int32, lifts.shape, 0) // PACK
    for a in range(3):
        lift_s[a] = jnp.where(band == a, lifts, jnp.zeros_like(lifts))
    for copy in copies:
        copy.wait()
    for j in range(team):
        at = slice(j * rows, (j + 1) * rows)
        keep = flag_s[j, :1, : 3 * PACK].astype(F32)
        r_s[at, :] = (dot_nt(h_s[at, :], downs[: 3 * PACK, :]) * keep).astype(BF)
    for a in range(3):
        r_own[a] = r_s[:rows, a * PACK : (a + 1) * PACK]
    span = n_line * HEAD
    tile = min(256, span)
    per = span // tile

    def step(i, carry):
        a = i // per
        at = pl.multiple_of((i % per) * tile, tile)
        y = dot_nn(h_s[...], w_s[a, :, pl.ds(at, tile)])
        y = y + adapter_scale * dot_nn(r_s[...], lift_s[a, :, pl.ds(at, tile)])
        y = y.astype(BF)
        for j in range(team):
            outs[j][:, pl.ds(pl.multiple_of(i * tile, tile), tile)] = y[j * rows : (j + 1) * rows]
        return carry

    lax.fori_loop(0, 3 * per, step, 0)


def project(ids, h, downs, near, far, sizes):
    team, n_line, rows, width = sizes
    span = n_line * HEAD
    full = pl.BlockSpec(memory_space=pltpu.VMEM)
    got = pl.pallas_call(
        functools.partial(project_kernel, sizes),
        in_specs=[pl.BlockSpec(memory_space=pltpu.SMEM), pl.BlockSpec(memory_space=pl.ANY)]
        + [full] * 3,
        out_specs=[full] * (team + 1),
        out_shape=[jax.ShapeDtypeStruct((rows, 3 * span), BF)] * team
        + [jax.ShapeDtypeStruct((3, rows, PACK), BF)],
        scratch_shapes=[
            pltpu.VMEM((team * rows, width), BF),
            pltpu.VMEM((team, 16, HEAD), BF),
            pltpu.VMEM((3, width, span), BF),
            pltpu.VMEM((team * rows, 3 * PACK), BF),
            pltpu.VMEM((4, 3 * PACK, span), BF),
            pltpu.SemaphoreType.DMA((2, team)),
        ],
        compiler_params=pltpu.CompilerParams(vmem_limit_bytes=VMEM),
        cost_estimate=pl.CostEstimate(
            flops=6 * team * rows * width * span, bytes_accessed=12 * width * span, transcendentals=0
        ),
    )(ids, h, downs, near, far)
    return got[:team], got[team]


def chip_columns(ref, chip, n_line, cols):
    parts = []
    for z in range(n_line):
        parts.append(ref[:, pl.ds(pl.multiple_of(z * cols + chip * HEAD, HEAD), HEAD)])
    return jnp.concatenate(parts, axis=1)


def mix_kernel(sizes, ids, seg_row, seg_col, pad_row, tokens, gain, d_out, l_out, keep, *refs):
    team, n_line, rows, width, cols = sizes
    qkv, refs = refs[:team], refs[team:]
    near, refs = refs[:team], refs[team:]
    far, refs = refs[:team], refs[team:]
    mixed, r_out, x1, h2, acc = refs
    chip, core = ids[1], ids[2]
    span = n_line * HEAD
    side = span // 2
    allowed = allowed_mask(seg_row[...], seg_col[...], pad_row[...])
    reduced = jnp.zeros((rows, PACK), F32)
    for j in range(team):
        for z in range(n_line):
            q, k, v = (
                qkv[j][:, a * span + z * HEAD : a * span + (z + 1) * HEAD] for a in range(3)
            )
            p = scores(q, k, allowed)
            mixed[:, j * span + z * HEAD : j * span + (z + 1) * HEAD] = dot_nn(
                p.astype(BF), v
            ).astype(BF)
        o = mixed[:, j * span : (j + 1) * span]
        reduced = reduced + dot_nt(o, chip_columns(d_out, chip ^ j, n_line, cols))
        mine = mixed[:, pl.ds(pl.multiple_of(j * span + core * side, HEAD), side)]
        other = mixed[:, pl.ds(pl.multiple_of(j * span + (1 - core) * side, HEAD), side)]
        part = dot_nn(mine, near[j][...]) + dot_nn(other, far[j][...])
        if j == 0:
            acc[...] = part
        else:
            acc[...] += part
    low = (reduced * keep[...]).astype(BF)
    r_out[...] = low
    total = tokens[...].astype(F32) + (acc[...] + adapter_scale * dot_nn(low, l_out[...]))
    x1[...] = total
    h2[...] = rms_forward(total, gain[...]).astype(BF)


def mix(ids, masks, tokens, gain, d_out, l_out, keep, qkv, near, far, sizes):
    team, n_line, rows, width, cols = sizes
    full = pl.BlockSpec(memory_space=pltpu.VMEM)
    return pl.pallas_call(
        functools.partial(mix_kernel, sizes),
        in_specs=[pl.BlockSpec(memory_space=pltpu.SMEM)] + [full] * (8 + 3 * team),
        out_specs=[full] * 4,
        out_shape=[
            jax.ShapeDtypeStruct((rows, width), BF),
            jax.ShapeDtypeStruct((rows, PACK), BF),
            jax.ShapeDtypeStruct((rows, width), F32),
            jax.ShapeDtypeStruct((rows, width), BF),
        ],
        scratch_shapes=[pltpu.VMEM((rows, width), F32)],
        compiler_params=pltpu.CompilerParams(vmem_limit_bytes=VMEM),
        cost_estimate=pl.CostEstimate(
            flops=2 * rows * width * width + 4 * rows * rows * width,
            bytes_accessed=2 * width * width + 12 * rows * width,
            transcendentals=rows * rows * HEADS,
        ),
    )(ids, *masks, tokens, gain, d_out, l_out, keep, *qkv, *near, *far)


def back_kernel(sizes, n_parts, ids, *refs):
    team, n_line, rows, width, cols = sizes
    (seg_row, seg_col, pad_row, tokens, cot, x1, gain1, gain2, own, downs, l_out, keep) = refs[:12]
    refs = refs[12:]
    parts, refs = refs[:n_parts], refs[n_parts:]
    mixed, r_own, r_out = refs[:3]
    refs = refs[3:]
    qkv, refs = refs[:team], refs[team:]
    near_o, refs = refs[:team], refs[team:]
    far_o, refs = refs[:team], refs[team:]
    weights, in_grad, grads, near_s, far_s, sems, dx1_s, da_s, do_s, do_b, dp_s, acc, h1_s, dr, lift_s = refs
    chip, core = ids[1], ids[2]
    span = n_line * HEAD
    side = span // 2
    half = width // 2
    lift_gap = 3 * PACK // 2
    lift_end = half + lift_gap
    slots = near_s.shape[0]

    def fetch(j):
        copies = []
        for side_at, buf in ((core, near_s), (1 - core, far_s)):
            source = ids[3] + (chip ^ j) * 2 + side_at
            number = 0 if buf is near_s else 1
            for z in range(n_line):
                at = pl.multiple_of((ids[0] + z) % n_line * HEAD, HEAD)
                copies.append(
                    pltpu.make_async_copy(
                        weights.at[source, z],
                        buf.at[j % slots, :, pl.ds(at, HEAD)],
                        sems.at[j % slots, number, z],
                    )
                )
        return copies

    for copy in fetch(0):
        copy.start()
    mask = keep[...]
    dh2 = own[...]
    for part in parts:
        dh2 = dh2 + part[...].astype(F32)
    dx1 = cot[...].astype(F32) + rms_backward(x1[...], gain2[...], dh2)
    dx1_s[...] = dx1
    da_s[...] = dx1.astype(BF)
    h1_s[...] = rms_forward(tokens[...].astype(F32), gain1[...]).astype(BF)
    da = da_s[...]
    d_low = (adapter_scale * dot_nt(da, l_out[...]) * mask).astype(BF)

    def put_all(row, block):
        for z in range(n_line):
            part = block[:, z * cols : (z + 1) * cols]
            grads[z, row : row + RANK, :] = (part[:RANK] + part[RANK:]).astype(BF)

    put_all(7 * RANK, adapter_scale * dot_tn(r_out[...], da))
    allowed = allowed_mask(seg_row[...], seg_col[...], pad_row[...])
    dr[...] = jnp.zeros_like(dr)
    here = pl.multiple_of(core * half, half)
    there = pl.multiple_of((1 - core) * half, half)
    acc[...] = jnp.zeros_like(acc)
    for j in range(team):
        ahead = j + slots - 1
        if 0 < ahead < team:
            for copy in fetch(ahead):
                copy.start()
        spot = chip ^ j

        def put(row, block):
            for z in range(n_line):
                at = pl.multiple_of(spot * HEAD, HEAD)
                part = block[:, z * HEAD : (z + 1) * HEAD]
                part = part[:RANK] + part[RANK:]
                grads[z, pl.ds(row, RANK), pl.ds(at, HEAD)] = part.astype(BF)

        do_s[:, pl.ds(pl.multiple_of(core * side, HEAD), side)] = dot_nt(da, near_o[j][...])
        do_s[:, pl.ds(pl.multiple_of((1 - core) * side, HEAD), side)] = dot_nt(da, far_o[j][...])
        do = do_s[...] + dot_nn(
            d_low, chip_columns(downs.at[3 * PACK :, :], spot, n_line, cols)
        )
        do = do.astype(BF)
        put(3 * RANK, dot_tn(d_low, mixed[:, j * span : (j + 1) * span]))
        do_b[...] = do

        def head(z, carry):
            at = pl.multiple_of(z * HEAD, HEAD)
            q, k, v = (
                qkv[j][:, pl.ds(pl.multiple_of(a * span + at, HEAD), HEAD)] for a in range(3)
            )
            p = scores(q, k, allowed)
            do_h = do_b[:, pl.ds(at, HEAD)]
            dp = dot_nt(do_h, v)
            delta = jnp.sum(dp * p, axis=-1, keepdims=True)
            ds = (p * (dp - delta)).astype(BF)
            heads = (
                dot_nn(ds, k) * score_scale,
                dot_tn(ds, q) * score_scale,
                dot_tn(p.astype(BF), do_h),
            )
            for a in range(3):
                dp_s[:, pl.ds(pl.multiple_of(a * span + at, HEAD), HEAD)] = heads[a].astype(BF)
            return carry

        lax.fori_loop(0, n_line, head, 0, unroll=2)
        for copy in fetch(j):
            copy.wait()
        slot = j % slots
        packs = jnp.where(
            core == 0,
            jnp.concatenate([near_s[slot, half:lift_end, :], far_s[slot, half:lift_end, :]]),
            jnp.concatenate([far_s[slot, half:lift_end, :], near_s[slot, half:lift_end, :]]),
        )
        for a in range(3):
            lift_s[a] = packs[a * PACK : (a + 1) * PACK]

        def grad(a, carry):
            g = dp_s[:, pl.ds(pl.multiple_of(a * span, HEAD), span)]
            lift = lift_s[a]
            dr[a] += dot_nt(g, lift)
            put(
                pl.multiple_of((4 + a) * RANK, RANK), adapter_scale * dot_tn(r_own[a], g)
            )
            rows_a = pl.ds(pl.multiple_of(a * half + lift_gap * jnp.minimum(a, 1), 16), half)
            acc[:, pl.ds(here, half)] += dot_nt(g, near_s[slot, rows_a, :])
            acc[:, pl.ds(there, half)] += dot_nt(g, far_s[slot, rows_a, :])
            return carry

        lax.fori_loop(0, 3, grad, 0)
    h1 = h1_s[...]
    for a in range(3):
        low = (adapter_scale * dr[a] * mask).astype(BF)
        put_all(a * RANK, dot_tn(low, h1))
        acc[...] += dot_nn(low, downs[a * PACK : (a + 1) * PACK, :])
    total = dx1_s[...] + rms_backward(tokens[...].astype(F32), gain1[...], acc[...])
    in_grad[...] = total.astype(BF)


def attention_back(ids, small, parts, kept, qkv, near_o, far_o, weights, sizes):
    team, n_line, rows, width, cols = sizes
    span = n_line * HEAD
    full = pl.BlockSpec(memory_space=pltpu.VMEM)
    count = len(small) + len(parts) + len(kept) + 3 * team
    slots = 2 if span <= 512 else 1
    return pl.pallas_call(
        functools.partial(back_kernel, sizes, len(parts)),
        in_specs=[pl.BlockSpec(memory_space=pltpu.SMEM)]
        + [full] * count
        + [pl.BlockSpec(memory_space=pl.ANY)],
        out_specs=[full] * 2,
        out_shape=[
            jax.ShapeDtypeStruct((rows, width), BF),
            jax.ShapeDtypeStruct((n_line, 8 * RANK, cols), BF),
        ],
        scratch_shapes=[
            pltpu.VMEM((slots, weights.shape[2], span), BF),
            pltpu.VMEM((slots, weights.shape[2], span), BF),
            pltpu.SemaphoreType.DMA((slots, 2, n_line)),
            pltpu.VMEM((rows, width), F32),
            pltpu.VMEM((rows, width), BF),
            pltpu.VMEM((rows, span), F32),
            pltpu.VMEM((rows, span), BF),
            pltpu.VMEM((rows, 3 * span), BF),
            pltpu.VMEM((rows, width), F32),
            pltpu.VMEM((rows, width), BF),
            pltpu.VMEM((3, rows, PACK), F32),
            pltpu.VMEM((3, PACK, span), BF),
        ],
        compiler_params=pltpu.CompilerParams(vmem_limit_bytes=VMEM),
        cost_estimate=pl.CostEstimate(
            flops=8 * rows * width * width + 10 * rows * rows * width,
            bytes_accessed=8 * width * width + 20 * rows * width,
            transcendentals=rows * rows * HEADS,
        ),
    )(ids, *small, *parts, *kept, *qkv, *near_o, *far_o, weights)


def expert_kernel(
    n_exp,
    has_sum,
    tile,
    source,
    h2,
    place,
    weight,
    mask,
    dy_in,
    dm_in,
    drl_in,
    w_gate,
    w_up,
    w_low,
    d_gu,
    l_gate,
    l_up,
    d_low,
    l_low,
    *refs,
):
    prior = None
    if has_sum:
        prior, refs = refs[0], refs[1:]
    (out, dh2, grads) = refs[:3]
    (x_s, hid_s, dg_s, du_s, sel, y_all, dx_all) = refs[3:]
    ff = w_gate.shape[2]

    def emit(row, value, column=0):
        at = (0, slice(row, row + value.shape[0]), slice(column, column + value.shape[1]))
        if has_sum:
            value = value + prior[at]
        grads[at] = value.astype(grads.dtype)

    e = pl.program_id(0)
    keep = mask[...]
    keep_one = keep[:, :PACK]
    base = pl.multiple_of(e * MOST, MOST)
    slots = lax.broadcasted_iota(jnp.int32, (MOST, place.shape[2]), 0)
    hit = slots == place[0]
    pick = jnp.where(hit, 1.0, 0.0).astype(BF)
    sel[pl.ds(base, MOST), :] = pick
    sw = jnp.sum(jnp.where(hit, weight[0], 0.0), axis=1, keepdims=True)
    x_s[...] = dot_nn(pick, h2[...]).astype(BF)
    x = x_s[...]
    dy = dy_in[0, 0]
    r_gu = (dot_nt(x, d_gu[0]) * keep).astype(BF)
    r_g, r_u = r_gu[:, :PACK], r_gu[:, PACK:]
    dr_low = drl_in[0, 0]
    for start in range(0, w_gate.shape[2], tile):
        at = slice(start, start + tile)
        gate = dot_nn(x, w_gate[0, :, at]) + adapter_scale * dot_nn(r_g, l_gate[0, :, at])
        up = dot_nn(x, w_up[0, :, at]) + adapter_scale * dot_nn(r_u, l_up[0, :, at])
        d_hidden = dm_in[0, 0, :, at].astype(F32)
        sig = 1.0 / (1.0 + jnp.exp(-gate))
        act = gate * sig
        hid_s[:, at] = (act * up).astype(BF)
        dg_s[:, at] = (d_hidden * up * sig * (1.0 + gate * (1.0 - sig))).astype(BF)
        du_s[:, at] = (d_hidden * act).astype(BF)
    hidden, d_gate, d_up = hid_s[...], dg_s[...], du_s[...]
    r_low = (dot_nt(hidden, d_low[0]) * keep_one).astype(BF)
    y = dot_nn(hidden, w_low[0]) + adapter_scale * dot_nn(r_low, l_low[0])
    y_all[pl.ds(base, MOST), :] = (y * sw).astype(BF)
    dr = jnp.concatenate([dot_nt(d_gate, l_gate[0]), dot_nt(d_up, l_up[0])], axis=1)
    dr = (adapter_scale * dr * keep).astype(BF)
    dx = dot_nt(d_gate, w_gate[0]) + dot_nt(d_up, w_up[0]) + dot_nn(dr, d_gu[0])
    dx_all[pl.ds(base, MOST), :] = dx.astype(BF)
    emit(0, dot_tn(dr, x))
    emit(2 * PACK, adapter_scale * dot_tn(r_g, d_gate))
    emit(2 * PACK, adapter_scale * dot_tn(r_u, d_up), ff)
    emit(3 * PACK, adapter_scale * dot_tn(r_low, dy))
    g_low = dot_tn(dr_low, hidden)
    emit(4 * PACK, g_low[:RANK])
    emit(4 * PACK, g_low[RANK:], ff)

    @pl.when(e == n_exp - 1)
    def _():
        out[...] = dot_tn(sel[...], y_all[...]).astype(out.dtype)
        dh2[...] = dot_tn(sel[...], dx_all[...]).astype(dh2.dtype)


def grad_kernel(n_line, tile, cot, place, weight, mask, w_low, d_low, l_low, dy, dm, drl, dy_s):
    slots = lax.broadcasted_iota(jnp.int32, (MOST, place.shape[3]), 0)
    for k in range(n_line):
        hit = slots == place[k, 0]
        pick = jnp.where(hit, 1.0, 0.0).astype(BF)
        sw = jnp.sum(jnp.where(hit, weight[k, 0], 0.0), axis=1, keepdims=True)
        block = (dot_nn(pick, cot[k]) * sw).astype(BF)
        dy_s[k * MOST : (k + 1) * MOST, :] = block
        dy[k, 0] = block
    full = dy_s[...]
    dr = adapter_scale * dot_nt(full, l_low[0])
    dr = jnp.concatenate(
        [dr[k * MOST : (k + 1) * MOST] * mask[k, :, :PACK] for k in range(n_line)], axis=0
    ).astype(BF)
    for k in range(n_line):
        drl[k, 0] = dr[k * MOST : (k + 1) * MOST]
    for start in range(0, w_low.shape[1], tile):
        at = slice(start, start + tile)
        block = dot_nt(full, w_low[0, at, :]) + dot_nn(dr, d_low[0, :, at])
        block = block.astype(BF)
        for k in range(n_line):
            dm[k, 0, :, at] = block[k * MOST : (k + 1) * MOST]


def grad_rows(cot, place, weight, mask, w_low, d_low, l_low):
    n_line, rows, width = cot.shape
    n_exp, ff = w_low.shape[:2]
    per_e = lambda e: (e, 0, 0)
    all_e = lambda e: (0, e, 0, 0)
    return pl.pallas_call(
        functools.partial(grad_kernel, n_line, 256),
        grid=(n_exp,),
        in_specs=[
            pl.BlockSpec((n_line, rows, width), lambda e: (0, 0, 0)),
            pl.BlockSpec((n_line, 1, 1, rows), all_e),
            pl.BlockSpec((n_line, 1, 1, rows), all_e),
            pl.BlockSpec((n_line, 1, 2 * PACK), lambda e: (0, 0, 0)),
            pl.BlockSpec((1, ff, width), per_e),
            pl.BlockSpec((1, PACK, ff), per_e),
            pl.BlockSpec((1, PACK, width), per_e),
        ],
        out_specs=[
            pl.BlockSpec((n_line, 1, MOST, width), all_e),
            pl.BlockSpec((n_line, 1, MOST, ff), all_e),
            pl.BlockSpec((n_line, 1, MOST, PACK), all_e),
        ],
        out_shape=[
            jax.ShapeDtypeStruct((n_line, n_exp, MOST, width), BF),
            jax.ShapeDtypeStruct((n_line, n_exp, MOST, ff), BF),
            jax.ShapeDtypeStruct((n_line, n_exp, MOST, PACK), BF),
        ],
        scratch_shapes=[pltpu.VMEM((n_line * MOST, width), BF)],
        compiler_params=pltpu.CompilerParams(
            vmem_limit_bytes=VMEM, dimension_semantics=("arbitrary",)
        ),
        cost_estimate=pl.CostEstimate(
            flops=3 * n_line * n_exp * MOST * width * ff,
            bytes_accessed=2 * n_exp * width * ff,
            transcendentals=0,
        ),
    )(cot, place, weight, mask, w_low, d_low, l_low)


def expert_chunk(source, h2, ready, place, weight, mask, params, prior, out_type, grad_type=F32):
    w_gate, w_up, w_low, d_gu, l_gate, l_up, d_low, l_low = params
    n_exp, width, ff = w_gate.shape
    rows = h2.shape[0]
    whole = lambda e, s: (0, 0)
    per_e = lambda e, s: (e, 0, 0)
    grad_specs = [pl.BlockSpec((1, 4 * PACK + RANK, width), per_e)]
    return pl.pallas_call(
        functools.partial(expert_kernel, n_exp, prior is not None, 256),
        grid_spec=pltpu.PrefetchScalarGridSpec(
            num_scalar_prefetch=1,
            grid=(n_exp,),
            in_specs=[
                pl.BlockSpec((rows, width), whole),
                pl.BlockSpec((1, 1, rows), per_e),
                pl.BlockSpec((1, 1, rows), per_e),
                pl.BlockSpec((1, 2 * PACK), whole),
                pl.BlockSpec((1, 1, MOST, width), lambda e, s: (s[0], e, 0, 0)),
                pl.BlockSpec((1, 1, MOST, ff), lambda e, s: (s[0], e, 0, 0)),
                pl.BlockSpec((1, 1, MOST, PACK), lambda e, s: (s[0], e, 0, 0)),
                pl.BlockSpec((1, width, ff), per_e),
                pl.BlockSpec((1, width, ff), per_e),
                pl.BlockSpec((1, ff, width), per_e),
                pl.BlockSpec((1, 2 * PACK, width), per_e),
                pl.BlockSpec((1, PACK, ff), per_e),
                pl.BlockSpec((1, PACK, ff), per_e),
                pl.BlockSpec((1, PACK, ff), per_e),
                pl.BlockSpec((1, PACK, width), per_e),
            ]
            + (grad_specs if prior is not None else []),
            out_specs=[
                pl.BlockSpec((rows, width), whole),
                pl.BlockSpec((rows, width), whole),
            ]
            + grad_specs,
            scratch_shapes=[
                pltpu.VMEM((MOST, width), BF),
                pltpu.VMEM((MOST, ff), BF),
                pltpu.VMEM((MOST, ff), BF),
                pltpu.VMEM((MOST, ff), BF),
                pltpu.VMEM((n_exp * MOST, rows), BF),
                pltpu.VMEM((n_exp * MOST, width), BF),
                pltpu.VMEM((n_exp * MOST, width), BF),
            ],
        ),
        out_shape=[
            jax.ShapeDtypeStruct((rows, width), out_type),
            jax.ShapeDtypeStruct((rows, width), out_type),
        ]
        + [jax.ShapeDtypeStruct((n_exp, 4 * PACK + RANK, width), grad_type)],
        compiler_params=pltpu.CompilerParams(
            vmem_limit_bytes=VMEM, dimension_semantics=("arbitrary",)
        ),
        cost_estimate=pl.CostEstimate(
            flops=16 * n_exp * MOST * width * ff,
            bytes_accessed=6 * n_exp * width * ff,
            transcendentals=n_exp * MOST * ff,
        ),
    )(
        source,
        h2,
        place,
        weight,
        mask,
        *ready,
        w_gate,
        w_up,
        w_low,
        d_gu,
        l_gate,
        l_up,
        d_low,
        l_low,
        *(prior or ()),
    )


def local(
    n_rep,
    n_shard,
    tokens,
    cotangent,
    segments,
    padding,
    routes,
    route_weights,
    adapter_set,
    norm_one,
    norm_two,
    query_weight,
    key_weight,
    value_weight,
    output_weight,
    query_down,
    key_down,
    value_down,
    output_down,
    query_lift,
    key_lift,
    value_lift,
    output_lift,
    expert_gate,
    expert_upper,
    expert_lower,
    gate_down,
    gate_lift,
    upper_down,
    upper_lift,
    lower_down,
    lower_lift,
):
    seq_len, width = tokens.shape
    n_exp, _, ff = expert_gate.shape
    cols = query_weight.shape[1]
    team = min(cols // HEAD, n_rep // 2)
    tiles = cols // HEAD
    half = width // 2
    plane = lax.axis_index("shard")
    rep = lax.axis_index("rep")
    core = rep % 2
    chip = (rep // 2) % team
    ids = jnp.stack([plane, chip, core, rep - rep % (2 * team)]).astype(jnp.int32)

    def rep_swap(x, bits):
        return lax.ppermute(x, "rep", [(a, a ^ bits) for a in range(n_rep)])

    def line_step(up, down):
        return (
            lax.ppermute(up, "shard", [(a, a - 1) for a in range(1, n_shard)]),
            lax.ppermute(down, "shard", [(a, a + 1) for a in range(n_shard - 1)]),
        )

    def line_steps(x):
        steps = [(x, x)]
        for _ in range(1, n_shard):
            steps.append(line_step(*steps[-1]))
        return steps

    def line_join(steps):
        joined = [steps[0][0]]
        for k in range(1, n_shard):
            joined.append(steps[k][0] + steps[n_shard - k][1])
        return joined

    def line_send(x, k):
        return lax.ppermute(x, "shard", [(a, (a + k) % n_shard) for a in range(n_shard)])

    def in_order(parts):
        buf = jnp.zeros((n_shard,) + parts[0].shape, parts[0].dtype)
        for k, part in enumerate(parts):
            buf = lax.dynamic_update_index_in_dim(buf, part, (plane + k) % n_shard, 0)
        return buf

    def chip_gather(x):
        return [x] + [rep_swap(x, j << 1) for j in range(1, team)]

    def after(x, *others):
        return lax.optimization_barrier((x,) + others)[0]

    chosen_set = adapter_set[0]
    set_flags = (jnp.arange(SETS, dtype=jnp.int32) == chosen_set).astype(F32)
    keep = jnp.repeat(set_flags, RANK)[None]
    masks = (segments, segments.reshape(seq_len, 1), padding)
    gain_one, gain_two = norm_one[None], norm_two[None]
    normed_one = rms_forward(tokens.astype(F32), gain_one).astype(BF)
    flag_rows = jnp.pad(jnp.tile(keep, (16, 3)), ((0, 0), (0, width - 3 * PACK))).astype(BF)
    all_h = lax.all_gather(jnp.concatenate([normed_one, flag_rows], axis=0), "rep")

    expert_ids = jnp.arange(EXPERTS, dtype=jnp.int32)
    picked = routes[:, :, None] == expert_ids[None, None, :]
    member = jnp.sum(picked.astype(jnp.int32), axis=1)
    before = jnp.cumsum(member, axis=0) - member
    place = jnp.where(member == 1, before, -1).T.astype(F32)
    per_expert = jnp.sum(jnp.where(picked, route_weights[:, :, None], 0.0), axis=1).T
    high = lax.reduce_precision(per_expert, 8, 7)
    mid = lax.reduce_precision(per_expert - high, 8, 7)
    low = per_expert - high - mid
    flag = jnp.broadcast_to(chosen_set.astype(F32), (EXPERTS, seq_len))
    info = jnp.concatenate([place, high, mid, low, flag], axis=0).astype(BF)
    fact_rows = info.size // HEAD

    def flat(table):
        return table.reshape(table.shape[0], PACK).T

    def pieces(x):
        return x.reshape(x.shape[0], tiles, HEAD).transpose(1, 0, 2).reshape(-1, HEAD)

    def whole_rows(x, height):
        x = x.reshape(n_shard, tiles, height, HEAD)
        return x.transpose(2, 0, 1, 3).reshape(height, width)

    def both(a, b, axis=0):
        return jnp.where(
            core == 0, jnp.concatenate([a, b], axis=axis), jnp.concatenate([b, a], axis=axis)
        )

    def slice_of(weight):
        return lax.dynamic_slice(weight, (core * half, chip * HEAD), (half, HEAD))

    def core_rows(table, height):
        return lax.dynamic_slice(table, (core * height, 0), (height, table.shape[1]))

    lift_rows = 3 * PACK // 2
    down_rows = 4 * PACK // 2
    last_rows = PACK // 2
    lift_pack = jnp.concatenate([flat(t) for t in (query_lift, key_lift, value_lift)], axis=0)
    down_pack = jnp.concatenate(
        [flat(t) for t in (query_down, key_down, value_down, output_down)], axis=0
    )
    out_rows = output_weight.reshape(2, n_shard // 2, tiles, HEAD, cols)
    out_own = lax.dynamic_slice(
        out_rows, (core, 0, chip, 0, 0), (1, n_shard // 2, 1, HEAD, cols)
    ).reshape(n_shard // 2 * HEAD, cols)
    first = [
        pieces(core_rows(down_pack, down_rows)),
        pieces(core_rows(flat(output_lift), last_rows)),
        info.reshape(fact_rows, HEAD),
        pieces(out_own),
    ]
    marks = [0]
    for piece in first:
        marks.append(marks[-1] + piece.shape[0])
    second = [
        slice_of(query_weight),
        lax.dynamic_slice(lift_pack, (core * lift_rows, chip * HEAD), (lift_rows, HEAD)),
        slice_of(key_weight),
        slice_of(value_weight),
    ]
    steps1 = line_steps(jnp.concatenate(first, axis=0))
    line1 = line_join(steps1)
    near1 = in_order(line1)
    out_block = whole_rows(near1[:, marks[3] :], n_shard // 2 * HEAD)
    steps2 = [(after(jnp.concatenate(second, axis=0), *steps1[-2]),) * 2]
    for number in range(1, n_shard):
        last = steps2[-1]
        steps2.append(line_step(*(after(last, out_block) if number == 2 else last)))
    line2 = jnp.stack(line_join(steps2))
    far1 = rep_swap(near1[:, : marks[2]], 1)
    downs = both(*(whole_rows(g[:, : marks[1]], down_rows) for g in (near1, far1)))
    lift_out = both(*(whole_rows(g[:, marks[1] : marks[2]], last_rows) for g in (near1, far1)))
    near_o = chip_gather(out_block)
    far2 = rep_swap(line2, 1)

    params = (
        expert_gate,
        expert_upper,
        expert_lower,
        jnp.concatenate(
            [t.reshape(n_exp, width, PACK).transpose(0, 2, 1) for t in (gate_down, upper_down)],
            axis=1,
        ),
        gate_lift.reshape(n_exp, -1, PACK).transpose(0, 2, 1),
        upper_lift.reshape(n_exp, -1, PACK).transpose(0, 2, 1),
        lower_down.reshape(n_exp, -1, PACK).transpose(0, 2, 1),
        lower_lift.reshape(n_exp, width, PACK).transpose(0, 2, 1),
    )

    def read(facts):
        mine = lax.dynamic_slice_in_dim(facts.astype(F32), plane * n_exp, n_exp, 2)
        flags = (jnp.arange(SETS, dtype=F32) == mine[:, 4, 0, :1]).astype(F32)
        mask = jnp.tile(jnp.repeat(flags, RANK, axis=1), (1, 2))
        return mine[:, 0].astype(jnp.int32), mine[:, 1] + mine[:, 2] + mine[:, 3], mask

    line_facts = read(near1[:, marks[2] : marks[3]].reshape(n_shard, 5, EXPERTS, seq_len))

    sizes = (team, n_shard, seq_len, width)
    made, r_own = project(ids, all_h, downs, line2, far2, sizes)
    made, near_o = lax.optimization_barrier((tuple(made), tuple(near_o)))
    far_o = [rep_swap(b, 1) for b in near_o]
    qkv = [made[0]] + [rep_swap(made[j], j << 1) for j in range(1, team)]
    sizes = sizes + (cols,)
    mixed, r_out, after_attn, normed_two = mix(
        ids, masks, tokens, gain_two, downs[3 * PACK :], lift_out, keep, qkv, near_o, far_o, sizes
    )

    table = [
        sorted((b for b in range(n_shard) if b != a), key=lambda b, a=a: (abs(a - b), a - b))
        for a in range(n_shard)
    ]

    def slot_facts(number):
        source = plane.astype(jnp.int32)
        if number is not None:
            source = sum(jnp.where(plane == a, t[number], 0) for a, t in enumerate(table))
            source = source.astype(jnp.int32)
        spot, share_of, mask = (
            lax.dynamic_index_in_dim(f, source, 0, keepdims=False) for f in line_facts
        )
        return source.reshape(1), spot[:, None], share_of[:, None], mask[None]

    facts_of = {number: slot_facts(number) for number in (*range(n_shard - 1), None)}
    early = [f for facts in facts_of.values() for f in facts]
    cot_line = lax.all_gather(
        after(cotangent, line2, all_h, *params, *line_facts, *early), "shard"
    )
    all_w = lax.all_gather(after(line2, normed_two), "rep")
    row_steps = [(normed_two, normed_two)]
    row_steps.append(line_step(*row_steps[0]))

    def choose(options):
        groups = []
        for a, array in options.items():
            for group in groups:
                if group[0] is array:
                    group[1].append(a)
                    break
            else:
                groups.append((array, [a]))
        value = groups[0][0]
        for array, planes in groups[1:]:
            here = plane == planes[0]
            for a in planes[1:]:
                here = here | (plane == a)
            value = jnp.where(here, array, value)
        return value

    def slot_rows(number):
        options = {}
        for a in range(n_shard):
            far = table[a][number] - a
            options[a] = row_steps[far][0] if far > 0 else row_steps[-far][1]
        return choose(options)

    def send_back(x, number):
        rounds = []
        for a in range(n_shard):
            pair = (a, table[a][number])
            for pairs in rounds:
                if all(pair[1] != q[1] for q in pairs):
                    pairs.append(pair)
                    break
            else:
                rounds.append([pair])
        return [lax.ppermute(x, "shard", pairs) for pairs in rounds]

    spots, shares, set_masks = line_facts
    ready = grad_rows(
        cot_line,
        spots[:, :, None],
        shares[:, :, None],
        set_masks[:, None],
        after(expert_lower, normed_two),
        params[6],
        params[7],
    )

    row_steps[1] = after(row_steps[1], ready[1])
    row_steps.append(line_step(*row_steps[1]))

    def chunk(number, prior, waits):
        rows = normed_two if number is None else slot_rows(number)
        source, spot, share_of, mask = facts_of[number]
        if waits:
            rows = after(rows, *waits)
        return expert_chunk(
            source,
            rows,
            ready,
            spot,
            share_of,
            mask,
            params,
            prior,
            F32 if number is None else BF,
            BF if number is None else F32,
        )

    results, prior, parts = [], None, []
    for number in range(n_shard - 1):
        waits = parts[-2] if number > 1 else ()
        results.append(chunk(number, prior, waits))
        prior = results[-1][2:]
        parts.append(send_back(results[-1][1], number))
        done = number + 2
        if done < n_shard:
            row_steps[done] = after(row_steps[done], results[-1][1])
            if done + 1 < n_shard:
                row_steps.append(line_step(*row_steps[done]))
    own = chunk(None, prior, parts[-2] if n_shard > 2 else ())
    back_parts = [part for pair in parts for part in pair]
    prior, dh2 = own[2:], own[1]
    if len(back_parts) > 6:
        dh2 = dh2 + sum(part.astype(F32) for part in back_parts)
        back_parts = []

    def partial_for(far):
        options = {}
        for a in range(n_shard):
            if 0 <= a + far < n_shard:
                options[a] = results[table[a].index(a + far)][0]
        return choose(options).astype(F32)

    out_steps, up, down = [], None, None
    for far in range(n_shard - 1, 0, -1):
        right, left = partial_for(far), partial_for(-far)
        if up is not None:
            if far == n_shard - 2:
                up, down = after((up, down), own[1])
            right, left = right + up.astype(F32), left + down.astype(F32)
        up = lax.ppermute(
            right.astype(BF), "shard", [(a, a + 1) for a in range(n_shard - far)]
        )
        down = lax.ppermute(
            left.astype(BF), "shard", [(a, a - 1) for a in range(far, n_shard)]
        )
        out_steps.append((up, down))
    pack_shape = prior[0].shape
    split = prior[0].reshape(2, -1, width)
    taken = rep_swap(lax.dynamic_index_in_dim(split, 1 - core, 0, keepdims=False), 1)

    input_grad, attn_flat = attention_back(
        ids,
        (*masks, after(tokens, *out_steps[0]), cotangent, after_attn, gain_one, gain_two, dh2)
        + (downs, lift_out, keep),
        back_parts,
        (mixed, r_own, r_out),
        qkv,
        near_o,
        far_o,
        all_w,
        sizes,
    )
    taken = after(taken, attn_flat)
    mine = lax.dynamic_index_in_dim(split, core, 0, keepdims=False).astype(F32)
    split = (mine + taken.astype(F32)).astype(BF).reshape(team, -1, width)
    chip_total = lax.dynamic_index_in_dim(split, chip, 0, keepdims=False).astype(F32)
    expert_parts = [
        rep_swap(lax.dynamic_index_in_dim(split, chip ^ j, 0, keepdims=False), j << 1)
        for j in range(1, team)
    ]
    for part in expert_parts:
        chip_total = chip_total + part.astype(F32)
    for b in range(team.bit_length(), n_rep.bit_length() - 1):
        rounded = chip_total.astype(BF)
        chip_total = rounded.astype(F32) + rep_swap(rounded, 1 << b).astype(F32)
    rounded = chip_total.astype(BF)
    half_total = jnp.zeros((team,) + rounded.shape, BF)
    for j, part in enumerate(chip_gather(rounded)):
        half_total = lax.dynamic_update_index_in_dim(half_total, part, chip ^ j, 0)
    expert_sums = both(half_total[None], rep_swap(half_total, 1)[None]).reshape(pack_shape)
    if n_shard > 2:
        attn_flat = after(attn_flat, *out_steps[-2])
    output = after_attn + own[0] + up.astype(F32) + down.astype(F32)
    output = output.astype(BF)

    def block_of(k):
        return lax.dynamic_index_in_dim(attn_flat, (plane + k) % n_shard, 0, keepdims=False)

    def placed(part, k):
        own_set = lax.dynamic_index_in_dim(set_masks[:, RANK], (plane - k) % n_shard, 0)
        hit = own_set == jnp.arange(SETS, dtype=F32)
        return jnp.where(hit[:, None, None], part.astype(F32)[None], 0.0)

    total = placed(block_of(0), 0)
    for k in range(1, n_shard):
        total = total + placed(line_send(block_of(k), k), k)
    rounded = total.astype(BF)
    total = rounded.astype(F32) + rep_swap(rounded, 1).astype(F32)
    total = lax.dynamic_index_in_dim(total, core, 0, keepdims=False)
    bits = n_rep.bit_length() - 1
    stages = [[2, 4, 6]] if bits > 2 else [[1 << b] for b in range(1, bits)]
    stages = stages + [[1 << b] for b in range(3, bits)]
    for stage in stages:
        rounded = total.astype(BF)
        total = rounded.astype(F32)
        for swap in stage:
            total = total + rep_swap(rounded, swap).astype(F32)
    rounded = total.astype(BF)
    attn_flat = both(rounded[None], rep_swap(rounded, 1)[None]).astype(F32)

    def unflat(g):
        return g.transpose(2, 0, 1)

    attn_outs = [unflat(attn_flat[:, a * RANK : (a + 1) * RANK]) for a in range(8)]

    def restore(row, height=PACK, column=0, long=width):
        g = expert_sums[:, row : row + height, column : column + long].astype(F32)
        return g.reshape(n_exp, SETS, RANK, long).transpose(0, 3, 1, 2)

    low_rows = expert_sums[:, 4 * PACK :].astype(F32)
    low_rows = jnp.stack([low_rows[:, :, :ff], low_rows[:, :, ff:]], axis=1)
    expert_outs = [
        restore(0),
        restore(2 * PACK, long=ff),
        restore(PACK),
        restore(2 * PACK, column=ff, long=ff),
        low_rows.transpose(0, 3, 1, 2),
        restore(3 * PACK),
    ]
    return (output, input_grad, *attn_outs, *expert_outs)


def solution(mesh):
    rows = P(("rep", "shard"), None)
    second = P(None, "shard")
    three = P("shard", None, None)
    four = P("shard", None, None, None)
    placed = (rows,) * 6 + (P(("rep", "shard")), P(), P()) + (second,) * 4
    placed = placed + (three,) * 11 + (four,) * 6
    return jax.shard_map(
        functools.partial(local, mesh.shape["rep"], mesh.shape["shard"]),
        mesh=mesh,
        in_specs=placed,
        out_specs=(rows, rows) + (three,) * 8 + (four,) * 6,
        check_vma=False,
    )
```

time: 666 us -> 570 us (0.86)
  waiting for transfers between devices: 235 us -> 131 us
  starting transfers between devices: 68.7 us -> 112 us
  local copies, waits for them, and re-layouts: 45.6 us -> 25.7 us
  other arithmetic: 49.5 us -> 38.5 us
    ppermute x12 -> x3, waiting for transfers between devices: 126 us -> 5.14 us  [line_send(): lax.ppermute(x, 'shard', [(a, (a + k) % n_shard) for a in range(n_shard)])]
    ppermute x12 -> x30, starting transfers between devices: 37.6 us -> 89.6 us  [the longest x9 45.7 us: line_step(): lax.ppermute(down, 'shard', [(a, a + 1) for a in range(n_shard - 1)])]
    ppermute x19 -> x25, waiting for transfers between devices: 60.7 us -> 75.1 us  [rep_swap(): return lax.ppermute(x, 'rep', [(a, a ^ bits) for a in range(n_rep)])]
    ppermute x12 -> x3, starting transfers between devices: 14.8 us -> 3.13 us  [line_send(): lax.ppermute(x, 'shard', [(a, (a + k) % n_shard) for a in range(n_shard)])]
    concatenate x5 -> x4, other arithmetic: 9.86 us -> 1.98 us  [the longest x1 1.08 us: local(): jnp.concatenate([normed_one, flag_rows], axis=0)]
    ppermute x19 -> x25, starting transfers between devices: 15.8 us -> 19.3 us  [rep_swap(): return lax.ppermute(x, 'rep', [(a, a ^ bits) for a in range(n_rep)])]
    pallas_call x5 -> x6, Pallas kernels: 214 us -> 210 us  [the longest x4 146 us: expert_chunk(): pl.pallas_call(functools.partial(expert_kernel, n_exp, prior is not None,...]
    ppermute x12 -> x30, waiting for transfers between devices: 48.5 us -> 50.2 us  [the longest x9 39.7 us: line_step(): lax.ppermute(up, 'shard', [(a, a - 1) for a in range(1, n_shard)])]
  transfers between devices with their start and end apart: 46 -> 61, of which waited for: 23 -> 16; matrix products, arithmetic and copies ran while one was open for 13% -> 9% of each run, Pallas kernels for 37% -> 43%
where the time goes in v3:
time: 570 us; the launch traced here: 563 us
  Pallas kernels  240 us (42%)
  waiting for transfers between devices  131 us (23%)
  starting transfers between devices  112 us (20%)
  other arithmetic  38.5 us (7%)
  local copies, waits for them, and re-layouts  25.7 us (5%)
  between operations  16.3 us (3%)
    pallas_call x4, Pallas kernels, expert_chunk(): pl.pallas_call(functools.partial(expert_kernel, n_exp, prior is not None,...  146 us
    ppermute x25, waiting for transfers between devices, rep_swap(): return lax.ppermute(x, 'rep', [(a, a ^ bits) for a in range(n_rep)])  75.1 us
    ppermute x9, starting transfers between devices, line_step(): lax.ppermute(down, 'shard', [(a, a + 1) for a in range(n_shard - 1)])  45.7 us
    ppermute x9, waiting for transfers between devices, line_step(): lax.ppermute(up, 'shard', [(a, a - 1) for a in range(1, n_shard)])  39.7 us
    pallas_call x1, Pallas kernels, attention_back(): pl.pallas_call(functools.partial(back_kernel, sizes, len(parts)), in_spec...  38.3 us
    pallas_call x1, Pallas kernels, grad_rows(): pl.pallas_call(functools.partial(grad_kernel, n_line, 256), grid=(n_exp,)...  25.8 us
    ppermute x25, starting transfers between devices, rep_swap(): return lax.ppermute(x, 'rep', [(a, a ^ bits) for a in range(n_rep)])  19.3 us
    pallas_call x1, Pallas kernels, project(): pl.pallas_call(functools.partial(project_kernel, sizes), in_specs=[pl.Blo...  16.5 us
  transfers between devices with their start and end apart: 61, of which 16 were waited for; matrix products, arithmetic and copies ran while one was open for 9% of the time, Pallas kernels for 43%

profile of v3, /device:TPU:0, one launch (start us, length us, event | category | flops | bytes accessed | tf_op | source)
XLA Modules:
  0.0 563.4 jit_solution(7522999673682523784)
XLA Ops:
  14.9 5.8 %collective-permute-start.1 = (bf16[1504,128]{1,0:T(8,128)(2,1)}, bf16[1504,128]{1,0:T(8,128)(2,1)}, u32[]{:S(2)}, u32[]{:S(2)}) collective-permute-start(bf16[1504,128]{1,0:T(8,128)(2,1)} %pad_maximum_fusion.4), channel_id=1, source_target_pairs={{0,1},{1,2},{2,3},{4,5},{5,6},{6,7},{8,9},{9,10},{10,11},{12,13},{... | collective-permute-start | bytes 1155080 | tf_op jit(solution)/shard_map/ppermute | solution.py:668
  22.1 6.4 %collective-permute-done.1 = bf16[1504,128]{1,0:T(8,128)(2,1)} collective-permute-done((bf16[1504,128]{1,0:T(8,128)(2,1)}, bf16[1504,128]{1,0:T(8,128)(2,1)}, u32[]{:S(2)}, u32[]{:S(2)}) %collective-permute-start.1) | collective-permute-done | bytes 385056 | tf_op jit(solution)/shard_map/ppermute | solution.py:668
  28.5 5.1 collective-permute-start.2
  36.5 4.0 collective-permute-done.2
  40.5 4.4 collective-permute-start.3
  48.1 5.5 collective-permute-start.8
  57.2 17.3 %collective-permute-done.5 = bf16[1504,128]{1,0:T(8,128)(2,1)S(1)} collective-permute-done((bf16[1504,128]{1,0:T(8,128)(2,1)S(1)}, bf16[1504,128]{1,0:T(8,128)(2,1)S(1)}, u32[]{:S(2)}, u32[]{:S(2)}) %collective-permute-start.5) | collective-permute-done | bytes 385056 | tf_op jit(solution)/shard_map/ppermute | solution.py:667
  80.2 4.6 collective-permute-start.9
  88.5 9.1 %collective-permute-done.11 = bf16[3120,128]{1,0:T(8,128)(2,1)S(1)} collective-permute-done((bf16[3120,128]{1,0:T(8,128)(2,1)}, bf16[3120,128]{1,0:T(8,128)(2,1)S(1)}, u32[]{:S(2)}, u32[]{:S(2)}) %collective-permute-start.11) | collective-permute-done | bytes 798752 | tf_op jit(solution)/shard_map/ppermute | solution.py:667
  98.9 4.6 collective-permute-start.10
  103.6 11.5 %collective-permute-done.12 = bf16[3120,128]{1,0:T(8,128)(2,1)S(1)} collective-permute-done((bf16[3120,128]{1,0:T(8,128)(2,1)S(1)}, bf16[3120,128]{1,0:T(8,128)(2,1)S(1)}, u32[]{:S(2)}, u32[]{:S(2)}) %collective-permute-start.12) | collective-permute-done | bytes 798752 | tf_op jit(solution)/shard_map/ppermute | solution.py:667
  131.3 16.5 %shard_map.405 = (bf16[256,1536]{1,0:T(8,128)(2,1)}, bf16[256,1536]{1,0:T(8,128)(2,1)}, bf16[256,1536]{1,0:T(8,128)(2,1)}, bf16[256,1536]{1,0:T(8,128)(2,1)}, bf16[3,256,32]{2,1,0:T(8,128)(2,1)}) custom-call(s32[4]{0:T(128)} %pad_add_fusion.ids, bf16[8,272,2048]{2,1,0:T(8,128)(2,1)} %bitcast.299, bf16[128,2048]{1,0:T(8,128)(2,1)} %maximum_select_fusion.1.downs.refs_9_, ...), custom_call_target="tpu_custom_call" | custom-call | flops 6442450944 | bytes 12582912 | tf_op jit(solution)/shard_map/pallas_call | solution.py:131
  147.9 22.2 %collective-permute-done.15.refs_6_.refs_27_ = bf16[256,2048]{1,0:T(8,128)(2,1)} collective-permute-done((bf16[256,2048]{1,0:T(8,128)(2,1)}, bf16[256,2048]{1,0:T(8,128)(2,1)}, u32[]{:S(2)}, u32[]{:S(2)}) %collective-permute-start.15) | collective-permute-done | bytes 1048608 | tf_op jit(solution)/shard_map/ppermute | solution.py:663
  172.7 16.4 %collective-permute-done.17.refs_1_.refs_22_ = bf16[256,1536]{1,0:T(8,128)(2,1)} collective-permute-done((bf16[256,1536]{1,0:T(8,128)(2,1)}, bf16[256,1536]{1,0:T(8,128)(2,1)}, u32[]{:S(2)}, u32[]{:S(2)}) %collective-permute-start.17) | collective-permute-done | bytes 786464 | tf_op jit(solution)/shard_map/ppermute | solution.py:663
  197.3 13.0 %collective-permute-done.19.refs_3_.refs_24_ = bf16[256,1536]{1,0:T(8,128)(2,1)} collective-permute-done((bf16[256,1536]{1,0:T(8,128)(2,1)}, bf16[256,1536]{1,0:T(8,128)(2,1)}, u32[]{:S(2)}, u32[]{:S(2)}) %collective-permute-start.19) | collective-permute-done | bytes 786464 | tf_op jit(solution)/shard_map/ppermute | solution.py:663
  212.0 13.3 %shard_map.406 = (bf16[256,2048]{1,0:T(8,128)(2,1)}, bf16[256,32]{1,0:T(8,128)(2,1)}, f32[256,2048]{1,0:T(8,128)}, bf16[256,2048]{1,0:T(8,128)(2,1)}) custom-call(s32[4]{0:T(128)} %pad_add_fusion.ids, s32[1,256]{1,0:T(1,128)} %refs_0_.1, s32[256,1]{1,0:T(8,128)} %copy.107.seg_col.refs_1_, s32[1,256]{1,0:T(1,128)} %refs_2_.1, bf16[256,2048]{1,0:T(8,128)(2,1)} %refs_3_, ...), custom_call_target="tpu_custom_call" | custom-call | flops 2684354560 | bytes 14680064 | tf_op jit(solution)/shard_map/pallas_call | solution.py:200
  227.7 5.4 collective-permute-start.25
  233.2 25.8 %shard_map.407 = (bf16[4,4,160,2048]{3,2,1,0:T(8,128)(2,1)}, bf16[4,4,160,1024]{3,2,1,0:T(8,128)(2,1)}, bf16[4,4,160,32]{3,2,1,0:T(8,128)(2,1)}) custom-call(bf16[4,256,2048]{2,1,0:T(8,128)(2,1)} %bitcast.300, s32[4,4,1,256]{3,2,1,0:T(1,128)} %get-tuple-element.154.place, f32[4,4,1,256]{3,2,1,0:T(1,128)} %bitcast.285, f32[4,1,64]{2,1,0:T(1,128)} %tile.28.mask, ...), custom_call_target="tpu_custom_call" | custom-call | flops 16106127360 | bytes 16777216 | tf_op jit(solution)/shard_map/pallas_call | solution.py:505
  260.3 4.6 collective-permute-start.27
  266.0 38.1 %shard_map.408 = (bf16[256,2048]{1,0:T(8,128)(2,1)}, bf16[256,2048]{1,0:T(8,128)(2,1)}, f32[4,144,2048]{2,1,0:T(8,128)}) custom-call(s32[1]{0:T(128)} %bitcast.64.source, bf16[256,2048]{1,0:T(8,128)(2,1)} %broadcast_select_fusion.h2, s32[4,1,256]{2,1,0:T(1,128)} %get-tuple-element.163.place, f32[4,1,256]{2,1,0:T(1,128)} %get-tuple-element.159.weight, ...), custom_call_target="tpu_custom_call" | custom-call | flops 21474836480 | bytes 50331648 | tf_op jit(solution)/shard_map/pallas_call | solution.py:546
  310.0 5.7 %collective-permute-start.31 = (bf16[256,2048]{1,0:T(8,128)(2,1)S(1)}, bf16[256,2048]{1,0:T(8,128)(2,1)}, u32[]{:S(2)}, u32[]{:S(2)}) collective-permute-start(bf16[256,2048]{1,0:T(8,128)(2,1)S(1)} %collective-permute-done.27), channel_id=1, source_target_pairs={{0,1},{1,2},{2,3},{4,5},{5,6},{6,7},{8,9},{9,10},{10,11},{12,13},{... | collective-permute-start | bytes 3145736 | tf_op jit(solution)/shard_map/ppermute | solution.py:668
  316.8 35.7 %shard_map.409 = (bf16[256,2048]{1,0:T(8,128)(2,1)}, bf16[256,2048]{1,0:T(8,128)(2,1)}, f32[4,144,2048]{2,1,0:T(8,128)}) custom-call(s32[1]{0:T(128)} %bitcast.51.source, bf16[256,2048]{1,0:T(8,128)(2,1)} %select_select_fusion.1.h2, s32[4,1,256]{2,1,0:T(1,128)} %get-tuple-element.162.place, f32[4,1,256]{2,1,0:T(1,128)} %get-tuple-element.158.weight, ...), custom_call_target="tpu_custom_call" | custom-call | flops 21474836480 | bytes 50331648 | tf_op jit(solution)/shard_map/pallas_call | solution.py:546
  356.8 36.3 %shard_map.410 = (bf16[256,2048]{1,0:T(8,128)(2,1)}, bf16[256,2048]{1,0:T(8,128)(2,1)}, f32[4,144,2048]{2,1,0:T(8,128)}) custom-call(s32[1]{0:T(128)} %bitcast.69.source, bf16[256,2048]{1,0:T(8,128)(2,1)} %select_select_fusion.h2, s32[4,1,256]{2,1,0:T(1,128)} %get-tuple-element.161.place, f32[4,1,256]{2,1,0:T(1,128)} %get-tuple-element.157.weight, ...), custom_call_target="tpu_custom_call" | custom-call | flops 21474836480 | bytes 50331648 | tf_op jit(solution)/shard_map/pallas_call | solution.py:546
  393.1 4.2 collective-permute-start.34
  398.1 5.6 collective-permute-start.40
  406.4 36.1 %shard_map.411 = (f32[256,2048]{1,0:T(8,128)}, f32[256,2048]{1,0:T(8,128)}, bf16[4,144,2048]{2,1,0:T(8,128)(2,1)}) custom-call(s32[1]{0:T(128)} %bitcast.source, bf16[256,2048]{1,0:T(8,128)(2,1)} %get-tuple-element.98.h2, s32[4,1,256]{2,1,0:T(1,128)} %get-tuple-element.160.place, f32[4,1,256]{2,1,0:T(1,128)} %get-tuple-element.156.weight, ...), custom_call_target="tpu_custom_call" | custom-call | flops 21474836480 | bytes 50331648 | tf_op jit(solution)/shard_map/pallas_call | solution.py:546
  446.6 4.4 collective-permute-start.36
  454.6 38.3 %shard_map.412 = (bf16[256,2048]{1,0:T(8,128)(2,1)}, bf16[4,128,512]{2,1,0:T(8,128)(2,1)}) custom-call(s32[4]{0:T(128)} %pad_add_fusion.ids, s32[1,256]{1,0:T(1,128)} %refs_0_.1, s32[256,1]{1,0:T(8,128)} %copy.107.seg_col.refs_1_, s32[1,256]{1,0:T(1,128)} %refs_2_.1, bf16[256,2048]{1,0:T(8,128)(2,1)} %refs_3_, bf16[256,2048]{1,0:T(8,128)(2,1)} %refs_4_.1, ...), custom_call_target="tpu_custom_call" | custom-call | flops 9932111872 | bytes 44040192 | tf_op jit(solution)/shard_map/pallas_call | solution.py:361
  503.1 5.1 collective-permute-done.43
  508.7 4.9 collective-permute-done.52
  519.3 5.2 collective-permute-start.37
  528.2 13.8 %collective-permute-done.55 = bf16[72,2048]{1,0:T(8,128)(2,1)S(1)} collective-permute-done((bf16[72,2048]{1,0:T(8,128)(2,1)S(1)}, bf16[72,2048]{1,0:T(8,128)(2,1)S(1)}, u32[]{:S(2)}, u32[]{:S(2)}) %collective-permute-start.55) | collective-permute-done | bytes 294944 | tf_op jit(solution)/shard_map/ppermute | solution.py:663
  (298 shorter events, 118.1 us)
Async XLA Ops:
  7.2 111.0 %all-gather.7.cloned.1.call-start = ((), (), s32[]{:S(2)}) async-start(), calls=%async_computation | async-start | bytes 10027008 | tf_op jit(solution)/shard_map/all_gather | solution.py:705
  12.5 220.6 %all-gather.9.cloned.1.call-start = ((), (), s32[]{:S(2)}) async-start(), calls=%async_computation.1 | async-start | bytes 5242880 | tf_op jit(solution)/shard_map/all_gather | solution.py:831
  46.8 31.5 %collective-permute-start.7 = (bf16[3120,128]{1,0:T(8,128)(2,1)S(1)}, bf16[3120,128]{1,0:T(8,128)(2,1)}, u32[]{:S(2)}, u32[]{:S(2)}) collective-permute-start(bf16[3120,128]{1,0:T(8,128)(2,1)S(1)} %pad_maximum_fusion.3), channel_id=1, source_target_pairs={{1,0},{2,1},{3,2},{5,4},{6,5},{7,6},{9,8},{10,9},{11,10},{13,12},{... | collective-permute-start | bytes 2396168 | tf_op jit(solution)/shard_map/ppermute | solution.py:667
  48.1 30.2 %collective-permute-start.8 = (bf16[3120,128]{1,0:T(8,128)(2,1)S(1)}, bf16[3120,128]{1,0:T(8,128)(2,1)}, u32[]{:S(2)}, u32[]{:S(2)}) collective-permute-start(bf16[3120,128]{1,0:T(8,128)(2,1)S(1)} %pad_maximum_fusion.3), channel_id=1, source_target_pairs={{0,1},{1,2},{2,3},{4,5},{5,6},{6,7},{8,9},{9,10},{10,11},{12,13},{... | collective-permute-start | bytes 2396168 | tf_op jit(solution)/shard_map/ppermute | solution.py:668
  53.6 20.9 %collective-permute-start.5 = (bf16[1504,128]{1,0:T(8,128)(2,1)S(1)}, bf16[1504,128]{1,0:T(8,128)(2,1)S(1)}, u32[]{:S(2)}, u32[]{:S(2)}) collective-permute-start(bf16[1504,128]{1,0:T(8,128)(2,1)S(1)} %collective-permute-done.4), channel_id=1, source_target_pairs={{1,0},{2,1},{3,2},{5,4},{6,5},{7,6},{9,8},{10,9},{11,10},{13,12},{... | collective-permute-start | bytes 1155080 | tf_op jit(solution)/shard_map/ppermute | solution.py:667
  118.3 336.3 %all-gather.11.cloned.1.call-start = ((), (), s32[]{:S(2)}) async-start(), calls=%async_computation.2 | async-start | bytes 28753920 | tf_op jit(solution)/shard_map/all_gather | solution.py:834
  120.8 27.1 %collective-permute-start.14 = (bf16[256,2048]{1,0:T(8,128)(2,1)}, bf16[256,2048]{1,0:T(8,128)(2,1)}, u32[]{:S(2)}, u32[]{:S(2)}) collective-permute-start(bf16[256,2048]{1,0:T(8,128)(2,1)} %reshape.331.refs_4_.refs_25_), channel_id=1, source_target_pairs={{0,8},{4,12},{8,0},{12,4},{16,24},{20,28},{24,16},{28,20},{1,9},{5... | collective-permute-start | bytes 3145736 | tf_op jit(solution)/shard_map/ppermute | solution.py:663
  122.3 47.8 %collective-permute-start.15 = (bf16[256,2048]{1,0:T(8,128)(2,1)}, bf16[256,2048]{1,0:T(8,128)(2,1)}, u32[]{:S(2)}, u32[]{:S(2)}) collective-permute-start(bf16[256,2048]{1,0:T(8,128)(2,1)} %reshape.331.refs_4_.refs_25_), channel_id=1, source_target_pairs={{0,16},{4,20},{8,24},{12,28},{16,0},{20,4},{24,8},{28,12},{1,17},{... | collective-permute-start | bytes 3145736 | tf_op jit(solution)/shard_map/ppermute | solution.py:663
  123.8 46.3 %collective-permute-start.16 = (bf16[256,2048]{1,0:T(8,128)(2,1)}, bf16[256,2048]{1,0:T(8,128)(2,1)}, u32[]{:S(2)}, u32[]{:S(2)}) collective-permute-start(bf16[256,2048]{1,0:T(8,128)(2,1)} %reshape.331.refs_4_.refs_25_), channel_id=1, source_target_pairs={{0,24},{4,28},{8,16},{12,20},{16,8},{20,12},{24,0},{28,4},{1,25},{... | collective-permute-start | bytes 3145736 | tf_op jit(solution)/shard_map/ppermute | solution.py:663
  172.2 38.1 %collective-permute-start.20 = (bf16[256,2048]{1,0:T(8,128)(2,1)}, bf16[256,2048]{1,0:T(8,128)(2,1)S(1)}, u32[]{:S(2)}, u32[]{:S(2)}) collective-permute-start(bf16[256,2048]{1,0:T(8,128)(2,1)} %reshape.331.refs_4_.refs_25_), channel_id=1, source_target_pairs={{0,4},{4,0},{8,12},{12,8},{16,20},{20,16},{24,28},{28,24},{1,5},{5... | collective-permute-start | bytes 3145736 | tf_op jit(solution)/shard_map/ppermute | solution.py:663
  172.2 38.1 %collective-permute-start.21 = (bf16[256,2048]{1,0:T(8,128)(2,1)}, bf16[256,2048]{1,0:T(8,128)(2,1)S(1)}, u32[]{:S(2)}, u32[]{:S(2)}) collective-permute-start(bf16[256,2048]{1,0:T(8,128)(2,1)} %collective-permute-done.14.refs_5_.refs_26_), channel_id=1, source_target_pairs={{0,4},{4,0},{8,12},{12,8},{16,20},{20,16},{24,28},{28,24},{1,5},{5... | collective-permute-start | bytes 3145736 | tf_op jit(solution)/shard_map/ppermute | solution.py:663
  172.7 37.6 %collective-permute-start.22 = (bf16[256,2048]{1,0:T(8,128)(2,1)}, bf16[256,2048]{1,0:T(8,128)(2,1)S(1)}, u32[]{:S(2)}, u32[]{:S(2)}) collective-permute-start(bf16[256,2048]{1,0:T(8,128)(2,1)} %collective-permute-done.15.refs_6_.refs_27_), channel_id=1, source_target_pairs={{0,4},{4,0},{8,12},{12,8},{16,20},{20,16},{24,28},{28,24},{1,5},{5... | collective-permute-start | bytes 3145736 | tf_op jit(solution)/shard_map/ppermute | solution.py:663
  189.1 21.2 %collective-permute-start.23 = (bf16[256,2048]{1,0:T(8,128)(2,1)}, bf16[256,2048]{1,0:T(8,128)(2,1)}, u32[]{:S(2)}, u32[]{:S(2)}) collective-permute-start(bf16[256,2048]{1,0:T(8,128)(2,1)} %collective-permute-done.16.refs_7_.refs_28_), channel_id=1, source_target_pairs={{0,4},{4,0},{8,12},{12,8},{16,20},{20,16},{24,28},{28,24},{1,5},{5... | collective-permute-start | bytes 3145736 | tf_op jit(solution)/shard_map/ppermute | solution.py:663
  226.5 32.5 %collective-permute-start.24 = (bf16[256,2048]{1,0:T(8,128)(2,1)S(1)}, bf16[256,2048]{1,0:T(8,128)(2,1)S(1)}, u32[]{:S(2)}, u32[]{:S(2)}) collective-permute-start(bf16[256,2048]{1,0:T(8,128)(2,1)S(1)} %copy-done.34), channel_id=1, source_target_pairs={{1,0},{2,1},{3,2},{5,4},{6,5},{7,6},{9,8},{10,9},{11,10},{13,12},{... | collective-permute-start | bytes 3145736 | tf_op jit(solution)/shard_map/ppermute | solution.py:667
  227.7 31.2 %collective-permute-start.25 = (bf16[256,2048]{1,0:T(8,128)(2,1)S(1)}, bf16[256,2048]{1,0:T(8,128)(2,1)S(1)}, u32[]{:S(2)}, u32[]{:S(2)}) collective-permute-start(bf16[256,2048]{1,0:T(8,128)(2,1)S(1)} %copy-done.34), channel_id=1, source_target_pairs={{0,1},{1,2},{2,3},{4,5},{5,6},{6,7},{8,9},{9,10},{10,11},{12,13},{... | collective-permute-start | bytes 3145736 | tf_op jit(solution)/shard_map/ppermute | solution.py:668
  259.0 49.7 %collective-permute-start.26 = (bf16[256,2048]{1,0:T(8,128)(2,1)S(1)}, bf16[256,2048]{1,0:T(8,128)(2,1)S(1)}, u32[]{:S(2)}, u32[]{:S(2)}) collective-permute-start(bf16[256,2048]{1,0:T(8,128)(2,1)S(1)} %collective-permute-done.24), channel_id=1, source_target_pairs={{1,0},{2,1},{3,2},{5,4},{6,5},{7,6},{9,8},{10,9},{11,10},{13,12},{... | collective-permute-start | bytes 3145736 | tf_op jit(solution)/shard_map/ppermute | solution.py:667
  260.3 48.4 %collective-permute-start.27 = (bf16[256,2048]{1,0:T(8,128)(2,1)S(1)}, bf16[256,2048]{1,0:T(8,128)(2,1)S(1)}, u32[]{:S(2)}, u32[]{:S(2)}) collective-permute-start(bf16[256,2048]{1,0:T(8,128)(2,1)S(1)} %collective-permute-done.25), channel_id=1, source_target_pairs={{0,1},{1,2},{2,3},{4,5},{5,6},{6,7},{8,9},{9,10},{10,11},{12,13},{... | collective-permute-start | bytes 3145736 | tf_op jit(solution)/shard_map/ppermute | solution.py:668
  304.1 52.7 %collective-permute-start.32 = (bf16[256,2048]{1,0:T(8,128)(2,1)}, bf16[256,2048]{1,0:T(8,128)(2,1)S(1)}, u32[]{:S(2)}, u32[]{:S(2)}) collective-permute-start(bf16[256,2048]{1,0:T(8,128)(2,1)} %get-tuple-element.93), channel_id=1, source_target_pairs={{0,1},{1,2},{2,3},{4,5},{5,6},{6,7},{8,9},{9,10},{10,11},{12,13},{... | collective-permute-start | bytes 3145736 | tf_op jit(solution)/shard_map/ppermute | solution.py:872
  307.9 48.9 %collective-permute-start.33 = (bf16[256,2048]{1,0:T(8,128)(2,1)}, bf16[256,2048]{1,0:T(8,128)(2,1)S(1)}, u32[]{:S(2)}, u32[]{:S(2)}) collective-permute-start(bf16[256,2048]{1,0:T(8,128)(2,1)} %get-tuple-element.93), channel_id=1, source_target_pairs={{3,2},{7,6},{11,10},{15,14},{19,18},{23,22},{27,26},{31,30}} | collective-permute-start | bytes 3145736 | tf_op jit(solution)/shard_map/ppermute | solution.py:872
  308.7 46.1 %collective-permute-start.30 = (bf16[256,2048]{1,0:T(8,128)(2,1)S(1)}, bf16[256,2048]{1,0:T(8,128)(2,1)S(1)}, u32[]{:S(2)}, u32[]{:S(2)}) collective-permute-start(bf16[256,2048]{1,0:T(8,128)(2,1)S(1)} %collective-permute-done.26), channel_id=1, source_target_pairs={{1,0},{2,1},{3,2},{5,4},{6,5},{7,6},{9,8},{10,9},{11,10},{13,12},{... | collective-permute-start | bytes 3145736 | tf_op jit(solution)/shard_map/ppermute | solution.py:667
  310.0 45.6 %collective-permute-start.31 = (bf16[256,2048]{1,0:T(8,128)(2,1)S(1)}, bf16[256,2048]{1,0:T(8,128)(2,1)}, u32[]{:S(2)}, u32[]{:S(2)}) collective-permute-start(bf16[256,2048]{1,0:T(8,128)(2,1)S(1)} %collective-permute-done.27), channel_id=1, source_target_pairs={{0,1},{1,2},{2,3},{4,5},{5,6},{6,7},{8,9},{9,10},{10,11},{12,13},{... | collective-permute-start | bytes 3145736 | tf_op jit(solution)/shard_map/ppermute | solution.py:668
  352.6 51.1 %collective-permute-start.28 = (bf16[256,2048]{1,0:T(8,128)(2,1)}, bf16[256,2048]{1,0:T(8,128)(2,1)S(1)}, u32[]{:S(2)}, u32[]{:S(2)}) collective-permute-start(bf16[256,2048]{1,0:T(8,128)(2,1)} %get-tuple-element.97), channel_id=1, source_target_pairs={{0,2},{1,0},{2,1},{4,6},{5,4},{6,5},{8,10},{9,8},{10,9},{12,14},{1... | collective-permute-start | bytes 3145736 | tf_op jit(solution)/shard_map/ppermute | solution.py:872
  354.8 50.6 %collective-permute-start.29 = (bf16[256,2048]{1,0:T(8,128)(2,1)}, bf16[256,2048]{1,0:T(8,128)(2,1)S(1)}, u32[]{:S(2)}, u32[]{:S(2)}) collective-permute-start(bf16[256,2048]{1,0:T(8,128)(2,1)} %get-tuple-element.97), channel_id=1, source_target_pairs={{3,1},{7,5},{11,9},{15,13},{19,17},{23,21},{27,25},{31,29}} | collective-permute-start | bytes 3145736 | tf_op jit(solution)/shard_map/ppermute | solution.py:872
  393.1 51.0 %collective-permute-start.34 = (bf16[256,2048]{1,0:T(8,128)(2,1)}, bf16[256,2048]{1,0:T(8,128)(2,1)S(1)}, u32[]{:S(2)}, u32[]{:S(2)}) collective-permute-start(bf16[256,2048]{1,0:T(8,128)(2,1)} %get-tuple-element.106), channel_id=1, source_target_pairs={{0,1},{4,5},{8,9},{12,13},{16,17},{20,21},{24,25},{28,29}} | collective-permute-start | bytes 3145736 | tf_op jit(solution)/shard_map/ppermute | solution.py:938
  397.4 46.8 %collective-permute-start.35 = (bf16[256,2048]{1,0:T(8,128)(2,1)}, bf16[256,2048]{1,0:T(8,128)(2,1)S(1)}, u32[]{:S(2)}, u32[]{:S(2)}) collective-permute-start(bf16[256,2048]{1,0:T(8,128)(2,1)} %get-tuple-element.106), channel_id=1, source_target_pairs={{3,2},{7,6},{11,10},{15,14},{19,18},{23,22},{27,26},{31,30}} | collective-permute-start | bytes 3145736 | tf_op jit(solution)/shard_map/ppermute | solution.py:941
  398.1 56.4 %collective-permute-start.40 = (bf16[256,2048]{1,0:T(8,128)(2,1)}, bf16[256,2048]{1,0:T(8,128)(2,1)}, u32[]{:S(2)}, u32[]{:S(2)}) collective-permute-start(bf16[256,2048]{1,0:T(8,128)(2,1)} %get-tuple-element.112), channel_id=1, source_target_pairs={{0,3},{2,0},{4,7},{6,4},{8,11},{10,8},{12,15},{14,12},{16,19},{18,... | collective-permute-start | bytes 3145736 | tf_op jit(solution)/shard_map/ppermute | solution.py:872
  403.7 50.8 %collective-permute-start.41 = (bf16[256,2048]{1,0:T(8,128)(2,1)}, bf16[256,2048]{1,0:T(8,128)(2,1)}, u32[]{:S(2)}, u32[]{:S(2)}) collective-permute-start(bf16[256,2048]{1,0:T(8,128)(2,1)} %get-tuple-element.112), channel_id=1, source_target_pairs={{1,3},{3,0},{5,7},{7,4},{9,11},{11,8},{13,15},{15,12},{17,19},{19,... | collective-permute-start | bytes 3145736 | tf_op jit(solution)/shard_map/ppermute | solution.py:872
  444.0 53.1 %collective-permute-start.50 = (bf16[288,2048]{1,0:T(8,128)(2,1)S(1)}, bf16[288,2048]{1,0:T(8,128)(2,1)S(1)}, u32[]{:S(2)}, u32[]{:S(2)}) collective-permute-start(bf16[288,2048]{1,0:T(8,128)(2,1)S(1)} %dynamic-slice_bitcast_fusion), channel_id=1, source_target_pairs={{0,4},{4,0},{8,12},{12,8},{16,20},{20,16},{24,28},{28,24},{1,5},{5... | collective-permute-start | bytes 3538952 | tf_op jit(solution)/shard_map/ppermute | solution.py:663
  446.6 46.3 %collective-permute-start.36 = (bf16[256,2048]{1,0:T(8,128)(2,1)}, bf16[256,2048]{1,0:T(8,128)(2,1)}, u32[]{:S(2)}, u32[]{:S(2)}) collective-permute-start(bf16[256,2048]{1,0:T(8,128)(2,1)} %get-tuple-element.129), channel_id=1, source_target_pairs={{0,1},{1,2},{4,5},{5,6},{8,9},{9,10},{12,13},{13,14},{16,17},{17,1... | collective-permute-start | bytes 3145736 | tf_op jit(solution)/shard_map/ppermute | solution.py:938
  451.0 41.9 %collective-permute-start.38 = (bf16[256,2048]{1,0:T(8,128)(2,1)}, bf16[256,2048]{1,0:T(8,128)(2,1)}, u32[]{:S(2)}, u32[]{:S(2)}) collective-permute-start(bf16[256,2048]{1,0:T(8,128)(2,1)} %get-tuple-element.130), channel_id=1, source_target_pairs={{2,1},{3,2},{6,5},{7,6},{10,9},{11,10},{14,13},{15,14},{18,17},{19... | collective-permute-start | bytes 3145736 | tf_op jit(solution)/shard_map/ppermute | solution.py:941
  517.9 29.9 %collective-permute-start.39 = (bf16[256,2048]{1,0:T(8,128)(2,1)S(1)}, bf16[256,2048]{1,0:T(8,128)(2,1)S(1)}, u32[]{:S(2)}, u32[]{:S(2)}) collective-permute-start(bf16[256,2048]{1,0:T(8,128)(2,1)S(1)} %get-tuple-element.135), channel_id=1, source_target_pairs={{1,0},{2,1},{3,2},{5,4},{6,5},{7,6},{9,8},{10,9},{11,10},{13,12},{... | collective-permute-start | bytes 3145736 | tf_op jit(solution)/shard_map/ppermute | solution.py:941
  519.3 28.4 %collective-permute-start.37 = (bf16[256,2048]{1,0:T(8,128)(2,1)S(1)}, bf16[256,2048]{1,0:T(8,128)(2,1)S(1)}, u32[]{:S(2)}, u32[]{:S(2)}) collective-permute-start(bf16[256,2048]{1,0:T(8,128)(2,1)S(1)} %get-tuple-element.134), channel_id=1, source_target_pairs={{0,1},{1,2},{2,3},{4,5},{5,6},{6,7},{8,9},{9,10},{10,11},{12,13},{... | collective-permute-start | bytes 3145736 | tf_op jit(solution)/shard_map/ppermute | solution.py:938
  (67 other events, 899.2 us)
Sparse Core Ops, SparseCore 0:
  12.7 59.2 all-gather.6
  118.4 82.1 all-gather.8
  225.4 127.3 all-gather.10

commit v4 on v3

--- a/solution.py
+++ b/solution.py
@@ -54,7 +54,7 @@
     s = dot_nt(q, k) * score_scale
     s = jnp.where(allowed, s, masked_score)
     e = jnp.exp(s - jnp.max(s, axis=-1, keepdims=True))
-    return e / jnp.sum(e, axis=-1, keepdims=True)
+    return e * (1.0 / jnp.sum(e, axis=-1, keepdims=True))
 
 
 def allowed_mask(seg_row, seg_col, pad_row):
@@ -330,19 +330,18 @@
         for a in range(3):
             lift_s[a] = packs[a * PACK : (a + 1) * PACK]
 
-        def grad(a, carry):
-            g = dp_s[:, pl.ds(pl.multiple_of(a * span, HEAD), span)]
-            lift = lift_s[a]
-            dr[a] += dot_nt(g, lift)
-            put(
-                pl.multiple_of((4 + a) * RANK, RANK), adapter_scale * dot_tn(r_own[a], g)
-            )
-            rows_a = pl.ds(pl.multiple_of(a * half + lift_gap * jnp.minimum(a, 1), 16), half)
-            acc[:, pl.ds(here, half)] += dot_nt(g, near_s[slot, rows_a, :])
-            acc[:, pl.ds(there, half)] += dot_nt(g, far_s[slot, rows_a, :])
-            return carry
-
-        lax.fori_loop(0, 3, grad, 0)
+        near_sum, far_sum = None, None
+        for a in range(3):
+            g = dp_s[:, a * span : (a + 1) * span]
+            dr[a] += dot_nt(g, lift_s[a])
+            put((4 + a) * RANK, adapter_scale * dot_tn(r_own[a], g))
+            start = a * half + (lift_gap if a else 0)
+            near_part = dot_nt(g, near_s[slot, start : start + half, :])
+            far_part = dot_nt(g, far_s[slot, start : start + half, :])
+            near_sum = near_part if a == 0 else near_sum + near_part
+            far_sum = far_part if a == 0 else far_sum + far_part
+        acc[:, pl.ds(here, half)] += near_sum
+        acc[:, pl.ds(there, half)] += far_sum
     h1 = h1_s[...]
     for a in range(3):
         low = (adapter_scale * dr[a] * mask).astype(BF)
@@ -417,7 +416,7 @@
     if has_sum:
         prior, refs = refs[0], refs[1:]
     (out, dh2, grads) = refs[:3]
-    (x_s, hid_s, dg_s, du_s, sel, y_all, dx_all) = refs[3:]
+    (x_s, hid_s, dg_s, du_s, sel, y_all, dx_all, gate_s, up_s, low_s, sems) = refs[3:]
     ff = w_gate.shape[2]
 
     def emit(row, value, column=0):
@@ -427,6 +426,26 @@
         grads[at] = value.astype(grads.dtype)
 
     e = pl.program_id(0)
+    slot = e % 2
+
+    def fetch(number):
+        pairs = ((w_gate, gate_s), (w_up, up_s), (w_low, low_s))
+        return [
+            pltpu.make_async_copy(w.at[number], buf.at[number % 2], sems.at[number % 2, i])
+            for i, (w, buf) in enumerate(pairs)
+        ]
+
+    @pl.when(e == 0)
+    def _():
+        for copy in fetch(e):
+            copy.start()
+
+    @pl.when(e + 1 < n_exp)
+    def _():
+        for copy in fetch(e + 1):
+            copy.start()
+
+    ready = fetch(e)
     keep = mask[...]
     keep_one = keep[:, :PACK]
     base = pl.multiple_of(e * MOST, MOST)
@@ -441,10 +460,12 @@
     r_gu = (dot_nt(x, d_gu[0]) * keep).astype(BF)
     r_g, r_u = r_gu[:, :PACK], r_gu[:, PACK:]
     dr_low = drl_in[0, 0]
+    ready[0].wait()
+    ready[1].wait()
     for start in range(0, w_gate.shape[2], tile):
         at = slice(start, start + tile)
-        gate = dot_nn(x, w_gate[0, :, at]) + adapter_scale * dot_nn(r_g, l_gate[0, :, at])
-        up = dot_nn(x, w_up[0, :, at]) + adapter_scale * dot_nn(r_u, l_up[0, :, at])
+        gate = dot_nn(x, gate_s[slot, :, at]) + adapter_scale * dot_nn(r_g, l_gate[0, :, at])
+        up = dot_nn(x, up_s[slot, :, at]) + adapter_scale * dot_nn(r_u, l_up[0, :, at])
         d_hidden = dm_in[0, 0, :, at].astype(F32)
         sig = 1.0 / (1.0 + jnp.exp(-gate))
         act = gate * sig
@@ -453,11 +474,12 @@
         du_s[:, at] = (d_hidden * act).astype(BF)
     hidden, d_gate, d_up = hid_s[...], dg_s[...], du_s[...]
     r_low = (dot_nt(hidden, d_low[0]) * keep_one).astype(BF)
-    y = dot_nn(hidden, w_low[0]) + adapter_scale * dot_nn(r_low, l_low[0])
+    ready[2].wait()
+    y = dot_nn(hidden, low_s[slot]) + adapter_scale * dot_nn(r_low, l_low[0])
     y_all[pl.ds(base, MOST), :] = (y * sw).astype(BF)
     dr = jnp.concatenate([dot_nt(d_gate, l_gate[0]), dot_nt(d_up, l_up[0])], axis=1)
     dr = (adapter_scale * dr * keep).astype(BF)
-    dx = dot_nt(d_gate, w_gate[0]) + dot_nt(d_up, w_up[0]) + dot_nn(dr, d_gu[0])
+    dx = dot_nt(d_gate, gate_s[slot]) + dot_nt(d_up, up_s[slot]) + dot_nn(dr, d_gu[0])
     dx_all[pl.ds(base, MOST), :] = dx.astype(BF)
     emit(0, dot_tn(dr, x))
     emit(2 * PACK, adapter_scale * dot_tn(r_g, d_gate))
@@ -556,9 +578,9 @@
                 pl.BlockSpec((1, 1, MOST, width), lambda e, s: (s[0], e, 0, 0)),
                 pl.BlockSpec((1, 1, MOST, ff), lambda e, s: (s[0], e, 0, 0)),
                 pl.BlockSpec((1, 1, MOST, PACK), lambda e, s: (s[0], e, 0, 0)),
-                pl.BlockSpec((1, width, ff), per_e),
-                pl.BlockSpec((1, width, ff), per_e),
-                pl.BlockSpec((1, ff, width), per_e),
+                pl.BlockSpec(memory_space=pl.ANY),
+                pl.BlockSpec(memory_space=pl.ANY),
+                pl.BlockSpec(memory_space=pl.ANY),
                 pl.BlockSpec((1, 2 * PACK, width), per_e),
                 pl.BlockSpec((1, PACK, ff), per_e),
                 pl.BlockSpec((1, PACK, ff), per_e),
@@ -579,6 +601,10 @@
                 pltpu.VMEM((n_exp * MOST, rows), BF),
                 pltpu.VMEM((n_exp * MOST, width), BF),
                 pltpu.VMEM((n_exp * MOST, width), BF),
+                pltpu.VMEM((2, width, ff), BF),
+                pltpu.VMEM((2, width, ff), BF),
+                pltpu.VMEM((2, ff, width), BF),
+                pltpu.SemaphoreType.DMA((2, 3)),
             ],
         ),
         out_shape=[
@@ -803,7 +829,7 @@
 
     sizes = (team, n_shard, seq_len, width)
     made, r_own = project(ids, all_h, downs, line2, far2, sizes)
-    made, near_o = lax.optimization_barrier((tuple(made), tuple(near_o)))
+    near_o = after(tuple(near_o), *made)
     far_o = [rep_swap(b, 1) for b in near_o]
     qkv = [made[0]] + [rep_swap(made[j], j << 1) for j in range(1, team)]
     sizes = sizes + (cols,)

time: 570 us -> 567 us (level)
  transfers between devices with their start and end apart: 61 -> 61, of which waited for: 16 -> 17; matrix products, arithmetic and copies ran while one was open for 9% -> 9% of each run, Pallas kernels for 43% -> 42%
where the time goes in v4:
time: 567 us; the launch traced here: 561 us
  Pallas kernels  238 us (42%)
  waiting for transfers between devices  129 us (23%)
  starting transfers between devices  113 us (20%)
  other arithmetic  38.5 us (7%)
  local copies, waits for them, and re-layouts  25.7 us (5%)
  between operations  16.3 us (3%)
    pallas_call x4, Pallas kernels, expert_chunk(): pl.pallas_call(functools.partial(expert_kernel, n_exp, prior is not None,...  146 us
    ppermute x25, waiting for transfers between devices, rep_swap(): return lax.ppermute(x, 'rep', [(a, a ^ bits) for a in range(n_rep)])  73 us
    ppermute x9, starting transfers between devices, line_step(): lax.ppermute(down, 'shard', [(a, a + 1) for a in range(n_shard - 1)])  45.7 us
    ppermute x9, waiting for transfers between devices, line_step(): lax.ppermute(up, 'shard', [(a, a - 1) for a in range(1, n_shard)])  39.7 us
    pallas_call x1, Pallas kernels, attention_back(): pl.pallas_call(functools.partial(back_kernel, sizes, len(parts)), in_spec...  36.1 us
    pallas_call x1, Pallas kernels, grad_rows(): pl.pallas_call(functools.partial(grad_kernel, n_line, 256), grid=(n_exp,)...  25.9 us
    ppermute x25, starting transfers between devices, rep_swap(): return lax.ppermute(x, 'rep', [(a, a ^ bits) for a in range(n_rep)])  20.3 us
    pallas_call x1, Pallas kernels, project(): pl.pallas_call(functools.partial(project_kernel, sizes), in_specs=[pl.Blo...  16.5 us
  transfers between devices with their start and end apart: 61, of which 17 were waited for; matrix products, arithmetic and copies ran while one was open for 9% of the time, Pallas kernels for 42%

profile of v4, /device:TPU:0, one launch (start us, length us, event | category | flops | bytes accessed | tf_op | source)
XLA Modules:
  0.0 560.5 jit_solution(2200605264089794817)
XLA Ops:
  14.9 5.8 %collective-permute-start.1 = (bf16[1504,128]{1,0:T(8,128)(2,1)}, bf16[1504,128]{1,0:T(8,128)(2,1)}, u32[]{:S(2)}, u32[]{:S(2)}) collective-permute-start(bf16[1504,128]{1,0:T(8,128)(2,1)} %pad_maximum_fusion.4), channel_id=1, source_target_pairs={{0,1},{1,2},{2,3},{4,5},{5,6},{6,7},{8,9},{9,10},{10,11},{12,13},{... | collective-permute-start | bytes 1155080 | tf_op jit(solution)/shard_map/ppermute | solution.py:694
  22.1 6.4 %collective-permute-done.1 = bf16[1504,128]{1,0:T(8,128)(2,1)} collective-permute-done((bf16[1504,128]{1,0:T(8,128)(2,1)}, bf16[1504,128]{1,0:T(8,128)(2,1)}, u32[]{:S(2)}, u32[]{:S(2)}) %collective-permute-start.1) | collective-permute-done | bytes 385056 | tf_op jit(solution)/shard_map/ppermute | solution.py:694
  28.5 5.1 collective-permute-start.2
  36.5 4.0 collective-permute-done.2
  40.5 4.4 collective-permute-start.3
  48.1 5.5 collective-permute-start.8
  57.2 17.3 %collective-permute-done.5 = bf16[1504,128]{1,0:T(8,128)(2,1)S(1)} collective-permute-done((bf16[1504,128]{1,0:T(8,128)(2,1)S(1)}, bf16[1504,128]{1,0:T(8,128)(2,1)S(1)}, u32[]{:S(2)}, u32[]{:S(2)}) %collective-permute-start.5) | collective-permute-done | bytes 385056 | tf_op jit(solution)/shard_map/ppermute | solution.py:693
  80.2 4.6 collective-permute-start.9
  88.5 9.1 %collective-permute-done.11 = bf16[3120,128]{1,0:T(8,128)(2,1)S(1)} collective-permute-done((bf16[3120,128]{1,0:T(8,128)(2,1)}, bf16[3120,128]{1,0:T(8,128)(2,1)S(1)}, u32[]{:S(2)}, u32[]{:S(2)}) %collective-permute-start.11) | collective-permute-done | bytes 798752 | tf_op jit(solution)/shard_map/ppermute | solution.py:693
  98.9 4.6 collective-permute-start.10
  103.6 11.5 %collective-permute-done.12 = bf16[3120,128]{1,0:T(8,128)(2,1)S(1)} collective-permute-done((bf16[3120,128]{1,0:T(8,128)(2,1)S(1)}, bf16[3120,128]{1,0:T(8,128)(2,1)S(1)}, u32[]{:S(2)}, u32[]{:S(2)}) %collective-permute-start.12) | collective-permute-done | bytes 798752 | tf_op jit(solution)/shard_map/ppermute | solution.py:693
  131.4 16.5 %shard_map.405 = (bf16[256,1536]{1,0:T(8,128)(2,1)}, bf16[256,1536]{1,0:T(8,128)(2,1)}, bf16[256,1536]{1,0:T(8,128)(2,1)}, bf16[256,1536]{1,0:T(8,128)(2,1)}, bf16[3,256,32]{2,1,0:T(8,128)(2,1)}) custom-call(s32[4]{0:T(128)} %pad_add_fusion.ids, bf16[8,272,2048]{2,1,0:T(8,128)(2,1)} %bitcast.299, bf16[128,2048]{1,0:T(8,128)(2,1)} %maximum_select_fusion.1.downs.refs_9_, ...), custom_call_target="tpu_custom_call" | custom-call | flops 6442450944 | bytes 12582912 | tf_op jit(solution)/shard_map/pallas_call | solution.py:131
  151.0 20.8 %collective-permute-done.18.refs_6_.refs_27_ = bf16[256,2048]{1,0:T(8,128)(2,1)} collective-permute-done((bf16[256,2048]{1,0:T(8,128)(2,1)}, bf16[256,2048]{1,0:T(8,128)(2,1)}, u32[]{:S(2)}, u32[]{:S(2)}) %collective-permute-start.18) | collective-permute-done | bytes 1048608 | tf_op jit(solution)/shard_map/ppermute | solution.py:689
  172.8 14.7 %collective-permute-done.14.refs_1_.refs_22_ = bf16[256,1536]{1,0:T(8,128)(2,1)} collective-permute-done((bf16[256,1536]{1,0:T(8,128)(2,1)}, bf16[256,1536]{1,0:T(8,128)(2,1)}, u32[]{:S(2)}, u32[]{:S(2)}) %collective-permute-start.14) | collective-permute-done | bytes 786464 | tf_op jit(solution)/shard_map/ppermute | solution.py:689
  195.7 13.6 %collective-permute-done.16.refs_3_.refs_24_ = bf16[256,1536]{1,0:T(8,128)(2,1)} collective-permute-done((bf16[256,1536]{1,0:T(8,128)(2,1)}, bf16[256,1536]{1,0:T(8,128)(2,1)}, u32[]{:S(2)}, u32[]{:S(2)}) %collective-permute-start.16) | collective-permute-done | bytes 786464 | tf_op jit(solution)/shard_map/ppermute | solution.py:689
  211.0 13.3 %shard_map.406 = (bf16[256,2048]{1,0:T(8,128)(2,1)}, bf16[256,32]{1,0:T(8,128)(2,1)}, f32[256,2048]{1,0:T(8,128)}, bf16[256,2048]{1,0:T(8,128)(2,1)}) custom-call(s32[4]{0:T(128)} %pad_add_fusion.ids, s32[1,256]{1,0:T(1,128)} %refs_0_.1, s32[256,1]{1,0:T(8,128)} %copy.107.seg_col.refs_1_, s32[1,256]{1,0:T(1,128)} %refs_2_.1, bf16[256,2048]{1,0:T(8,128)(2,1)} %refs_3_, ...), custom_call_target="tpu_custom_call" | custom-call | flops 2684354560 | bytes 14680064 | tf_op jit(solution)/shard_map/pallas_call | solution.py:200
  226.8 5.4 collective-permute-start.25
  232.2 25.9 %shard_map.407 = (bf16[4,4,160,2048]{3,2,1,0:T(8,128)(2,1)}, bf16[4,4,160,1024]{3,2,1,0:T(8,128)(2,1)}, bf16[4,4,160,32]{3,2,1,0:T(8,128)(2,1)}) custom-call(bf16[4,256,2048]{2,1,0:T(8,128)(2,1)} %bitcast.300, s32[4,4,1,256]{3,2,1,0:T(1,128)} %get-tuple-element.146.place, f32[4,4,1,256]{3,2,1,0:T(1,128)} %bitcast.285, f32[4,1,64]{2,1,0:T(1,128)} %tile.28.mask, ...), custom_call_target="tpu_custom_call" | custom-call | flops 16106127360 | bytes 16777216 | tf_op jit(solution)/shard_map/pallas_call | solution.py:527
  259.4 4.6 collective-permute-start.27
  265.1 36.0 %shard_map.408 = (bf16[256,2048]{1,0:T(8,128)(2,1)}, bf16[256,2048]{1,0:T(8,128)(2,1)}, f32[4,144,2048]{2,1,0:T(8,128)}) custom-call(s32[1]{0:T(128)} %bitcast.64.source, bf16[256,2048]{1,0:T(8,128)(2,1)} %broadcast_select_fusion.h2, s32[4,1,256]{2,1,0:T(1,128)} %get-tuple-element.155.place, f32[4,1,256]{2,1,0:T(1,128)} %get-tuple-element.151.weight, ...), custom_call_target="tpu_custom_call" | custom-call | flops 21474836480 | bytes 50331648 | tf_op jit(solution)/shard_map/pallas_call | solution.py:568
  307.0 5.7 %collective-permute-start.31 = (bf16[256,2048]{1,0:T(8,128)(2,1)S(1)}, bf16[256,2048]{1,0:T(8,128)(2,1)}, u32[]{:S(2)}, u32[]{:S(2)}) collective-permute-start(bf16[256,2048]{1,0:T(8,128)(2,1)S(1)} %collective-permute-done.27), channel_id=1, source_target_pairs={{0,1},{1,2},{2,3},{4,5},{5,6},{6,7},{8,9},{9,10},{10,11},{12,13},{... | collective-permute-start | bytes 3145736 | tf_op jit(solution)/shard_map/ppermute | solution.py:694
  313.8 36.3 %shard_map.409 = (bf16[256,2048]{1,0:T(8,128)(2,1)}, bf16[256,2048]{1,0:T(8,128)(2,1)}, f32[4,144,2048]{2,1,0:T(8,128)}) custom-call(s32[1]{0:T(128)} %bitcast.51.source, bf16[256,2048]{1,0:T(8,128)(2,1)} %select_select_fusion.1.h2, s32[4,1,256]{2,1,0:T(1,128)} %get-tuple-element.154.place, f32[4,1,256]{2,1,0:T(1,128)} %get-tuple-element.150.weight, ...), custom_call_target="tpu_custom_call" | custom-call | flops 21474836480 | bytes 50331648 | tf_op jit(solution)/shard_map/pallas_call | solution.py:568
  354.3 37.0 %shard_map.410 = (bf16[256,2048]{1,0:T(8,128)(2,1)}, bf16[256,2048]{1,0:T(8,128)(2,1)}, f32[4,144,2048]{2,1,0:T(8,128)}) custom-call(s32[1]{0:T(128)} %bitcast.69.source, bf16[256,2048]{1,0:T(8,128)(2,1)} %select_select_fusion.h2, s32[4,1,256]{2,1,0:T(1,128)} %get-tuple-element.153.place, f32[4,1,256]{2,1,0:T(1,128)} %get-tuple-element.149.weight, ...), custom_call_target="tpu_custom_call" | custom-call | flops 21474836480 | bytes 50331648 | tf_op jit(solution)/shard_map/pallas_call | solution.py:568
  391.4 4.3 collective-permute-start.34
  396.4 5.5 collective-permute-start.40
  404.7 36.7 %shard_map.411 = (f32[256,2048]{1,0:T(8,128)}, f32[256,2048]{1,0:T(8,128)}, bf16[4,144,2048]{2,1,0:T(8,128)(2,1)}) custom-call(s32[1]{0:T(128)} %bitcast.source, bf16[256,2048]{1,0:T(8,128)(2,1)} %get-tuple-element.90.h2, s32[4,1,256]{2,1,0:T(1,128)} %get-tuple-element.152.place, f32[4,1,256]{2,1,0:T(1,128)} %get-tuple-element.148.weight, ...), custom_call_target="tpu_custom_call" | custom-call | flops 21474836480 | bytes 50331648 | tf_op jit(solution)/shard_map/pallas_call | solution.py:568
  445.6 4.4 collective-permute-start.36
  453.6 36.1 %shard_map.412 = (bf16[256,2048]{1,0:T(8,128)(2,1)}, bf16[4,128,512]{2,1,0:T(8,128)(2,1)}) custom-call(s32[4]{0:T(128)} %pad_add_fusion.ids, s32[1,256]{1,0:T(1,128)} %refs_0_.1, s32[256,1]{1,0:T(8,128)} %copy.107.seg_col.refs_1_, s32[1,256]{1,0:T(1,128)} %refs_2_.1, bf16[256,2048]{1,0:T(8,128)(2,1)} %refs_3_, bf16[256,2048]{1,0:T(8,128)(2,1)} %refs_4_.1, ...), custom_call_target="tpu_custom_call" | custom-call | flops 9932111872 | bytes 44040192 | tf_op jit(solution)/shard_map/pallas_call | solution.py:360
  499.7 5.5 collective-permute-done.43
  505.5 4.8 collective-permute-done.52
  515.7 5.2 collective-permute-start.37
  525.2 13.2 %collective-permute-done.55 = bf16[72,2048]{1,0:T(8,128)(2,1)S(1)} collective-permute-done((bf16[72,2048]{1,0:T(8,128)(2,1)S(1)}, bf16[72,2048]{1,0:T(8,128)(2,1)S(1)}, u32[]{:S(2)}, u32[]{:S(2)}) %collective-permute-start.55) | collective-permute-done | bytes 294944 | tf_op jit(solution)/shard_map/ppermute | solution.py:689
  (298 shorter events, 120.3 us)
Async XLA Ops:
  7.2 111.0 %all-gather.7.cloned.1.call-start = ((), (), s32[]{:S(2)}) async-start(), calls=%async_computation | async-start | bytes 10027008 | tf_op jit(solution)/shard_map/all_gather | solution.py:731
  12.5 219.7 %all-gather.9.cloned.1.call-start = ((), (), s32[]{:S(2)}) async-start(), calls=%async_computation.1 | async-start | bytes 5242880 | tf_op jit(solution)/shard_map/all_gather | solution.py:857
  46.8 31.5 %collective-permute-start.7 = (bf16[3120,128]{1,0:T(8,128)(2,1)S(1)}, bf16[3120,128]{1,0:T(8,128)(2,1)}, u32[]{:S(2)}, u32[]{:S(2)}) collective-permute-start(bf16[3120,128]{1,0:T(8,128)(2,1)S(1)} %pad_maximum_fusion.3), channel_id=1, source_target_pairs={{1,0},{2,1},{3,2},{5,4},{6,5},{7,6},{9,8},{10,9},{11,10},{13,12},{... | collective-permute-start | bytes 2396168 | tf_op jit(solution)/shard_map/ppermute | solution.py:693
  48.1 30.2 %collective-permute-start.8 = (bf16[3120,128]{1,0:T(8,128)(2,1)S(1)}, bf16[3120,128]{1,0:T(8,128)(2,1)}, u32[]{:S(2)}, u32[]{:S(2)}) collective-permute-start(bf16[3120,128]{1,0:T(8,128)(2,1)S(1)} %pad_maximum_fusion.3), channel_id=1, source_target_pairs={{0,1},{1,2},{2,3},{4,5},{5,6},{6,7},{8,9},{9,10},{10,11},{12,13},{... | collective-permute-start | bytes 2396168 | tf_op jit(solution)/shard_map/ppermute | solution.py:694
  118.3 335.3 %all-gather.11.cloned.1.call-start = ((), (), s32[]{:S(2)}) async-start(), calls=%async_computation.2 | async-start | bytes 28753920 | tf_op jit(solution)/shard_map/all_gather | solution.py:860
  122.4 28.6 %collective-permute-start.17 = (bf16[256,2048]{1,0:T(8,128)(2,1)}, bf16[256,2048]{1,0:T(8,128)(2,1)}, u32[]{:S(2)}, u32[]{:S(2)}) collective-permute-start(bf16[256,2048]{1,0:T(8,128)(2,1)} %reshape.331.refs_4_.refs_25_), channel_id=1, source_target_pairs={{0,8},{4,12},{8,0},{12,4},{16,24},{20,28},{24,16},{28,20},{1,9},{5... | collective-permute-start | bytes 3145736 | tf_op jit(solution)/shard_map/ppermute | solution.py:689
  124.0 47.8 %collective-permute-start.18 = (bf16[256,2048]{1,0:T(8,128)(2,1)}, bf16[256,2048]{1,0:T(8,128)(2,1)}, u32[]{:S(2)}, u32[]{:S(2)}) collective-permute-start(bf16[256,2048]{1,0:T(8,128)(2,1)} %reshape.331.refs_4_.refs_25_), channel_id=1, source_target_pairs={{0,16},{4,20},{8,24},{12,28},{16,0},{20,4},{24,8},{28,12},{1,17},{... | collective-permute-start | bytes 3145736 | tf_op jit(solution)/shard_map/ppermute | solution.py:689
  125.5 46.8 %collective-permute-start.19 = (bf16[256,2048]{1,0:T(8,128)(2,1)}, bf16[256,2048]{1,0:T(8,128)(2,1)}, u32[]{:S(2)}, u32[]{:S(2)}) collective-permute-start(bf16[256,2048]{1,0:T(8,128)(2,1)} %reshape.331.refs_4_.refs_25_), channel_id=1, source_target_pairs={{0,24},{4,28},{8,16},{12,20},{16,8},{20,12},{24,0},{28,4},{1,25},{... | collective-permute-start | bytes 3145736 | tf_op jit(solution)/shard_map/ppermute | solution.py:689
  147.9 39.6 %collective-permute-start.14 = (bf16[256,1536]{1,0:T(8,128)(2,1)}, bf16[256,1536]{1,0:T(8,128)(2,1)}, u32[]{:S(2)}, u32[]{:S(2)}) collective-permute-start(bf16[256,1536]{1,0:T(8,128)(2,1)} %get-tuple-element.69), channel_id=1, source_target_pairs={{0,8},{4,12},{8,0},{12,4},{16,24},{20,28},{24,16},{28,20},{1,9},{5... | collective-permute-start | bytes 2359304 | tf_op jit(solution)/shard_map/ppermute | solution.py:689
  149.5 39.2 %collective-permute-start.15 = (bf16[256,1536]{1,0:T(8,128)(2,1)}, bf16[256,1536]{1,0:T(8,128)(2,1)}, u32[]{:S(2)}, u32[]{:S(2)}) collective-permute-start(bf16[256,1536]{1,0:T(8,128)(2,1)} %get-tuple-element.70), channel_id=1, source_target_pairs={{0,16},{4,20},{8,24},{12,28},{16,0},{20,4},{24,8},{28,12},{1,17},{... | collective-permute-start | bytes 2359304 | tf_op jit(solution)/shard_map/ppermute | solution.py:689
  172.2 37.1 %collective-permute-start.20 = (bf16[256,2048]{1,0:T(8,128)(2,1)}, bf16[256,2048]{1,0:T(8,128)(2,1)S(1)}, u32[]{:S(2)}, u32[]{:S(2)}) collective-permute-start(bf16[256,2048]{1,0:T(8,128)(2,1)} %reshape.331.refs_4_.refs_25_), channel_id=1, source_target_pairs={{0,4},{4,0},{8,12},{12,8},{16,20},{20,16},{24,28},{28,24},{1,5},{5... | collective-permute-start | bytes 3145736 | tf_op jit(solution)/shard_map/ppermute | solution.py:689
  172.3 37.1 %collective-permute-start.21 = (bf16[256,2048]{1,0:T(8,128)(2,1)}, bf16[256,2048]{1,0:T(8,128)(2,1)S(1)}, u32[]{:S(2)}, u32[]{:S(2)}) collective-permute-start(bf16[256,2048]{1,0:T(8,128)(2,1)} %collective-permute-done.17.refs_5_.refs_26_), channel_id=1, source_target_pairs={{0,4},{4,0},{8,12},{12,8},{16,20},{20,16},{24,28},{28,24},{1,5},{5... | collective-permute-start | bytes 3145736 | tf_op jit(solution)/shard_map/ppermute | solution.py:689
  172.8 36.6 %collective-permute-start.22 = (bf16[256,2048]{1,0:T(8,128)(2,1)}, bf16[256,2048]{1,0:T(8,128)(2,1)S(1)}, u32[]{:S(2)}, u32[]{:S(2)}) collective-permute-start(bf16[256,2048]{1,0:T(8,128)(2,1)} %collective-permute-done.18.refs_6_.refs_27_), channel_id=1, source_target_pairs={{0,4},{4,0},{8,12},{12,8},{16,20},{20,16},{24,28},{28,24},{1,5},{5... | collective-permute-start | bytes 3145736 | tf_op jit(solution)/shard_map/ppermute | solution.py:689
  225.5 32.6 %collective-permute-start.24 = (bf16[256,2048]{1,0:T(8,128)(2,1)S(1)}, bf16[256,2048]{1,0:T(8,128)(2,1)S(1)}, u32[]{:S(2)}, u32[]{:S(2)}) collective-permute-start(bf16[256,2048]{1,0:T(8,128)(2,1)S(1)} %copy-done.34), channel_id=1, source_target_pairs={{1,0},{2,1},{3,2},{5,4},{6,5},{7,6},{9,8},{10,9},{11,10},{13,12},{... | collective-permute-start | bytes 3145736 | tf_op jit(solution)/shard_map/ppermute | solution.py:693
  226.8 31.3 %collective-permute-start.25 = (bf16[256,2048]{1,0:T(8,128)(2,1)S(1)}, bf16[256,2048]{1,0:T(8,128)(2,1)S(1)}, u32[]{:S(2)}, u32[]{:S(2)}) collective-permute-start(bf16[256,2048]{1,0:T(8,128)(2,1)S(1)} %copy-done.34), channel_id=1, source_target_pairs={{0,1},{1,2},{2,3},{4,5},{5,6},{6,7},{8,9},{9,10},{10,11},{12,13},{... | collective-permute-start | bytes 3145736 | tf_op jit(solution)/shard_map/ppermute | solution.py:694
  258.1 47.6 %collective-permute-start.26 = (bf16[256,2048]{1,0:T(8,128)(2,1)S(1)}, bf16[256,2048]{1,0:T(8,128)(2,1)S(1)}, u32[]{:S(2)}, u32[]{:S(2)}) collective-permute-start(bf16[256,2048]{1,0:T(8,128)(2,1)S(1)} %collective-permute-done.24), channel_id=1, source_target_pairs={{1,0},{2,1},{3,2},{5,4},{6,5},{7,6},{9,8},{10,9},{11,10},{13,12},{... | collective-permute-start | bytes 3145736 | tf_op jit(solution)/shard_map/ppermute | solution.py:693
  259.4 46.3 %collective-permute-start.27 = (bf16[256,2048]{1,0:T(8,128)(2,1)S(1)}, bf16[256,2048]{1,0:T(8,128)(2,1)S(1)}, u32[]{:S(2)}, u32[]{:S(2)}) collective-permute-start(bf16[256,2048]{1,0:T(8,128)(2,1)S(1)} %collective-permute-done.25), channel_id=1, source_target_pairs={{0,1},{1,2},{2,3},{4,5},{5,6},{6,7},{8,9},{9,10},{10,11},{12,13},{... | collective-permute-start | bytes 3145736 | tf_op jit(solution)/shard_map/ppermute | solution.py:694
  301.1 53.2 %collective-permute-start.32 = (bf16[256,2048]{1,0:T(8,128)(2,1)}, bf16[256,2048]{1,0:T(8,128)(2,1)S(1)}, u32[]{:S(2)}, u32[]{:S(2)}) collective-permute-start(bf16[256,2048]{1,0:T(8,128)(2,1)} %get-tuple-element.85), channel_id=1, source_target_pairs={{0,1},{1,2},{2,3},{4,5},{5,6},{6,7},{8,9},{9,10},{10,11},{12,13},{... | collective-permute-start | bytes 3145736 | tf_op jit(solution)/shard_map/ppermute | solution.py:898
  304.9 49.4 %collective-permute-start.33 = (bf16[256,2048]{1,0:T(8,128)(2,1)}, bf16[256,2048]{1,0:T(8,128)(2,1)S(1)}, u32[]{:S(2)}, u32[]{:S(2)}) collective-permute-start(bf16[256,2048]{1,0:T(8,128)(2,1)} %get-tuple-element.85), channel_id=1, source_target_pairs={{3,2},{7,6},{11,10},{15,14},{19,18},{23,22},{27,26},{31,30}} | collective-permute-start | bytes 3145736 | tf_op jit(solution)/shard_map/ppermute | solution.py:898
  305.7 46.7 %collective-permute-start.30 = (bf16[256,2048]{1,0:T(8,128)(2,1)S(1)}, bf16[256,2048]{1,0:T(8,128)(2,1)S(1)}, u32[]{:S(2)}, u32[]{:S(2)}) collective-permute-start(bf16[256,2048]{1,0:T(8,128)(2,1)S(1)} %collective-permute-done.26), channel_id=1, source_target_pairs={{1,0},{2,1},{3,2},{5,4},{6,5},{7,6},{9,8},{10,9},{11,10},{13,12},{... | collective-permute-start | bytes 3145736 | tf_op jit(solution)/shard_map/ppermute | solution.py:693
  307.0 46.1 %collective-permute-start.31 = (bf16[256,2048]{1,0:T(8,128)(2,1)S(1)}, bf16[256,2048]{1,0:T(8,128)(2,1)}, u32[]{:S(2)}, u32[]{:S(2)}) collective-permute-start(bf16[256,2048]{1,0:T(8,128)(2,1)S(1)} %collective-permute-done.27), channel_id=1, source_target_pairs={{0,1},{1,2},{2,3},{4,5},{5,6},{6,7},{8,9},{9,10},{10,11},{12,13},{... | collective-permute-start | bytes 3145736 | tf_op jit(solution)/shard_map/ppermute | solution.py:694
  350.2 51.8 %collective-permute-start.28 = (bf16[256,2048]{1,0:T(8,128)(2,1)}, bf16[256,2048]{1,0:T(8,128)(2,1)S(1)}, u32[]{:S(2)}, u32[]{:S(2)}) collective-permute-start(bf16[256,2048]{1,0:T(8,128)(2,1)} %get-tuple-element.89), channel_id=1, source_target_pairs={{0,2},{1,0},{2,1},{4,6},{5,4},{6,5},{8,10},{9,8},{10,9},{12,14},{1... | collective-permute-start | bytes 3145736 | tf_op jit(solution)/shard_map/ppermute | solution.py:898
  352.4 51.3 %collective-permute-start.29 = (bf16[256,2048]{1,0:T(8,128)(2,1)}, bf16[256,2048]{1,0:T(8,128)(2,1)S(1)}, u32[]{:S(2)}, u32[]{:S(2)}) collective-permute-start(bf16[256,2048]{1,0:T(8,128)(2,1)} %get-tuple-element.89), channel_id=1, source_target_pairs={{3,1},{7,5},{11,9},{15,13},{19,17},{23,21},{27,25},{31,29}} | collective-permute-start | bytes 3145736 | tf_op jit(solution)/shard_map/ppermute | solution.py:898
  391.4 51.7 %collective-permute-start.34 = (bf16[256,2048]{1,0:T(8,128)(2,1)}, bf16[256,2048]{1,0:T(8,128)(2,1)S(1)}, u32[]{:S(2)}, u32[]{:S(2)}) collective-permute-start(bf16[256,2048]{1,0:T(8,128)(2,1)} %get-tuple-element.98), channel_id=1, source_target_pairs={{0,1},{4,5},{8,9},{12,13},{16,17},{20,21},{24,25},{28,29}} | collective-permute-start | bytes 3145736 | tf_op jit(solution)/shard_map/ppermute | solution.py:964
  395.7 47.4 %collective-permute-start.35 = (bf16[256,2048]{1,0:T(8,128)(2,1)}, bf16[256,2048]{1,0:T(8,128)(2,1)S(1)}, u32[]{:S(2)}, u32[]{:S(2)}) collective-permute-start(bf16[256,2048]{1,0:T(8,128)(2,1)} %get-tuple-element.98), channel_id=1, source_target_pairs={{3,2},{7,6},{11,10},{15,14},{19,18},{23,22},{27,26},{31,30}} | collective-permute-start | bytes 3145736 | tf_op jit(solution)/shard_map/ppermute | solution.py:967
  396.4 57.1 %collective-permute-start.40 = (bf16[256,2048]{1,0:T(8,128)(2,1)}, bf16[256,2048]{1,0:T(8,128)(2,1)}, u32[]{:S(2)}, u32[]{:S(2)}) collective-permute-start(bf16[256,2048]{1,0:T(8,128)(2,1)} %get-tuple-element.104), channel_id=1, source_target_pairs={{0,3},{2,0},{4,7},{6,4},{8,11},{10,8},{12,15},{14,12},{16,19},{18,... | collective-permute-start | bytes 3145736 | tf_op jit(solution)/shard_map/ppermute | solution.py:898
  402.0 51.5 %collective-permute-start.41 = (bf16[256,2048]{1,0:T(8,128)(2,1)}, bf16[256,2048]{1,0:T(8,128)(2,1)}, u32[]{:S(2)}, u32[]{:S(2)}) collective-permute-start(bf16[256,2048]{1,0:T(8,128)(2,1)} %get-tuple-element.104), channel_id=1, source_target_pairs={{1,3},{3,0},{5,7},{7,4},{9,11},{11,8},{13,15},{15,12},{17,19},{19,... | collective-permute-start | bytes 3145736 | tf_op jit(solution)/shard_map/ppermute | solution.py:898
  443.0 50.9 %collective-permute-start.50 = (bf16[288,2048]{1,0:T(8,128)(2,1)S(1)}, bf16[288,2048]{1,0:T(8,128)(2,1)S(1)}, u32[]{:S(2)}, u32[]{:S(2)}) collective-permute-start(bf16[288,2048]{1,0:T(8,128)(2,1)S(1)} %dynamic-slice_bitcast_fusion), channel_id=1, source_target_pairs={{0,4},{4,0},{8,12},{12,8},{16,20},{20,16},{24,28},{28,24},{1,5},{5... | collective-permute-start | bytes 3538952 | tf_op jit(solution)/shard_map/ppermute | solution.py:689
  445.6 44.1 %collective-permute-start.36 = (bf16[256,2048]{1,0:T(8,128)(2,1)}, bf16[256,2048]{1,0:T(8,128)(2,1)}, u32[]{:S(2)}, u32[]{:S(2)}) collective-permute-start(bf16[256,2048]{1,0:T(8,128)(2,1)} %get-tuple-element.121), channel_id=1, source_target_pairs={{0,1},{1,2},{4,5},{5,6},{8,9},{9,10},{12,13},{13,14},{16,17},{17,1... | collective-permute-start | bytes 3145736 | tf_op jit(solution)/shard_map/ppermute | solution.py:964
  450.0 39.8 %collective-permute-start.38 = (bf16[256,2048]{1,0:T(8,128)(2,1)}, bf16[256,2048]{1,0:T(8,128)(2,1)}, u32[]{:S(2)}, u32[]{:S(2)}) collective-permute-start(bf16[256,2048]{1,0:T(8,128)(2,1)} %get-tuple-element.122), channel_id=1, source_target_pairs={{2,1},{3,2},{6,5},{7,6},{10,9},{11,10},{14,13},{15,14},{18,17},{19... | collective-permute-start | bytes 3145736 | tf_op jit(solution)/shard_map/ppermute | solution.py:967
  514.3 30.6 %collective-permute-start.39 = (bf16[256,2048]{1,0:T(8,128)(2,1)S(1)}, bf16[256,2048]{1,0:T(8,128)(2,1)S(1)}, u32[]{:S(2)}, u32[]{:S(2)}) collective-permute-start(bf16[256,2048]{1,0:T(8,128)(2,1)S(1)} %get-tuple-element.127), channel_id=1, source_target_pairs={{1,0},{2,1},{3,2},{5,4},{6,5},{7,6},{9,8},{10,9},{11,10},{13,12},{... | collective-permute-start | bytes 3145736 | tf_op jit(solution)/shard_map/ppermute | solution.py:967
  515.7 29.2 %collective-permute-start.37 = (bf16[256,2048]{1,0:T(8,128)(2,1)S(1)}, bf16[256,2048]{1,0:T(8,128)(2,1)S(1)}, u32[]{:S(2)}, u32[]{:S(2)}) collective-permute-start(bf16[256,2048]{1,0:T(8,128)(2,1)S(1)} %get-tuple-element.126), channel_id=1, source_target_pairs={{0,1},{1,2},{2,3},{4,5},{5,6},{6,7},{8,9},{9,10},{10,11},{12,13},{... | collective-permute-start | bytes 3145736 | tf_op jit(solution)/shard_map/ppermute | solution.py:964
  (67 other events, 903.4 us)
Sparse Core Ops, SparseCore 0:
  12.7 59.2 all-gather.6
  118.4 82.1 all-gather.8
  224.4 127.6 all-gather.10
